TPU v7x, 32 devices: a whole 2x2x4 slice. The times are simulated.
32 devices in a mesh: dp: 2 (over core), row: 4 (over y, x), col: 4 (over z).
Axes of the slice: x: 2, y: 2, z: 4, core: 2. Of those that a mesh axis runs over, the one named last changes fastest.
Arguments:
- tokens: bfloat16 [4096, 2048], P(('dp', 'col'), 'row'), may hold values from -6 to 6
- segment_ids: int32 [2, 2048], P('dp'), may hold values from 0 to 2, never falling along the last dimension, each value on 1 to 1536 neighbouring positions
- ln1_gain: bfloat16 [2048], P('row'), may hold values from 0.25 to 1.75
- ln1_bias: bfloat16 [2048], P('row'), may hold values from -3 to 3
- w_query: bfloat16 [2048, 2048], P('row', 'col'), may hold values from -0.125 to 0.125
- b_query: bfloat16 [2048], P('col'), may hold values from -3 to 3
- w_keyval: bfloat16 [2048, 256], P('row'), may hold values from -0.125 to 0.125
- b_value: bfloat16 [128], replicated, may hold values from -1.1953125 to 1.1953125
- w_out: bfloat16 [2048, 2048], P('col', 'row'), may hold values from -0.5 to 0.5
- b_out: bfloat16 [2048], P('row'), may hold values from -2 to 2
- ln2_gain: bfloat16 [2048], P('row'), may hold values from 0.25 to 1.75
- ln2_bias: bfloat16 [2048], P('row'), may hold values from -3 to 3
- w_up: bfloat16 [2048, 8192], P('row', 'col'), may hold values from -0.16572815 to 0.16572815
- b_up: bfloat16 [8192], P('col'), may hold values from -3 to 3
- w_down: bfloat16 [8192, 2048], P('col', 'row'), may hold values from -0.0625 to 0.0625
- b_down: bfloat16 [2048], P('row'), may hold values from -2 to 2
- d_output: bfloat16 [4096, 2048], P(('dp', 'col'), 'row'), may hold values from -6 to 6
Outputs:
- output: bfloat16 [4096, 2048], P(('dp', 'col'), 'row')
- grad_tokens: float32 [4096, 2048], P(('dp', 'col'), 'row')
- grad_ln1_gain: float32 [2048], P('row')
- grad_ln1_bias: float32 [2048], P('row')
- grad_w_query: float32 [2048, 2048], P('row', 'col')
- grad_b_query: float32 [2048], P('col')
- grad_w_keyval: float32 [2048, 256], P('row')
- grad_b_value: float32 [128], replicated
- grad_w_out: float32 [2048, 2048], P('col', 'row')
- grad_b_out: float32 [2048], P('row')
- grad_ln2_gain: float32 [2048], P('row')
- grad_ln2_bias: float32 [2048], P('row')
- grad_w_up: float32 [2048, 8192], P('row', 'col')
- grad_b_up: float32 [8192], P('col')
- grad_w_down: float32 [8192, 2048], P('col', 'row')
- grad_b_down: float32 [2048], P('row')
Inputs may be any that keep to these rules, and one draw needn't show every extreme that they name: `segment_ids`: in each sequence the segment ids never fall; each document holds 1 to 1536 tokens, and one holds exactly 1536.
All inputs are finite; a program needn't handle non-finite values.
Results may differ from a plain program's by a relative error of at most 0.014.
Values may be sent and summed in bfloat16 or wider, within the bound.
No kernel may reach another device: no remote copies, remote signals or barrier semaphores. Data moves between devices by JAX's collectives and lax.ppermute only.
A program may use at most 320 MiB of HBM per device.

v0:
```python
import jax
import jax.numpy as jnp
from jax import lax
from jax.sharding import PartitionSpec as P

epsilon = 1e-05
negative = -1e30


def gelu_tanh(values):
    return jax.nn.gelu(values, approximate=True)


def row_totals(pair):
    return lax.psum((pair[0], pair[1]), "row")


def norm_forward(values, gain, offset, width):
    totals = row_totals((jnp.sum(values, axis=1), jnp.sum(values * values, axis=1)))
    average = totals[0] / width
    spread = totals[1] / width - average * average
    inv_std = lax.rsqrt(spread + epsilon)
    centred = (values - average[:, None]) * inv_std[:, None]
    normed = centred * gain.astype(jnp.float32) + offset.astype(jnp.float32)
    return (normed.astype(jnp.bfloat16), centred, inv_std)


def norm_backward(grad_out, centred, inv_std, gain, width):
    scaled = grad_out * gain.astype(jnp.float32)
    totals = row_totals((jnp.sum(scaled, axis=1), jnp.sum(scaled * centred, axis=1)))
    grad_in = inv_std[:, None] * (
        scaled - totals[0][:, None] / width - centred * (totals[1][:, None] / width)
    )
    return (grad_in, jnp.sum(grad_out * centred, axis=0), jnp.sum(grad_out, axis=0))


def gather_col(rows):
    return lax.all_gather(rows, "col", axis=0, tiled=True)


def gather_row(branch_rows):
    return lax.all_gather(branch_rows, "row", axis=0, tiled=True)


def contract_last(left, right):
    return lax.dot_general(
        left, right, (((1,), (1,)), ((), ())), preferred_element_type=jnp.float32
    )


def contract_first(left, right):
    return lax.dot_general(
        left, right, (((0,), (0,)), ((), ())), preferred_element_type=jnp.float32
    )


def row_scatter(gathered, product):
    return lax.psum_scatter(product(gathered), "row", scatter_dimension=0, tiled=True)


def col_scatter(gathered, product):
    return lax.psum_scatter(product(gathered), "col", scatter_dimension=0, tiled=True)


def grad_col_scatter(gathered, product):
    return lax.psum_scatter(product(gathered), "col", scatter_dimension=0, tiled=True)


def key_bounds(key_blocks):
    first_block = 0
    return (first_block, key_blocks)


def block_scores(
    query_rows, query_pos, query_seg, keys_all, segments, key_index, key_span, scaling
):
    key_start = key_index * key_span
    key_rows = lax.dynamic_slice_in_dim(keys_all, key_start, key_span, 0)
    key_seg = lax.dynamic_slice_in_dim(segments, key_start, key_span, 0)
    key_pos = key_start + jnp.arange(key_span, dtype=jnp.int32)
    raw = contract_last(query_rows, key_rows) * scaling
    allowed = (query_seg[:, None] == key_seg[None, :]) & (key_pos[None, :] <= query_pos[:, None])
    return jnp.where(allowed, raw, negative)


def per_device(
    tokens,
    segment_ids,
    ln1_gain,
    ln1_bias,
    w_query,
    b_query,
    w_keyval,
    b_value,
    w_out,
    b_out,
    ln2_gain,
    ln2_bias,
    w_up,
    b_up,
    w_down,
    b_down,
    d_output,
):
    width = tokens.shape[1] * lax.axis_size("row")
    head_size = b_value.shape[0]
    query_cols = w_query.shape[1]
    heads_local = query_cols // head_size
    local_tokens = tokens.shape[0]
    group_tokens = local_tokens * lax.axis_size("col")
    query_tokens = group_tokens // lax.axis_size("row")
    col_index = lax.axis_index("col")
    row_start = lax.axis_index("row") * query_tokens
    segments = segment_ids[0]
    residual = tokens.astype(jnp.float32)
    normed_one, centred_one, inv_one = norm_forward(residual, ln1_gain, ln1_bias, width)
    gathered_one = gather_col(normed_one)

    def first_product(piece):
        return jnp.concatenate(
            [
                jnp.dot(piece, w_query, preferred_element_type=jnp.float32),
                jnp.dot(piece, w_keyval, preferred_element_type=jnp.float32),
            ],
            axis=1,
        )

    mixed = row_scatter(gathered_one, first_product)
    queries = (mixed[:, :query_cols] + b_query.astype(jnp.float32)).astype(jnp.bfloat16)
    keys_own = mixed[:, query_cols : query_cols + head_size]
    values_own = mixed[:, query_cols + head_size :] + b_value.astype(jnp.float32)
    keyval_own = jnp.concatenate([keys_own, values_own], axis=1).astype(jnp.bfloat16)
    keyval_all = lax.all_gather(keyval_own, "row", axis=0, tiled=True)
    keys_all = keyval_all[:, :head_size]
    values_all = keyval_all[:, head_size:]
    scaling = head_size ** (-0.5)
    query_span = min(128, query_tokens)
    key_span = min(512, group_tokens)
    query_blocks = query_tokens // query_span
    key_blocks = group_tokens // key_span
    block_rows = query_span * heads_local
    row_offsets = jnp.arange(block_rows, dtype=jnp.int32) // heads_local
    query_view = queries.reshape(query_blocks, block_rows, head_size)

    def query_meta(block_index):
        first_token = row_start + block_index * query_span
        query_pos = first_token + row_offsets
        seg_block = lax.dynamic_slice_in_dim(segments, first_token, query_span, 0)
        query_seg = jnp.repeat(seg_block, heads_local, total_repeat_length=block_rows)
        first_block, end_block = key_bounds(key_blocks)
        return (query_pos, query_seg, first_block, end_block)

    def forward_block(block_index, loop_state):
        outputs, log_sums = loop_state
        query_rows = lax.dynamic_index_in_dim(query_view, block_index, 0, keepdims=False)
        query_pos, query_seg, first_block, end_block = query_meta(block_index)

        def max_step(key_index, max_state):
            running_max, running_sum = max_state
            scores = block_scores(
                query_rows, query_pos, query_seg, keys_all, segments, key_index, key_span, scaling
            )
            new_max = jnp.maximum(running_max, jnp.max(scores, axis=1))
            running_sum = running_sum * jnp.exp(running_max - new_max) + jnp.sum(
                jnp.exp(scores - new_max[:, None]), axis=1
            )
            return (new_max, running_sum)

        start_state = (
            jnp.full((block_rows,), negative, jnp.float32),
            jnp.zeros((block_rows,), jnp.float32),
        )
        running_max, running_sum = lax.fori_loop(first_block, end_block, max_step, start_state)
        log_sum = running_max + jnp.log(running_sum)

        def value_step(key_index, value_total):
            scores = block_scores(
                query_rows, query_pos, query_seg, keys_all, segments, key_index, key_span, scaling
            )
            weights = jnp.exp(scores - log_sum[:, None]).astype(jnp.bfloat16)
            value_rows = lax.dynamic_slice_in_dim(values_all, key_index * key_span, key_span, 0)
            return value_total + jnp.dot(weights, value_rows, preferred_element_type=jnp.float32)

        value_total = lax.fori_loop(
            first_block, end_block, value_step, jnp.zeros((block_rows, head_size), jnp.float32)
        )
        outputs = lax.dynamic_update_index_in_dim(
            outputs, value_total.astype(jnp.bfloat16), block_index, 0
        )
        log_sums = lax.dynamic_update_index_in_dim(log_sums, log_sum, block_index, 0)
        return (outputs, log_sums)

    start_outputs = (
        jnp.zeros((query_blocks, block_rows, head_size), jnp.bfloat16),
        jnp.zeros((query_blocks, block_rows), jnp.float32),
    )
    attended_view, log_sums = lax.fori_loop(0, query_blocks, forward_block, start_outputs)
    attended = attended_view.reshape(query_tokens, query_cols)
    gathered_att = gather_row(attended)

    def out_product(piece):
        return jnp.dot(piece, w_out, preferred_element_type=jnp.float32)

    attn_term = col_scatter(gathered_att, out_product)
    hidden_one = residual + attn_term + b_out.astype(jnp.float32)
    normed_two, centred_two, inv_two = norm_forward(hidden_one, ln2_gain, ln2_bias, width)
    gathered_two = gather_col(normed_two)

    def up_product(piece):
        return jnp.dot(piece, w_up, preferred_element_type=jnp.float32)

    upper = row_scatter(gathered_two, up_product) + b_up.astype(jnp.float32)
    activated = gelu_tanh(upper).astype(jnp.bfloat16)
    gathered_act = gather_row(activated)

    def down_product(piece):
        return jnp.dot(piece, w_down, preferred_element_type=jnp.float32)

    ffn_term = col_scatter(gathered_act, down_product)
    final = hidden_one + ffn_term + b_down.astype(jnp.float32)
    output = final.astype(jnp.bfloat16)
    grad_out_rows = gather_col(d_output)
    grad_b_down = jnp.sum(grad_out_rows.astype(jnp.float32), axis=0)
    act_rows = gather_row(activated)
    grad_w_down = contract_first(act_rows, grad_out_rows)

    def act_product(piece):
        return contract_last(piece, w_down)

    grad_act = row_scatter(grad_out_rows, act_product)
    unused_value, gelu_pull = jax.vjp(gelu_tanh, upper)
    grad_upper = gelu_pull(grad_act)[0].astype(jnp.bfloat16)
    grad_upper_rows = gather_row(grad_upper)
    two_rows = gather_col(normed_two)
    grad_w_up = contract_first(two_rows, grad_upper_rows)
    grad_b_up = jnp.sum(grad_upper_rows.astype(jnp.float32), axis=0)

    def two_product(piece):
        return contract_last(piece, w_up)

    grad_normed_two = grad_col_scatter(grad_upper_rows, two_product)
    grad_in_two, grad_gain_two, grad_bias_two = norm_backward(
        grad_normed_two, centred_two, inv_two, ln2_gain, width
    )
    grad_hidden = d_output.astype(jnp.float32) + grad_in_two
    grad_branch = grad_hidden.astype(jnp.bfloat16)
    grad_branch_rows = gather_col(grad_branch)
    grad_b_out = jnp.sum(grad_branch_rows.astype(jnp.float32), axis=0)
    att_rows = gather_row(attended)
    grad_w_out = contract_first(att_rows, grad_branch_rows)

    def att_product(piece):
        return contract_last(piece, w_out)

    grad_att = row_scatter(grad_branch_rows, att_product).astype(jnp.bfloat16)
    grad_view = grad_att.reshape(query_blocks, block_rows, head_size)

    def backward_block(block_index, loop_state):
        grad_queries, grad_keyvals = loop_state
        query_rows = lax.dynamic_index_in_dim(query_view, block_index, 0, keepdims=False)
        grad_rows = lax.dynamic_index_in_dim(grad_view, block_index, 0, keepdims=False)
        log_sum = lax.dynamic_index_in_dim(log_sums, block_index, 0, keepdims=False)
        query_pos, query_seg, first_block, end_block = query_meta(block_index)

        def probs_and_grads(key_index):
            scores = block_scores(
                query_rows, query_pos, query_seg, keys_all, segments, key_index, key_span, scaling
            )
            probs = jnp.exp(scores - log_sum[:, None])
            value_rows = lax.dynamic_slice_in_dim(values_all, key_index * key_span, key_span, 0)
            return (probs, contract_last(grad_rows, value_rows))

        def delta_step(key_index, accum):
            probs, grad_probs = probs_and_grads(key_index)
            return accum + jnp.sum(probs * grad_probs, axis=1)

        delta = lax.fori_loop(
            first_block, end_block, delta_step, jnp.zeros((block_rows,), jnp.float32)
        )

        def grad_step(key_index, inner_state):
            query_grad, keyval_grads = inner_state
            key_start = key_index * key_span
            probs, grad_probs = probs_and_grads(key_index)
            grad_scores = (probs * (grad_probs - delta[:, None])).astype(jnp.bfloat16)
            key_rows = lax.dynamic_slice_in_dim(keys_all, key_start, key_span, 0)
            query_grad = query_grad + jnp.dot(
                grad_scores, key_rows, preferred_element_type=jnp.float32
            )
            key_grad = contract_first(grad_scores, query_rows) * scaling
            value_grad = contract_first(probs.astype(jnp.bfloat16), grad_rows)
            current = lax.dynamic_slice_in_dim(keyval_grads, key_start, key_span, 0)
            updated = current + jnp.concatenate([key_grad, value_grad], axis=1)
            keyval_grads = lax.dynamic_update_slice_in_dim(keyval_grads, updated, key_start, 0)
            return (query_grad, keyval_grads)

        query_grad, grad_keyvals = lax.fori_loop(
            first_block,
            end_block,
            grad_step,
            (jnp.zeros((block_rows, head_size), jnp.float32), grad_keyvals),
        )
        grad_queries = lax.dynamic_update_index_in_dim(
            grad_queries, query_grad * scaling, block_index, 0
        )
        return (grad_queries, grad_keyvals)

    start_grads = (
        jnp.zeros((query_blocks, block_rows, head_size), jnp.float32),
        jnp.zeros((group_tokens, 2 * head_size), jnp.float32),
    )
    grad_query_view, keyval_part = lax.fori_loop(0, query_blocks, backward_block, start_grads)
    grad_queries = grad_query_view.reshape(query_tokens, query_cols).astype(jnp.bfloat16)
    grad_keyvals = lax.psum(keyval_part, ("row", "col")).astype(jnp.bfloat16)
    grad_b_value = jnp.sum(grad_keyvals[:, head_size:].astype(jnp.float32), axis=0)
    grad_query_rows = gather_row(grad_queries)
    one_rows = gather_col(normed_one)
    grad_w_query = contract_first(one_rows, grad_query_rows)
    grad_b_query = jnp.sum(grad_query_rows.astype(jnp.float32), axis=0)

    def query_product(piece):
        return contract_last(piece, w_query)

    query_term = grad_col_scatter(grad_query_rows, query_product)
    grad_w_keyval = contract_first(one_rows, grad_keyvals)
    own_keyvals = lax.dynamic_slice_in_dim(grad_keyvals, col_index * local_tokens, local_tokens, 0)
    grad_normed_one = query_term + contract_last(own_keyvals, w_keyval)
    grad_in_one, grad_gain_one, grad_bias_one = norm_backward(
        grad_normed_one, centred_one, inv_one, ln1_gain, width
    )
    grad_tokens = grad_hidden + grad_in_one
    matrix_grads = lax.psum(
        (
            grad_w_query,
            grad_b_query,
            grad_w_keyval,
            grad_b_value,
            grad_w_out,
            grad_b_out,
            grad_w_up,
            grad_b_up,
            grad_w_down,
            grad_b_down,
        ),
        "dp",
    )
    norm_grads = lax.psum(
        (grad_gain_one, grad_bias_one, grad_gain_two, grad_bias_two), ("dp", "col")
    )
    return (
        output,
        grad_tokens,
        norm_grads[0],
        norm_grads[1],
        matrix_grads[0],
        matrix_grads[1],
        matrix_grads[2],
        matrix_grads[3],
        matrix_grads[4],
        matrix_grads[5],
        norm_grads[2],
        norm_grads[3],
        matrix_grads[6],
        matrix_grads[7],
        matrix_grads[8],
        matrix_grads[9],
    )


def solution(mesh):
    in_specs = (
        P(("dp", "col"), "row"),
        P("dp", None),
        P("row"),
        P("row"),
        P("row", "col"),
        P("col"),
        P("row", None),
        P(),
        P("col", "row"),
        P("row"),
        P("row"),
        P("row"),
        P("row", "col"),
        P("col"),
        P("col", "row"),
        P("row"),
        P(("dp", "col"), "row"),
    )
    out_specs = (
        P(("dp", "col"), "row"),
        P(("dp", "col"), "row"),
        P("row"),
        P("row"),
        P("row", "col"),
        P("col"),
        P("row", None),
        P(),
        P("col", "row"),
        P("row"),
        P("row"),
        P("row"),
        P("row", "col"),
        P("col"),
        P("col", "row"),
        P("row"),
    )
    return jax.shard_map(
        per_device, mesh=mesh, in_specs=in_specs, out_specs=out_specs, check_vma=False
    )
```

profile of v0, /device:TPU:0, one launch (start us, length us, event | category | flops | bytes accessed | tf_op | source)
XLA Modules:
  0.0 1656.1 jit_solution(3461989284698036647)
XLA Ops:
  10.1 11.3 all-reduce.4
  24.2 45.4 %all-gather.10.cloned.1.call-done = bf16[2048,512]{1,0:T(8,128)(2,1)} async-done(((bf16[512,512]{1,0:T(8,128)(2,1)}), bf16[2048,512]{1,0:T(8,128)(2,1)}) %all-gather.10.cloned.1.call-update) | async-done | bytes 2097168 | tf_op jit(solution)/shard_map/all_gather | solution.py:38
  77.2 68.5 %reduce-scatter.9.cloned.1.call-done = f32[512,768]{0,1:T(8,128)} async-done(((f32[2048,768]{0,1:T(8,128)}), f32[512,768]{0,1:T(8,128)}) %reduce-scatter.9.cloned.1.call-update) | async-done | bytes 1572880 | tf_op jit(solution)/shard_map/reduce_scatter | solution.py:58
  151.2 23.8 %all-gather.12.cloned.1.call-done = bf16[2048,256]{0,1:T(8,128)(2,1)} async-done(((bf16[512,256]{0,1:T(8,128)(2,1)}), bf16[2048,256]{0,1:T(8,128)(2,1)}) %all-gather.12.cloned.1.call-update) | async-done | bytes 1048592 | tf_op jit(solution)/shard_map/all_gather | solution.py:133
  178.3 74.9 %while.240 = (s32[]{:T(128)}, bf16[4,512,128]{2,1,0:T(8,128)(2,1)}, f32[4,512]{1,0:T(4,128)S(1)}, bf16[4,512,128]{2,1,0:T(8,128)(2,1)}, s32[]{:T(128)}, /*index=...) while((s32[]{:T(128)}, bf16[4,512,128]{2,1,0:T(8,128)(2,1)}, ...), condition=%wide.region_12.14_spmd.clone, body=%wide.region_5.13_spmd.clone.sunk | while | flops 205472272 | bytes 4028301 | solution.py:197
  182.8 6.5 while.244
  189.4 6.9 while.245
  201.5 6.5 while.244
  208.1 6.9 while.245
  220.3 6.5 while.244
  226.8 6.9 while.245
  239.0 6.5 while.244
  245.6 6.9 while.245
  255.4 35.4 %all-gather.14.cloned.1.call-done = bf16[2048,512]{1,0:T(8,128)(2,1)} async-done(((bf16[512,512]{1,0:T(8,128)(2,1)}), bf16[2048,512]{1,0:T(8,128)(2,1)}) %all-gather.14.cloned.1.call-update) | async-done | bytes 2097168 | tf_op jit(solution)/shard_map/all_gather | solution.py:42
  296.5 76.2 %reduce-scatter.11.cloned.1.call-done = f32[512,512]{1,0:T(8,128)} async-done(((f32[2048,512]{1,0:T(8,128)}), f32[512,512]{1,0:T(8,128)}) %reduce-scatter.11.cloned.1.call-update) | async-done | bytes 1048592 | tf_op jit(solution)/shard_map/reduce_scatter | solution.py:62
  374.4 9.8 all-reduce.3
  385.5 35.2 %all-gather.20.cloned.1.call-done = bf16[2048,512]{1,0:T(8,128)(2,1)} async-done(((bf16[512,512]{1,0:T(8,128)(2,1)}), bf16[2048,512]{1,0:T(8,128)(2,1)}) %all-gather.20.cloned.1.call-update) | async-done | bytes 2097168 | tf_op jit(solution)/shard_map/all_gather | solution.py:38
  420.7 12.8 fusion.102
  433.6 34.0 %all-gather.16.cloned.1.call-done = bf16[2048,512]{1,0:T(8,128)(2,1)} async-done(((bf16[512,512]{1,0:T(8,128)(2,1)}), bf16[2048,512]{1,0:T(8,128)(2,1)}) %all-gather.16.cloned.1.call-update) | async-done | bytes 2097168 | tf_op jit(solution)/shard_map/all_gather | solution.py:38
  467.7 9.9 fusion.100
  478.3 145.3 %reduce-scatter.17.cloned.1.call-done = f32[512,2048]{1,0:T(8,128)} async-done(((f32[2048,2048]{1,0:T(8,128)}), f32[512,2048]{1,0:T(8,128)}) %reduce-scatter.17.cloned.1.call-update) | async-done | bytes 4194320 | tf_op jit(solution)/shard_map/reduce_scatter | solution.py:58
  623.6 157.2 %reduce-scatter.13.cloned.1.call-done = f32[512,2048]{1,0:T(8,128)} async-done(((f32[2048,2048]{1,0:T(8,128)}), f32[512,2048]{1,0:T(8,128)}) %reduce-scatter.13.cloned.1.call-update) | async-done | bytes 4194320 | tf_op jit(solution)/shard_map/reduce_scatter | solution.py:58
  780.8 6.7 fusion.73
  788.3 87.0 %all-gather.22.cloned.1.call-done = bf16[2048,2048]{1,0:T(8,128)(2,1)} async-done(((bf16[512,2048]{1,0:T(8,128)(2,1)}), bf16[2048,2048]{1,0:T(8,128)(2,1)}) %all-gather.22.cloned.1.call-update) | async-done | bytes 8388624 | tf_op jit(solution)/shard_map/all_gather | solution.py:42
  875.3 9.5 fusion.103
  885.0 80.4 %all-gather.18.cloned.1.call-done = bf16[2048,2048]{1,0:T(8,128)(2,1)} async-done(((bf16[512,2048]{1,0:T(8,128)(2,1)}), bf16[2048,2048]{1,0:T(8,128)(2,1)}) %all-gather.18.cloned.1.call-update) | async-done | bytes 8388624 | tf_op jit(solution)/shard_map/all_gather | solution.py:42
  965.5 9.4 fusion.101
  975.6 69.5 %reduce-scatter.19.cloned.1.call-done = f32[512,512]{1,0:T(8,128)} async-done(((f32[2048,512]{1,0:T(8,128)}), f32[512,512]{1,0:T(8,128)}) %reduce-scatter.19.cloned.1.call-update) | async-done | bytes 1048592 | tf_op jit(solution)/shard_map/reduce_scatter | solution.py:66
  1046.9 9.8 all-reduce.2
  1056.8 68.5 %reduce-scatter.15.cloned.1.call-done = f32[512,512]{1,0:T(8,128)} async-done(((f32[2048,512]{1,0:T(8,128)}), f32[512,512]{1,0:T(8,128)}) %reduce-scatter.15.cloned.1.call-update) | async-done | bytes 1048592 | tf_op jit(solution)/shard_map/reduce_scatter | solution.py:62
  1128.5 46.5 %all-gather.24.cloned.1.call-done = bf16[2048,512]{1,0:T(8,128)(2,1)} async-done(((bf16[512,512]{1,0:T(8,128)(2,1)}), bf16[2048,512]{1,0:T(8,128)(2,1)}) %all-gather.24.cloned.1.call-update) | async-done | bytes 2097168 | tf_op jit(solution)/shard_map/all_gather | solution.py:38
  1180.0 51.5 %reduce-scatter.21.cloned.1.call-done = f32[512,512]{1,0:T(8,128)} async-done(((f32[2048,512]{1,0:T(8,128)}), f32[512,512]{1,0:T(8,128)}) %reduce-scatter.21.cloned.1.call-update) | async-done | bytes 1048592 | tf_op jit(solution)/shard_map/reduce_scatter | solution.py:58
  1234.1 140.3 %while.243 = (s32[]{:T(128)}, bf16[4,512,128]{2,1,0:T(8,128)(2,1)}, f32[2048,256]{0,1:T(8,128)S(1)}, bf16[4,512,128]{2,1,0:T(8,128)(2,1)}, s32[]{:T(128)}, /*ind...) while((s32[]{:T(128)}, bf16[4,512,128]{2,1,0:T(8,128)(2,1)}, ...), condition=%wide.region_33.35_spmd.clone, body=%wide.region_27.34_spmd.clone.sunk | while | flops 475019264 | bytes 12001785 | solution.py:312
  1238.7 10.8 while.246
  1249.6 18.9 %while.247 = (s32[]{:T(128)}, f32[512,128]{1,0:T(8,128)S(1)}, f32[2048,256]{0,1:T(8,128)S(1)}, s32[512]{0:T(512)S(1)}, s32[2048]{0:T(1024)S(1)}, /*index=5*/s32[...) while((s32[]{:T(128)}, f32[512,128]{1,0:T(8,128)S(1)}, ...), condition=%wide.region_32.33_spmd.clone, body=%wide.region_31.32_spmd.clone.sunk | while | flops 338625024 | bytes 8276197 | solution.py:297
  1273.8 10.8 while.246
  1284.7 18.9 %while.247 = (s32[]{:T(128)}, f32[512,128]{1,0:T(8,128)S(1)}, f32[2048,256]{0,1:T(8,128)S(1)}, s32[512]{0:T(512)S(1)}, s32[2048]{0:T(1024)S(1)}, /*index=5*/s32[...) while((s32[]{:T(128)}, f32[512,128]{1,0:T(8,128)S(1)}, ...), condition=%wide.region_32.33_spmd.clone, body=%wide.region_31.32_spmd.clone.sunk | while | flops 338625024 | bytes 8276197 | solution.py:297
  1308.9 10.8 while.246
  1319.7 18.9 %while.247 = (s32[]{:T(128)}, f32[512,128]{1,0:T(8,128)S(1)}, f32[2048,256]{0,1:T(8,128)S(1)}, s32[512]{0:T(512)S(1)}, s32[2048]{0:T(1024)S(1)}, /*index=5*/s32[...) while((s32[]{:T(128)}, f32[512,128]{1,0:T(8,128)S(1)}, ...), condition=%wide.region_32.33_spmd.clone, body=%wide.region_31.32_spmd.clone.sunk | while | flops 338625024 | bytes 8276197 | solution.py:297
  1344.0 10.8 while.246
  1354.8 18.9 %while.247 = (s32[]{:T(128)}, f32[512,128]{1,0:T(8,128)S(1)}, f32[2048,256]{0,1:T(8,128)S(1)}, s32[512]{0:T(512)S(1)}, s32[2048]{0:T(1024)S(1)}, /*index=5*/s32[...) while((s32[]{:T(128)}, f32[512,128]{1,0:T(8,128)S(1)}, ...), condition=%wide.region_32.33_spmd.clone, body=%wide.region_31.32_spmd.clone.sunk | while | flops 338625024 | bytes 8276197 | solution.py:297
  1376.7 35.4 %all-gather.26.cloned.1.call-done = bf16[2048,512]{1,0:T(8,128)(2,1)} async-done(((bf16[512,512]{1,0:T(8,128)(2,1)}), bf16[2048,512]{1,0:T(8,128)(2,1)}) %all-gather.26.cloned.1.call-update) | async-done | bytes 2097168 | tf_op jit(solution)/shard_map/all_gather | solution.py:42
  1412.1 5.0 fusion.105
  1417.4 10.7 fusion.109
  1428.1 9.9 fusion.110
  1440.3 145.1 %all-reduce.11 = bf16[2048,256]{0,1:T(8,128)(2,1)S(1)} all-reduce(f32[2048,256]{0,1:T(8,128)S(1)} %get-tuple-element.1463), channel_id=1, replica_groups=mesh['dp'=2,'row'=4,'col'=4] {'row','col'}, use_global_device_ids=true, to_apply=%region_35.37 | all-reduce | flops 524288 | bytes 3145728 | tf_op jit(solution)/shard_map/psum | solution.py:314
  1608.2 9.4 all-reduce.1
  1617.7 15.2 all-reduce
  (638 shorter events, 302.8 us)
Async XLA Ops:
  7.2 460.5 %copy-start = (bf16[512,2048]{1,0:T(8,128)(2,1)S(1)}, bf16[512,2048]{1,0:T(8,128)(2,1)}, u32[]{:S(2)}) copy-start(bf16[512,2048]{1,0:T(8,128)(2,1)} %param.47) | copy-start | bytes 6291460
  7.2 62.4 %copy-start.17 = (bf16[512,512]{1,0:T(8,128)(2,1)S(1)}, bf16[512,512]{1,0:T(8,128)(2,1)}, u32[]{:S(2)}) copy-start(bf16[512,512]{1,0:T(8,128)(2,1)} %param.39) | copy-start | bytes 1572868
  7.2 62.4 %all-gather.10.cloned.1.call-start = ((), (), s32[]{:S(2)}) async-start(), calls=%async_computation.8 | async-start | bytes 2621440 | tf_op jit(solution)/shard_map/all_gather | solution.py:38
  9.4 14.7 copy-start.25
  24.1 48.5 %copy-start.23 = (bf16[512,256]{1,0:T(8,128)(2,1)S(1)}, bf16[512,256]{1,0:T(8,128)(2,1)}, u32[]{:S(2)}) copy-start(bf16[512,256]{1,0:T(8,128)(2,1)} %param.41) | copy-start | bytes 786436
  24.1 121.5 %reduce-scatter.9.cloned.1.call-start = ((), (), s32[]{:S(2)}) async-start(), calls=%async_computation.9 | async-start | bytes 7864320 | tf_op jit(solution)/shard_map/reduce_scatter | solution.py:58
  69.6 3.1 copy-start.2
  76.5 71.9 %copy-start.32 = (bf16[512]{0:T(512)(128)(2,1)S(1)}, bf16[512]{0:T(512)(128)(2,1)}, u32[]{:S(2)}) copy-start(bf16[512]{0:T(512)(128)(2,1)} %param.40) | copy-start | bytes 3076
  76.5 98.5 %all-gather.12.cloned.1.call-start = ((), (), s32[]{:S(2)}) async-start(), calls=%async_computation.10 | async-start | bytes 1310720 | tf_op jit(solution)/shard_map/all_gather | solution.py:133
  148.4 142.5 %all-gather.14.cloned.1.call-start = ((), (), s32[]{:S(2)}) async-start(), calls=%async_computation.11 | async-start | bytes 2621440 | tf_op jit(solution)/shard_map/all_gather | solution.py:42
  151.2 27.1 %copy-start.8 = (s32[1,2048]{1,0:T(1,128)S(1)}, s32[1,2048]{1,0:T(1,128)}, u32[]{:S(2)}) copy-start(s32[1,2048]{1,0:T(1,128)} %param.36) | copy-start | bytes 24580
  151.2 27.1 %copy-start.22 = (s32[4,128]{1,0:T(4,128)S(1)}, s32[4,128]{1,0:T(4,128)}, u32[]{:S(2)}) copy-start(s32[4,128]{1,0:T(4,128)} %constant.615.clone.2) | copy-start | bytes 6148
  255.4 117.4 %reduce-scatter.11.cloned.1.call-start = ((), (), s32[]{:S(2)}) async-start(), calls=%async_computation.12 | async-start | bytes 5242880 | tf_op jit(solution)/shard_map/reduce_scatter | solution.py:62
  295.8 124.9 %all-gather.20.cloned.1.call-start = ((), (), s32[]{:S(2)}) async-start(), calls=%async_computation.17 | async-start | bytes 2621440 | tf_op jit(solution)/shard_map/all_gather | solution.py:38
  296.4 171.2 %all-gather.16.cloned.1.call-start = ((), (), s32[]{:S(2)}) async-start(), calls=%async_computation.13 | async-start | bytes 2621440 | tf_op jit(solution)/shard_map/all_gather | solution.py:38
  385.3 238.3 %reduce-scatter.17.cloned.1.call-start = ((), (), s32[]{:S(2)}) async-start(), calls=%async_computation.18 | async-start | bytes 20971520 | tf_op jit(solution)/shard_map/reduce_scatter | solution.py:58
  433.6 347.2 %reduce-scatter.13.cloned.1.call-start = ((), (), s32[]{:S(2)}) async-start(), calls=%async_computation.14 | async-start | bytes 20971520 | tf_op jit(solution)/shard_map/reduce_scatter | solution.py:58
  477.6 397.6 %all-gather.22.cloned.1.call-start = ((), (), s32[]{:S(2)}) async-start(), calls=%async_computation.19 | async-start | bytes 10485760 | tf_op jit(solution)/shard_map/all_gather | solution.py:42
  787.5 178.0 %all-gather.18.cloned.1.call-start = ((), (), s32[]{:S(2)}) async-start(), calls=%async_computation.15 | async-start | bytes 10485760 | tf_op jit(solution)/shard_map/all_gather | solution.py:42
  788.2 256.8 %reduce-scatter.19.cloned.1.call-start = ((), (), s32[]{:S(2)}) async-start(), calls=%async_computation.20 | async-start | bytes 5242880 | tf_op jit(solution)/shard_map/reduce_scatter | solution.py:66
  884.7 80.7 %copy-start.37 = (bf16[2048,512]{1,0:T(8,128)(2,1)S(1)}, bf16[2048,512]{1,0:T(8,128)(2,1)}, u32[]{:S(2)}) copy-start(bf16[2048,512]{1,0:T(8,128)(2,1)} %param.49) | copy-start | bytes 6291460
  884.8 240.5 %reduce-scatter.15.cloned.1.call-start = ((), (), s32[]{:S(2)}) async-start(), calls=%async_computation.16 | async-start | bytes 5242880 | tf_op jit(solution)/shard_map/reduce_scatter | solution.py:62
  974.9 150.4 %copy-start.18 = (bf16[512,512]{1,0:T(8,128)(2,1)S(1)}, bf16[512,512]{1,0:T(8,128)(2,1)}, u32[]{:S(2)}) copy-start(bf16[512,512]{1,0:T(8,128)(2,1)} %param.51) | copy-start | bytes 1572868
  974.9 200.0 %all-gather.24.cloned.1.call-start = ((), (), s32[]{:S(2)}) async-start(), calls=%async_computation.21 | async-start | bytes 2621440 | tf_op jit(solution)/shard_map/all_gather | solution.py:38
  1045.1 80.2 %copy-start.10 = (f32[512,512]{1,0:T(8,128)S(1)}, f32[512,512]{1,0:T(8,128)}, u32[]{:S(2)}) copy-start(f32[512,512]{1,0:T(8,128)} %reduce-scatter.19.cloned.1.call-done) | copy-start | bytes 3145732
  1125.3 49.7 %copy-start.16 = (bf16[512,512]{1,0:T(8,128)(2,1)S(1)}, bf16[512,512]{1,0:T(8,128)(2,1)}, u32[]{:S(2)}) copy-start(bf16[512,512]{1,0:T(8,128)(2,1)} %param.43) | copy-start | bytes 1572868
  1128.4 103.1 %reduce-scatter.21.cloned.1.call-start = ((), (), s32[]{:S(2)}) async-start(), calls=%async_computation.22 | async-start | bytes 5242880 | tf_op jit(solution)/shard_map/reduce_scatter | solution.py:58
  1179.9 232.2 %all-gather.26.cloned.1.call-start = ((), (), s32[]{:S(2)}) async-start(), calls=%async_computation.23 | async-start | bytes 2621440 | tf_op jit(solution)/shard_map/all_gather | solution.py:42
  1376.6 229.2 %reduce-scatter.23.cloned.1.call-start = ((), (), s32[]{:S(2)}) async-start(), calls=%async_computation.24 | async-start | bytes 5242880 | tf_op jit(solution)/shard_map/reduce_scatter | solution.py:66
  1417.1 219.7 %all-reduce.10.cloned.1.call-start = ((), (), s32[]{:S(2)}) async-start(), calls=%async_computation.25 | async-start | bytes 22020096 | tf_op jit(solution)/shard_map/psum | solution.py:332
  1417.4 10.7 copy-start.19
  1428.1 9.9 copy-start.4
  1428.1 9.9 copy-start.13
  1585.4 7.5 copy-start.14
  1585.4 3.6 copy-start.3
  1594.9 4.9 copy-start.5
  1594.9 5.3 copy-start.15
  1599.8 1.7 copy-start.6
  1599.8 6.0 copy-start.7
  1599.8 6.0 copy-start.24
  1599.8 6.0 copy-start.26
  1599.8 6.0 copy-start.28
  1599.9 6.0 copy-start.30
  1601.8 31.1 %copy-start.9 = (f32[512,512]{1,0:T(8,128)S(1)}, f32[512,512]{1,0:T(8,128)}, u32[]{:S(2)}) copy-start(f32[512,512]{1,0:T(8,128)} %get-tuple-element.1863) | copy-start | bytes 3145732
  1636.8 4.3 copy-start.21
  1636.8 5.3 copy-start.12
  1642.0 3.7 copy-start.11
  1645.7 3.1 copy-start.1
  (9 other events, 6.9 us)
Sparse Core Ops, SparseCore 0:
  24.3 45.2 all-gather.9
  76.6 68.9 reduce-scatter.8
  148.5 26.4 all-gather.11
  255.5 35.3 all-gather.13
  296.0 76.7 reduce-scatter.10
  374.3 46.4 all-gather.19
  423.0 44.6 all-gather.15
  471.0 152.5 reduce-scatter.16
  627.0 153.7 reduce-scatter.12
  787.6 87.5 all-gather.21
  877.8 87.6 all-gather.17
  968.3 76.7 reduce-scatter.18
  1048.0 77.2 reduce-scatter.14
  1128.5 46.4 all-gather.23
  1180.0 51.4 reduce-scatter.20
  1376.7 35.2 all-gather.25
  1417.2 119.1 reduce-scatter.22
  1593.1 43.6 all-reduce.9
where the time goes:
time: 1670 us; the launch traced here: 1660 us
  waiting for transfers between devices  1060 us (63%)
  matrix products  252 us (15%)
  blocking collectives  205 us (12%)
  local copies, waits for them, and re-layouts  68.6 us (4%)
  other arithmetic  46.7 us (3%)
    reduce_scatter x4, waiting for transfers between devices, row_scatter(): lax.psum_scatter(product(gathered), 'row', scatter_dimension=0, tiled=True)  422 us
    all_gather x4, waiting for transfers between devices, gather_row(): return lax.all_gather(branch_rows, 'row', axis=0, tiled=True)  238 us
    all_gather x4, waiting for transfers between devices, gather_col(): return lax.all_gather(rows, 'col', axis=0, tiled=True)  161 us
    psum x1, blocking collectives, per_device(): grad_keyvals = lax.psum(keyval_part, ('row', 'col')).astype(jnp.bfloat16)  145 us
    reduce_scatter x2, waiting for transfers between devices, col_scatter(): lax.psum_scatter(product(gathered), 'col', scatter_dimension=0, tiled=True)  145 us
    dot_general x85, matrix products, contract_last(): lax.dot_general(left, right, (((1,), (1,)), ((), ())), preferred_element_...  137 us
    reduce_scatter x2, waiting for transfers between devices, grad_col_scatter(): lax.psum_scatter(product(gathered), 'col', scatter_dimension=0, tiled=True)  69.5 us
    psum x4, blocking collectives, row_totals(): return lax.psum((pair[0], pair[1]), 'row')  40.4 us
  transfers between devices with their start and end apart: 18, of which 17 were waited for; matrix products, arithmetic and copies ran while one was open for 5% of the time, Pallas kernels for 0%

commit v1 on v0

v1 whole, which is shorter than its diff:
```python
import functools
import math

import jax
import jax.numpy as jnp
from jax import lax
from jax.experimental import pallas as pl
from jax.experimental.pallas import tpu as pltpu
from jax.sharding import Mesh
from jax.sharding import PartitionSpec as P

epsilon = 1e-05
negative = -1e30
log2e = math.log2(math.e)
f32 = jnp.float32
bf16 = jnp.bfloat16


def dot_nn(a, b):
    return lax.dot_general(a, b, (((1,), (0,)), ((), ())), preferred_element_type=f32)


def dot_nt(a, b):
    return lax.dot_general(a, b, (((1,), (1,)), ((), ())), preferred_element_type=f32)


def dot_tn(a, b):
    return lax.dot_general(a, b, (((0,), (0,)), ((), ())), preferred_element_type=f32)


def swap(a, axis):
    return lax.ppermute(a, axis, [(0, 1), (1, 0)])


def cross(a):
    return lax.ppermute(a, ("rx", "cl"), [(0, 3), (1, 2), (2, 1), (3, 0)])


def fetch(a, axis, step):
    n = lax.axis_size(axis)
    return lax.ppermute(a, axis, [(s, (s - step) % n) for s in range(n)])


def after(a, b):
    return lax.optimization_barrier((a, b))[0]


def block_gather(a):
    return jnp.concatenate([a, swap(a, "rx"), swap(a, "cl"), cross(a)], axis=0)


def block_scatter(p):
    t = p.shape[0] // 4
    low = p.astype(bf16)
    got_x = swap(low[t : 2 * t], "rx")
    got_z = swap(low[2 * t : 3 * t], "cl")
    got_d = cross(low[3 * t :])
    return p[:t] + got_x.astype(f32) + got_z.astype(f32) + got_d.astype(f32)


def end_swap(a):
    return lax.ppermute(a, ("ch", "cl"), [(1, 2), (2, 1)])


def line_gather(a):
    far = swap(a, "ch")
    near = swap(a, "cl")
    mid = end_swap(a)
    end = lax.ppermute(far, ("ch", "cl"), [(1, 0), (2, 3)])
    return jnp.concatenate([a, near, far, mid + end], axis=0)


def line_scatter(p):
    t = p.shape[0] // 4
    low = p.astype(bf16)
    end = lax.ppermute(low[3 * t :], ("ch", "cl"), [(0, 1), (3, 2)])
    near = swap(low[t : 2 * t], "cl")
    far = swap((p[2 * t : 3 * t] + end.astype(f32)).astype(bf16), "ch")
    mid = end_swap(low[3 * t :])
    return p[:t] + near.astype(f32) + far.astype(f32) + mid.astype(f32)


def gather_axis(a, axis):
    n = lax.axis_size(axis)
    if n == 2:
        b = swap(a, axis)
        first = lax.axis_index(axis) == 0
        return jnp.stack([jnp.where(first, a, b), jnp.where(first, b, a)])
    return lax.all_gather(a, axis, axis=0, tiled=False)


def scatter_axis(a, axis):
    n = lax.axis_size(axis)
    me = lax.axis_index(axis)
    total = lax.dynamic_index_in_dim(a, me, 0, keepdims=False)
    for step in range(1, n):
        part = lax.dynamic_index_in_dim(a, (me - step) % n, 0, keepdims=False)
        total = total + fetch(part.astype(bf16), axis, step).astype(f32)
    return total


def sum_small(v):
    for axis in ("dp", "rx", "cl", "ch", "ry"):
        if lax.axis_size(axis) == 2:
            v = v + swap(v, axis)
        else:
            v = lax.psum(v, axis)
    return v


def half_of(w, axis):
    n = w.shape[axis] // 2
    return lax.dynamic_slice_in_dim(w, lax.axis_index("dp") * n, n, axis)


def scatter_rows(g, feat):
    every = ("ry", "rx", "dp")
    n = 1
    for axis in every:
        n *= lax.axis_size(axis)
    g = g.astype(bf16)
    if feat == 1:
        g = g.reshape(g.shape[0], n, g.shape[1] // n).transpose(1, 0, 2)
    else:
        g = g.reshape(n, g.shape[0] // n, g.shape[1])
    part = lax.psum_scatter(g, every, scatter_dimension=0, tiled=False)
    pair = gather_axis(part, "dp")
    return jnp.concatenate([pair[0], pair[1]], axis=feat).astype(f32)


class Place:
    def __init__(self):
        self.dp = lax.axis_index("dp")
        self.ry = lax.axis_index("ry")
        self.rx = lax.axis_index("rx")
        self.ch = lax.axis_index("ch")
        self.cl = lax.axis_index("cl")
        self.rows_y = lax.axis_size("ry")
        self.rows = 2 * self.rows_y

    def row_of(self, k):
        return ((self.ry + k // 2) % self.rows_y) * 2 + (self.rx ^ (k % 2))

    def slot_of(self, r):
        return ((r // 2 - self.ry) % self.rows_y) * 2 + (self.rx ^ (r % 2))

    def to_relative(self, a):
        w = a.shape[1] // self.rows
        return jnp.concatenate(
            [lax.dynamic_slice_in_dim(a, self.row_of(k) * w, w, 1) for k in range(self.rows)], axis=1
        )

    def to_absolute(self, a):
        w = a.shape[1] // self.rows
        return jnp.concatenate(
            [lax.dynamic_slice_in_dim(a, self.slot_of(r) * w, w, 1) for r in range(self.rows)], axis=1
        )

    def hidden_part(self, w, half, quarter, axis):
        q = w.shape[axis] // 4
        return lax.dynamic_slice_in_dim(w, (half * 2 + quarter) * q, q, axis)

    def gather_weight(self, w, hidden):
        feat = 1 - hidden
        mine = self.hidden_part(w, self.rx, self.dp, hidden)
        theirs = self.hidden_part(w, 1 - self.rx, self.dp, hidden)
        block = jnp.concatenate([mine, swap(theirs, "rx")], axis=feat)
        other = swap(block, "ch")
        parts = []
        for b in (block, other):
            b = jnp.concatenate([b] + [fetch(b, "ry", j) for j in range(1, self.rows_y)], axis=feat)
            parts += [b, swap(b, "dp")]
        return jnp.concatenate(parts, axis=hidden)

    def gather_hidden(self, b):
        mine = jnp.concatenate(
            [self.hidden_part(b, self.rx, self.dp, 0), self.hidden_part(b, self.rx, 1 - self.dp, 0)]
        )
        return jnp.concatenate([mine, swap(mine, "ch")])

    def scatter_weight(self, g, hidden):
        feat = 1 - hidden
        q = g.shape[hidden] // 4
        cut = lambda a, lo, n, axis: lax.slice_in_dim(a, lo, lo + n, axis=axis)
        got = swap(
            jnp.concatenate([cut(g, q, q, hidden), cut(g, 3 * q, q, hidden)], axis=hidden).astype(bf16), "dp"
        )
        own = jnp.concatenate([cut(g, 0, q, hidden), cut(g, 2 * q, q, hidden)], axis=hidden)
        total = own + got.astype(f32)
        span = g.shape[feat] // self.rows_y
        part = cut(total, 0, span, feat)
        for j in range(1, self.rows_y):
            sent = cut(total, j * span, span, feat).astype(bf16)
            n = self.rows_y
            part = part + lax.ppermute(sent, "ry", [(s, (s + j) % n) for s in range(n)]).astype(f32)
        part = cut(part, 0, q, hidden) + swap(cut(part, q, q, hidden).astype(bf16), "ch").astype(f32)
        part = part.astype(bf16)
        width = span // 2
        pair = jnp.concatenate([cut(part, 0, width, feat), swap(cut(part, width, width, feat), "rx")], axis=hidden)
        far = swap(pair, "dp")
        pieces = [[cut(pair, 0, q, hidden), cut(far, 0, q, hidden)], [cut(pair, q, q, hidden), cut(far, q, q, hidden)]]
        out = []
        for i in range(2):
            for d in range(2):
                near = jnp.where(self.dp == d, pieces[i][0], pieces[i][1])
                away = jnp.where(self.dp == d, pieces[1 - i][0], pieces[1 - i][1])
                out.append(jnp.where(self.rx == 0, near, away))
        return jnp.concatenate(out, axis=hidden).astype(f32)

    def place_hidden(self, v, blocks):
        q = v.shape[0] // 4
        whole = jnp.zeros((blocks * 4 * q,), f32)
        for a in range(2):
            for d in range(2):
                c = (self.ch ^ a) * 2 + self.cl
                start = c * 4 * q + (self.rx * 2 + (self.dp ^ d)) * q
                k = 2 * a + d
                whole = lax.dynamic_update_slice_in_dim(whole, v[k * q : (k + 1) * q], start, 0)
        return whole


def stack_heads(a, heads):
    w = a.shape[1] // heads
    return jnp.concatenate([a[:, h * w : (h + 1) * w] for h in range(heads)], axis=0)


def attend_forward(
    bounds, q_ref, k_ref, v_ref, low_ref, pos_ref, o_ref, lse_ref, *, heads, span, scale
):
    chunk = pl.program_id(0)
    rows = stack_heads(q_ref[...], heads)
    n, width = rows.shape
    low = jnp.concatenate([low_ref[0]] * heads, axis=1)
    pos = jnp.concatenate([pos_ref[0]] * heads, axis=1)

    def step(kb, state):
        top, total, acc = state
        start = pl.multiple_of(kb * span, span)
        keys = k_ref[pl.ds(start, span), :]
        values = v_ref[pl.ds(start, span), :]
        s = dot_nt(keys, rows) * scale
        at = start + lax.broadcasted_iota(jnp.int32, (span, n), 0)
        s = jnp.where((at >= low) & (at <= pos), s, negative)
        new = jnp.maximum(top, jnp.max(s, axis=0, keepdims=True))
        p = jnp.exp2(s - new)
        fade = jnp.exp2(top - new)
        total = total * fade + jnp.sum(p, axis=0, keepdims=True)
        acc = acc * fade + dot_tn(values, p.astype(bf16))
        return new, total, acc

    start_state = (
        jnp.full((1, n), negative, f32),
        jnp.zeros((1, n), f32),
        jnp.zeros((width, n), f32),
    )
    top, total, acc = lax.fori_loop(bounds[chunk, 0], bounds[chunk, 1], step, start_state)
    out = (acc / total).T.astype(bf16)
    t = n // heads
    for h in range(heads):
        o_ref[:, h * width : (h + 1) * width] = out[h * t : (h + 1) * t]
    lse_ref[0] = top + jnp.log2(total)


def attend_backward(
    bounds, q_ref, o_ref, g_ref, lse_ref, k_ref, v_ref, low_ref, pos_ref, dq_ref, dkv_ref, *, heads, span, scale, plain
):
    chunk = pl.program_id(0)

    @pl.when(chunk == 0)
    def _():
        dkv_ref[...] = jnp.zeros_like(dkv_ref)

    rows = stack_heads(q_ref[...], heads)
    outs = stack_heads(o_ref[...], heads)
    grads = stack_heads(g_ref[...], heads)
    n, width = rows.shape
    low = jnp.concatenate([low_ref[0]] * heads, axis=1)
    pos = jnp.concatenate([pos_ref[0]] * heads, axis=1)
    lse = lse_ref[0]
    delta = jnp.sum((outs.astype(f32) * grads.astype(f32)).T, axis=0, keepdims=True)

    def step(kb, acc):
        start = pl.multiple_of(kb * span, span)
        keys = k_ref[pl.ds(start, span), :]
        values = v_ref[pl.ds(start, span), :]
        s = dot_nt(keys, rows) * scale
        at = start + lax.broadcasted_iota(jnp.int32, (span, n), 0)
        p = jnp.where((at >= low) & (at <= pos), jnp.exp2(s - lse), 0.0)
        dp = dot_nt(values, grads)
        ds = (p * (dp - delta)).astype(bf16)
        acc = acc + dot_tn(keys, ds)
        dkv_ref[pl.ds(start, span), :width] += dot_nn(ds, rows) * plain
        dkv_ref[pl.ds(start, span), width:] += dot_nn(p.astype(bf16), grads)
        return acc

    acc = lax.fori_loop(bounds[chunk, 0], bounds[chunk, 1], step, jnp.zeros((width, n), f32))
    out = (acc * plain).T.astype(bf16)
    t = n // heads
    for h in range(heads):
        dq_ref[:, h * width : (h + 1) * width] = out[h * t : (h + 1) * t]


class Attention:
    def __init__(self, tokens, chunks, hidden, length, head):
        self.t, self.chunks, self.hidden, self.length, self.head = tokens, chunks, hidden, length, head
        self.heads = hidden // head
        self.span = min(512, length)
        self.plain = head ** (-0.5)
        self.scale = self.plain * log2e
        self.params = pltpu.CompilerParams(
            dimension_semantics=("arbitrary",), vmem_limit_bytes=48 * 1024 * 1024
        )
        self.rows_spec = pl.BlockSpec((tokens, hidden), lambda i, b: (i, 0))
        self.kv_spec = pl.BlockSpec((length, head), lambda i, b: (0, 0))
        self.vec_spec = pl.BlockSpec((1, 1, tokens), lambda i, b: (i, 0, 0))
        self.lse_spec = pl.BlockSpec((1, 1, tokens * self.heads), lambda i, b: (i, 0, 0))
        self.cells = tokens * chunks * self.heads * length

    def forward(self, bounds, q, k, v, low, pos):
        body = functools.partial(attend_forward, heads=self.heads, span=self.span, scale=self.scale)
        return pl.pallas_call(
            body,
            grid_spec=pltpu.PrefetchScalarGridSpec(
                num_scalar_prefetch=1,
                grid=(self.chunks,),
                in_specs=[self.rows_spec, self.kv_spec, self.kv_spec, self.vec_spec, self.vec_spec],
                out_specs=[self.rows_spec, self.lse_spec],
            ),
            out_shape=[
                jax.ShapeDtypeStruct(q.shape, bf16),
                jax.ShapeDtypeStruct((self.chunks, 1, self.t * self.heads), f32),
            ],
            compiler_params=self.params,
            cost_estimate=pl.CostEstimate(
                flops=4 * self.cells * self.head, bytes_accessed=4 << 20, transcendentals=self.cells
            ),
        )(bounds, q, k, v, low, pos)

    def backward(self, bounds, q, o, g, lse, k, v, low, pos):
        body = functools.partial(
            attend_backward, heads=self.heads, span=self.span, scale=self.scale, plain=self.plain
        )
        return pl.pallas_call(
            body,
            grid_spec=pltpu.PrefetchScalarGridSpec(
                num_scalar_prefetch=1,
                grid=(self.chunks,),
                in_specs=[self.rows_spec] * 3
                + [self.lse_spec, self.kv_spec, self.kv_spec, self.vec_spec, self.vec_spec],
                out_specs=[
                    self.rows_spec,
                    pl.BlockSpec((self.length, 2 * self.head), lambda i, b: (0, 0)),
                ],
            ),
            out_shape=[
                jax.ShapeDtypeStruct(q.shape, bf16),
                jax.ShapeDtypeStruct((self.length, 2 * self.head), f32),
            ],
            compiler_params=self.params,
            cost_estimate=pl.CostEstimate(
                flops=10 * self.cells * self.head, bytes_accessed=8 << 20, transcendentals=self.cells
            ),
        )(bounds, q, o, g, lse, k, v, low, pos)


def norm_parts(v):
    mean = jnp.mean(v, axis=1, keepdims=True)
    spread = jnp.mean(v * v, axis=1, keepdims=True) - mean * mean
    inv_std = lax.rsqrt(spread + epsilon)
    return (v - mean) * inv_std, inv_std


def norm_back(e, centred, inv_std, gain):
    c = e * gain
    m1 = jnp.mean(c, axis=1, keepdims=True)
    m2 = jnp.mean(c * centred, axis=1, keepdims=True)
    return (c - m1 - centred * m2) * inv_std


gelu_a = math.sqrt(2.0 / math.pi)
gelu_b = 0.044715


def gelu(u):
    return 0.5 * u * (1.0 + jnp.tanh(gelu_a * (u + gelu_b * u * u * u)))


def gelu_slope(u):
    th = jnp.tanh(gelu_a * (u + gelu_b * u * u * u))
    return 0.5 * (1.0 + th) + 0.5 * u * (1.0 - th * th) * gelu_a * (1.0 + 3.0 * gelu_b * u * u)


def per_device(
    tokens,
    segment_ids,
    ln1_gain,
    ln1_bias,
    w_query,
    b_query,
    w_keyval,
    b_value,
    w_out,
    b_out,
    ln2_gain,
    ln2_bias,
    w_up,
    b_up,
    w_down,
    b_down,
    d_output,
):
    at = Place()
    rows = at.rows
    blocks = 2 * lax.axis_size("ch")
    col_tokens, row_width = tokens.shape
    t = col_tokens // rows
    width = row_width * rows
    head = b_value.shape[0]
    length = segment_ids.shape[1]
    row_axes = ("ry", "rx")
    row = at.ry * 2 + at.rx
    col = at.ch * 2 + at.cl

    vectors = jnp.stack([ln1_gain, ln1_bias, ln2_gain, ln2_bias, b_out, b_down])
    vectors = gather_axis(gather_axis(vectors, "rx"), "ry")
    vectors = vectors.transpose(2, 0, 1, 3).reshape(6, 1, width).astype(f32)
    gain_one, bias_one, gain_two, bias_two, out_bias, down_bias = vectors

    own = lax.all_to_all(tokens, row_axes, 0, 1, tiled=True).astype(f32)
    own_grad = lax.all_to_all(d_output, row_axes, 0, 1, tiled=True)

    kv_weight = gather_axis(gather_axis(w_keyval, "rx"), "ry").reshape(width, 2 * head)
    query_weight = at.gather_weight(w_query, 1)
    out_weight = at.gather_weight(after(w_out, query_weight), 0)
    every = ("ry", "rx", "dp")
    up_weight = lax.all_gather(half_of(w_up, 0), every, axis=0, tiled=True)
    down_weight = lax.all_gather(half_of(w_down, 1), every, axis=1, tiled=True)
    query_bias = at.gather_hidden(b_query).astype(f32)
    up_bias = b_up.astype(f32)

    segments = segment_ids[0]
    base = jnp.stack(
        [
            ((at.ch * 2 + (at.cl ^ (k // 2))) * col_tokens + (at.ry * 2 + (at.rx ^ (k % 2))) * t)
            for k in range(4)
        ]
    ).astype(jnp.int32)
    pos = base[:, None] + jnp.arange(t, dtype=jnp.int32)[None, :]
    seg_rows = jnp.stack([lax.dynamic_slice_in_dim(segments, base[k], t, 0) for k in range(4)])
    low = jnp.sum((segments[None, None, :] < seg_rows[:, :, None]).astype(jnp.int32), axis=2)
    attention = Attention(t, 4, query_weight.shape[1], length, head)
    span = attention.span
    bounds = jnp.stack([low[:, 0] // span, (base + t - 1) // span + 1], axis=1)
    low, pos = low[:, None, :], pos[:, None, :]

    centred_one, inv_one = norm_parts(own)
    normed_one = (centred_one * gain_one + bias_one).astype(bf16)
    kv_own = dot_nn(normed_one, kv_weight)
    kv_own = jnp.concatenate([kv_own[:, :head], kv_own[:, head:] + b_value.astype(f32)], axis=1).astype(bf16)
    kv = kv_own
    for axis in ("ch", "cl", "ry", "rx"):
        kv = gather_axis(kv, axis)
    kv = kv.transpose(3, 2, 1, 0, 4, 5).reshape(length, 2 * head)
    keys, values = kv[:, :head], kv[:, head:]
    block_one = at.to_relative(block_gather(normed_one))
    queries = (dot_nn(block_one, query_weight) + query_bias).astype(bf16)
    attended, lse = attention.forward(bounds, queries, keys, values, low, pos)

    hidden_one = own + out_bias + block_scatter(at.to_absolute(dot_nn(attended, out_weight)))
    centred_two, inv_two = norm_parts(hidden_one)
    normed_two = (centred_two * gain_two + bias_two).astype(bf16)
    block_two = line_gather(normed_two)

    block_grad = line_gather(own_grad)
    upper = dot_nn(block_two, up_weight) + up_bias
    activated = gelu(upper).astype(bf16)
    grad_upper = (dot_nt(block_grad, down_weight) * gelu_slope(upper)).astype(bf16)
    grad_two = line_scatter(dot_nt(grad_upper, up_weight))
    grad_w_down = scatter_rows(dot_tn(activated, block_grad), 1)
    grad_w_up = scatter_rows(dot_tn(block_two, grad_upper), 0)
    final = hidden_one + down_bias + line_scatter(dot_nn(after(activated, grad_two), down_weight))
    output = lax.all_to_all(final.astype(bf16), row_axes, 1, 0, tiled=True)

    grad_hidden = own_grad.astype(f32) + norm_back(grad_two, centred_two, inv_two, gain_two)
    grad_branch = grad_hidden.astype(bf16)
    block_branch = at.to_relative(block_gather(grad_branch))
    grad_w_out = at.scatter_weight(dot_tn(attended, block_branch), 0)
    grad_att = dot_nt(block_branch, out_weight).astype(bf16)
    grad_query, grad_kv = attention.backward(
        bounds, queries, attended, grad_att, lse, keys, values, low, pos
    )
    grad_kv = grad_kv.reshape(blocks // 2, 2, rows // 2, 2, t, 2 * head)
    grad_kv = grad_kv.transpose(3, 1, 2, 0, 4, 5)
    for axis in ("rx", "cl", "ry", "ch"):
        grad_kv = scatter_axis(grad_kv, axis)
    kv_grad_own = grad_kv.astype(bf16)
    grad_one = block_scatter(at.to_absolute(dot_nt(grad_query, query_weight)))
    grad_one = grad_one + dot_nt(kv_grad_own, kv_weight)
    grad_w_query = at.scatter_weight(dot_tn(block_one, grad_query), 1)
    grad_own = grad_hidden + norm_back(grad_one, centred_one, inv_one, gain_one)
    grad_tokens = lax.all_to_all(grad_own.astype(bf16), row_axes, 1, 0, tiled=True).astype(f32)

    kv_part = dot_tn(normed_one, kv_grad_own).reshape(rows // 2, 2, row_width, 2 * head).transpose(1, 0, 2, 3)
    for axis in ("rx", "ry"):
        kv_part = scatter_axis(kv_part, axis)
    for axis in ("cl", "ch", "dp"):
        if lax.axis_size(axis) == 2:
            kv_part = kv_part.astype(bf16)
            kv_part = kv_part.astype(f32) + swap(kv_part, axis).astype(f32)
        else:
            kv_part = lax.psum(kv_part, axis)
    grad_w_keyval = kv_part

    sums = lambda a: jnp.sum(a.astype(f32), axis=0)
    early = jnp.concatenate(
        [
            lax.dynamic_update_slice_in_dim(
                jnp.zeros((b_up.shape[0] * blocks,), f32), sums(grad_upper), col * b_up.shape[0], 0
            ),
            sums(own_grad),
            sums(grad_branch),
            sums(grad_two * centred_two),
            sums(grad_two),
        ]
    )
    late = jnp.concatenate(
        [
            at.place_hidden(sums(grad_query), blocks),
            sums(grad_one * centred_one),
            sums(grad_one),
            sums(kv_grad_own[:, head:]),
        ]
    )
    early, late = sum_small(early), sum_small(late)
    hid = b_up.shape[0]
    of_col = lambda v, n: lax.dynamic_slice_in_dim(v, col * n, n, 0)
    of_row = lambda v, at_: lax.dynamic_slice_in_dim(v, at_ + row * row_width, row_width, 0)
    top = hid * blocks
    grad_b_up = of_col(early, hid)
    grad_b_down = of_row(early, top)
    grad_b_out = of_row(early, top + width)
    grad_ln2_gain = of_row(early, top + 2 * width)
    grad_ln2_bias = of_row(early, top + 3 * width)
    hid = b_query.shape[0]
    top = hid * blocks
    grad_b_query = of_col(late, hid)
    grad_ln1_gain = of_row(late, top)
    grad_ln1_bias = of_row(late, top + width)
    grad_b_value = late[top + 2 * width :]
    return (
        output,
        grad_tokens,
        grad_ln1_gain,
        grad_ln1_bias,
        grad_w_query,
        grad_b_query,
        grad_w_keyval,
        grad_b_value,
        grad_w_out,
        grad_b_out,
        grad_ln2_gain,
        grad_ln2_bias,
        grad_w_up,
        grad_b_up,
        grad_w_down,
        grad_b_down,
    )


def solution(mesh):
    dp, rows, cols = (mesh.shape[name] for name in ("dp", "row", "col"))
    fine = Mesh(
        mesh.devices.reshape(dp, rows // 2, 2, cols // 2, 2), ("dp", "ry", "rx", "ch", "cl")
    )
    row, col = ("ry", "rx"), ("ch", "cl")
    tok = P(("dp", "ch", "cl"), row)
    in_specs = (
        tok,
        P("dp", None),
        P(row),
        P(row),
        P(row, col),
        P(col),
        P(row, None),
        P(),
        P(col, row),
        P(row),
        P(row),
        P(row),
        P(row, col),
        P(col),
        P(col, row),
        P(row),
        tok,
    )
    out_specs = (
        tok,
        tok,
        P(row),
        P(row),
        P(row, col),
        P(col),
        P(row, None),
        P(),
        P(col, row),
        P(row),
        P(row),
        P(row),
        P(row, col),
        P(col),
        P(col, row),
        P(row),
    )
    return jax.shard_map(
        per_device, mesh=fine, in_specs=in_specs, out_specs=out_specs, check_vma=False
    )
```

time: 1670 us -> 639 us (0.38)
  waiting for transfers between devices: 1060 us -> 307 us
  blocking collectives: 205 us -> 0 us
  matrix products: 252 us -> 71.6 us
  starting transfers between devices: 1.38 us -> 123 us
  local copies, waits for them, and re-layouts: 68.6 us -> 45.4 us
    reduce_scatter x8 -> x2, waiting for transfers between devices: 637 us -> 0.02 us  [scatter_rows(): part = lax.psum_scatter(g, every, scatter_dimension=0, tiled=False)]
    all_gather x9 -> x2, waiting for transfers between devices: 423 us -> 0.01 us  [the longest x1 0.01 us: per_device(): up_weight = lax.all_gather(half_of(w_up, 0), every, axis=0, tiled=True)]
    ppermute x0 -> x80, waiting for transfers between devices: none -> 306 us  [the longest x56 176 us: swap(): return lax.ppermute(a, axis, [(0, 1), (1, 0)])]
    psum x7 -> x0, blocking collectives: 205 us -> none  [the longest x1 145 us: per_device(): grad_keyvals = lax.psum(keyval_part, ('row', 'col')).astype(jnp.bfloat16)]
    dot_general x159 -> x15, matrix products: 252 us -> 71.6 us  [the longest x5 24.6 us: dot_nt(): lax.dot_general(a, b, (((1,), (1,)), ((), ())), preferred_element_type=f32)]
    ppermute x0 -> x80, starting transfers between devices: none -> 107 us  [the longest x56 61.5 us: swap(): return lax.ppermute(a, axis, [(0, 1), (1, 0)])]
    gather x8 -> x0, local copies, waits for them, and re-layouts: 26.7 us -> none  [query_meta(): jnp.repeat(seg_block, heads_local, total_repeat_length=block_rows)]
  transfers between devices with their start and end apart: 18 -> 88, of which waited for: 17 -> 41; matrix products, arithmetic and copies ran while one was open for 5% -> 23% of each run, Pallas kernels for 0% -> 2%
where the time goes in v1:
time: 639 us; the launch traced here: 634 us
  waiting for transfers between devices  307 us (48%)
  starting transfers between devices  123 us (19%)
  matrix products  71.6 us (11%)
  other arithmetic  59.2 us (9%)
  local copies, waits for them, and re-layouts  45.4 us (7%)
  between operations  16.1 us (3%)
  Pallas kernels  12.8 us (2%)
    ppermute x56, waiting for transfers between devices, swap(): return lax.ppermute(a, axis, [(0, 1), (1, 0)])  176 us
    ppermute x10, waiting for transfers between devices, fetch(): return lax.ppermute(a, axis, [(s, (s - step) % n) for s in range(n)])  83.6 us
    ppermute x56, starting transfers between devices, swap(): return lax.ppermute(a, axis, [(0, 1), (1, 0)])  61.5 us
    dot_general x5, matrix products, dot_nt(): lax.dot_general(a, b, (((1,), (1,)), ((), ())), preferred_element_type=f32)  24.6 us
    dot_general x5, matrix products, dot_nn(): lax.dot_general(a, b, (((1,), (0,)), ((), ())), preferred_element_type=f32)  24.5 us
    dot_general x5, matrix products, dot_tn(): lax.dot_general(a, b, (((0,), (0,)), ((), ())), preferred_element_type=f32)  22.5 us
    ppermute x2, waiting for transfers between devices, line_scatter(): end = lax.ppermute(low[3 * t:], ('ch', 'cl'), [(0, 1), (3, 2)])  18.6 us
    ppermute x10, starting transfers between devices, fetch(): return lax.ppermute(a, axis, [(s, (s - step) % n) for s in range(n)])  17.4 us
  transfers between devices with their start and end apart: 88, of which 41 were waited for; matrix products, arithmetic and copies ran while one was open for 23% of the time, Pallas kernels for 2%

profile of v1, /device:TPU:0, one launch (start us, length us, event | category | flops | bytes accessed | tf_op | source)
XLA Modules:
  0.0 634.3 jit_solution(11704350098915908007)
XLA Ops:
  27.1 8.5 %collective-permute-done = bf16[6,512]{1,0:T(8,128)(2,1)S(1)} collective-permute-done((bf16[6,512]{1,0:T(8,128)(2,1)S(1)}, bf16[6,512]{1,0:T(8,128)(2,1)S(1)}, u32[]{:S(2)}, u32[]{:S(2)}) %collective-permute-start) | collective-permute-done | bytes 6176 | tf_op jit(solution)/shard_map/ppermute | solution.py:32
  41.4 4.1 collective-permute-done.12
  53.5 4.1 all-to-all-start.1
  63.2 10.6 %collective-permute-done.13 = bf16[2,512,256]{2,1,0:T(8,128)(2,1)} collective-permute-done((bf16[2,512,256]{2,1,0:T(8,128)(2,1)}, bf16[2,512,256]{2,1,0:T(8,128)(2,1)}, u32[]{:S(2)}, u32[]{:S(2)}) %collective-permute-start.13) | collective-permute-done | bytes 524320 | tf_op jit(solution)/shard_map/ppermute | solution.py:32
  75.5 8.3 %collective-permute-done.9 = bf16[1024,128]{1,0:T(8,128)(2,1)} collective-permute-done((bf16[1024,128]{1,0:T(8,128)(2,1)}, bf16[1024,128]{1,0:T(8,128)(2,1)}, u32[]{:S(2)}, u32[]{:S(2)}) %collective-permute-start.9) | collective-permute-done | bytes 262176 | tf_op jit(solution)/shard_map/ppermute | solution.py:41
  84.8 4.2 collective-permute-done.14
  91.0 10.8 %collective-permute-done.2 = bf16[128,2048]{1,0:T(8,128)(2,1)S(1)} collective-permute-done((bf16[128,2048]{1,0:T(8,128)(2,1)S(1)}, bf16[128,2048]{1,0:T(8,128)(2,1)S(1)}, u32[]{:S(2)}, u32[]{:S(2)}) %collective-permute-start.2) | collective-permute-done | bytes 524320 | tf_op jit(solution)/shard_map/ppermute | solution.py:32
  104.0 4.1 pad_maximum_fusion.4
  110.5 6.4 %collective-permute-done.18 = bf16[128,512]{1,0:T(8,128)(2,1)S(1)} collective-permute-done((bf16[128,512]{1,0:T(8,128)(2,1)S(1)}, bf16[128,512]{1,0:T(8,128)(2,1)S(1)}, u32[]{:S(2)}, u32[]{:S(2)}) %collective-permute-start.18) | collective-permute-done | bytes 131104 | tf_op jit(solution)/shard_map/ppermute | solution.py:32
  119.8 10.3 %collective-permute-done.19 = bf16[128,1024]{1,0:T(8,128)(2,1)S(1)} collective-permute-done((bf16[128,1024]{1,0:T(8,128)(2,1)S(1)}, bf16[128,1024]{1,0:T(8,128)(2,1)S(1)}, u32[]{:S(2)}, u32[]{:S(2)}) %collective-permute-start.19) | collective-permute-done | bytes 262176 | tf_op jit(solution)/shard_map/ppermute | solution.py:41
  130.6 4.6 collective-permute-done.17
  139.1 5.2 shard_map.288
  154.2 3.6 collective-permute-start.32
  160.4 15.6 %collective-permute-done.26 = bf16[128,2048]{1,0:T(8,128)(2,1)} collective-permute-done((bf16[128,2048]{1,0:T(8,128)(2,1)}, bf16[128,2048]{1,0:T(8,128)(2,1)}, u32[]{:S(2)}, u32[]{:S(2)}) %collective-permute-start.26) | collective-permute-done | bytes 524320 | tf_op jit(solution)/shard_map/ppermute | solution.py:36
  176.1 10.8 %collective-permute-done.25 = bf16[128,2048]{1,0:T(8,128)(2,1)} collective-permute-done((bf16[128,2048]{1,0:T(8,128)(2,1)}, bf16[128,2048]{1,0:T(8,128)(2,1)}, u32[]{:S(2)}, u32[]{:S(2)}) %collective-permute-start.25) | collective-permute-done | bytes 524320 | tf_op jit(solution)/shard_map/ppermute | solution.py:32
  196.6 21.5 %collective-permute-done.28 = bf16[128,2048]{1,0:T(8,128)(2,1)S(1)} collective-permute-done((bf16[128,2048]{1,0:T(8,128)(2,1)S(1)}, bf16[128,2048]{1,0:T(8,128)(2,1)S(1)}, u32[]{:S(2)}, u32[]{:S(2)}) %collective-permute-start.28) | collective-permute-done | bytes 524320 | tf_op jit(solution)/shard_map/ppermute | solution.py:32
  222.6 7.4 %collective-permute-start.31 = (bf16[128,2048]{1,0:T(8,128)(2,1)}, bf16[128,2048]{1,0:T(8,128)(2,1)}, u32[]{:S(2)}, u32[]{:S(2)}) collective-permute-start(bf16[128,2048]{1,0:T(8,128)(2,1)} %bitcast.83), channel_id=1, source_target_pairs={{0,1},{1,0},{2,3},{3,2},{4,5},{5,4},{6,7},{7,6},{8,9},{9,8},{10,11... | collective-permute-start | bytes 1572872 | tf_op jit(solution)/shard_map/ppermute | solution.py:32
  230.9 4.0 collective-permute-done.30
  235.8 10.4 %collective-permute-done.27 = bf16[128,2048]{1,0:T(8,128)(2,1)} collective-permute-done((bf16[128,2048]{1,0:T(8,128)(2,1)S(1)}, bf16[128,2048]{1,0:T(8,128)(2,1)}, u32[]{:S(2)}, u32[]{:S(2)}) %collective-permute-start.27) | collective-permute-done | bytes 524320 | tf_op jit(solution)/shard_map/ppermute | solution.py:32
  246.2 12.1 %multiply_convert_fusion = (bf16[512,2048]{1,0:T(8,128)(2,1)}, f32[512,2048]{1,0:T(8,128)}) fusion(f32[2048]{0:T(1024)S(1)} %convert_element_type.320, bf16[2048,2048]{1,0:T(8,128)(2,1)} %all-gather.3.cloned.1.call-done, bf16[128,2048]{1,0:T(8,128)(2,1)} %add.661, bf16[128,2048]{1,0:T(8,128)(2,1)} %copy-done.58, ...), kind=kOutput, calls=%fused_computation.14 | convolution fusion | flops 4313841664 | bytes 16785408 | tf_op jit(solution)/shard_map/dot_general | solution.py:20
  258.3 12.1 %convert_reduce_fusion = (f32[2048]{0:T(1024)S(1)}, bf16[512,2048]{1,0:T(8,128)(2,1)S(1)}) fusion(f32[512,2048]{1,0:T(8,128)} %get-tuple-element.227, f32[2048]{0:T(1024)S(1)} %convert_element_type.320, bf16[2048,2048]{1,0:T(8,128)(2,1)} %all-gather.5.cloned.1.call-done, bf16[128,2048]{1,0:T(8,128)(2,1)} %add.667, bf16[128,2048]{1,0:T(8,128)(2,1)} %copy-done.57, ...), kind=kOutput, calls=%fused_computation.13 | convolution fusion | flops 4326422528 | bytes 16793600 | tf_op jit(solution)/shard_map/dot_general | solution.py:24
  270.5 8.4 %convolution_convert_fusion.1 = bf16[2048,2048]{1,0:T(8,128)(2,1)} fusion(bf16[512,2048]{1,0:T(8,128)(2,1)S(1)} %get-tuple-element.231, bf16[128,2048]{1,0:T(8,128)(2,1)S(1)} %copy-done.18, bf16[128,2048]{1,0:T(8,128)(2,1)S(1)} %copy-done.59, bf16[128,2048]{1,0:T(8,128)(2,1)} %collective-permute-done.27, bf16[128,2048]{1,0:T(8,128)(2,1)S(1)} %copy-done.20), kind=kOutput, calls=%fused_computation.1 | convolution fusion | flops 4307550208 | bytes 12582912 | tf_op jit(solution)/shard_map/dot_general | solution.py:28
  278.9 7.6 %fusion.74 = (bf16[512,2048]{1,0:T(8,128)(2,1)S(1)}, f32[512,2048]{1,0:T(8,128)S(1)}) fusion(bf16[512,2048]{1,0:T(8,128)(2,1)} %copy-done.61, bf16[2048,2048]{1,0:T(8,128)(2,1)} %all-gather.3.cloned.1.call-done), kind=kOutput, calls=%fused_computation.271 | convolution fusion | flops 4296015872 | bytes 16777216 | tf_op jit(solution)/shard_map/dot_general | solution.py:24
  291.5 9.2 %collective-permute-done.36 = bf16[128,2048]{1,0:T(8,128)(2,1)S(1)} collective-permute-done((bf16[128,2048]{1,0:T(8,128)(2,1)S(1)}, bf16[128,2048]{1,0:T(8,128)(2,1)S(1)}, u32[]{:S(2)}, u32[]{:S(2)}) %collective-permute-start.36) | collective-permute-done | bytes 524320 | tf_op jit(solution)/shard_map/ppermute | solution.py:76
  300.8 4.0 collective-permute-start.37
  304.7 7.2 %collective-permute-done.35 = bf16[128,2048]{1,0:T(8,128)(2,1)S(1)} collective-permute-done((bf16[128,2048]{1,0:T(8,128)(2,1)S(1)}, bf16[128,2048]{1,0:T(8,128)(2,1)S(1)}, u32[]{:S(2)}, u32[]{:S(2)}) %collective-permute-start.35) | collective-permute-done | bytes 524320 | tf_op jit(solution)/shard_map/ppermute | solution.py:32
  311.9 6.1 collective-permute-done.37
  321.2 9.5 %fusion.75 = (bf16[512,2048]{1,0:T(8,128)(2,1)S(1)}, f32[512,2048]{1,0:T(8,128)}) fusion(bf16[512,2048]{1,0:T(8,128)(2,1)S(1)} %copy-done.62, bf16[2048,2048]{1,0:T(8,128)(2,1)} %all-gather.5.cloned.1.call-done), kind=kOutput, calls=%fused_computation.272 | convolution fusion | flops 4296015872 | bytes 16777216 | tf_op jit(solution)/shard_map/dot_general | solution.py:20
  331.8 8.8 %collective-permute-start.40 = (bf16[128,2048]{1,0:T(8,128)(2,1)}, bf16[128,2048]{1,0:T(8,128)(2,1)}, u32[]{:S(2)}, u32[]{:S(2)}) collective-permute-start(bf16[128,2048]{1,0:T(8,128)(2,1)} %get-tuple-element.156), channel_id=1, source_target_pairs={{0,1},{3,2},{4,5},{7,6},{8,9},{11,10},{12,13},{15,14},{16,17},{19,... | collective-permute-start | bytes 1572872 | tf_op jit(solution)/shard_map/ppermute | solution.py:76
  343.0 9.4 %collective-permute-done.40 = bf16[128,2048]{1,0:T(8,128)(2,1)} collective-permute-done((bf16[128,2048]{1,0:T(8,128)(2,1)}, bf16[128,2048]{1,0:T(8,128)(2,1)}, u32[]{:S(2)}, u32[]{:S(2)}) %collective-permute-start.40) | collective-permute-done | bytes 524320 | tf_op jit(solution)/shard_map/ppermute | solution.py:76
  357.6 6.0 collective-permute-done.39
  363.6 12.2 %collective-permute-done.41 = bf16[128,2048]{1,0:T(8,128)(2,1)S(1)} collective-permute-done((bf16[128,2048]{1,0:T(8,128)(2,1)S(1)}, bf16[128,2048]{1,0:T(8,128)(2,1)S(1)}, u32[]{:S(2)}, u32[]{:S(2)}) %collective-permute-start.41) | collective-permute-done | bytes 524320 | tf_op jit(solution)/shard_map/ppermute | solution.py:32
  375.8 4.2 convert_reduce_fusion.2
  385.9 4.2 collective-permute-done.75
  400.1 4.1 all-to-all-start.2
  407.1 10.1 %convolution_convert_fusion = bf16[2048,2048]{0,1:T(8,128)(2,1)} fusion(bf16[512,2048]{1,0:T(8,128)(2,1)} %get-tuple-element.24, bf16[128,2048]{1,0:T(8,128)(2,1)} %add.667, bf16[128,2048]{1,0:T(8,128)(2,1)} %copy-done.57, bf16[128,2048]{1,0:T(8,128)(2,1)} %collective-permute-done.31, bf16[128,2048]{1,0:T(8,128)(2,1)} %bitcast.83), kind=kOutput, calls=%fused_computation | convolution fusion | flops 4307550208 | bytes 12582912 | tf_op jit(solution)/shard_map/dot_general | solution.py:28
  417.2 11.4 %copy.88 = bf16[2048,8,256]{2,0,1:T(8,128)(2,1)} copy(bf16[2048,8,256]{0,2,1:T(8,128)(2,1)} %bitcast.161) | data formatting | bytes 16777216 | tf_op jit(solution)/shard_map/reshape | solution.py:123
  434.4 7.5 %shard_map.289 = (bf16[512,512]{1,0:T(8,128)(2,1)S(1)}, f32[2048,256]{1,0:T(8,128)S(1)}) custom-call(s32[4,2]{1,0:T(4,128)S(1)} %pad_add_fusion.1.bounds, bf16[512,512]{1,0:T(8,128)(2,1)S(1)} %fusion.7.q_ref, bf16[512,512]{1,0:T(8,128)(2,1)S(1)} %get-tuple-element.22.o_ref, bf16[512,512]{1,0:T(8,128)(2,1)S(1)} %convolution_convert_fusion.2.g_ref, ...), custom_call_target="tpu_custom_call" | custom-call | flops 5368709120 | bytes 8388608 | tf_op jit(solution)/shard_map/pallas_call | solution.py:343
  458.5 44.5 %collective-permute-done.49 = bf16[2,2,2,128,256]{4,3,2,1,0:T(8,128)(2,1)} collective-permute-done((bf16[2,2,2,128,256]{4,3,2,1,0:T(8,128)(2,1)S(1)}, bf16[2,2,2,128,256]{4,3,2,1,0:T(8,128)(2,1)}, u32[]{:S(2)}, u32[]{:S(2)}) %collective-permute-start.49) | collective-permute-done | bytes 524320 | tf_op jit(solution)/shard_map/ppermute | solution.py:41
  507.2 5.2 collective-permute-done.50
  512.6 7.2 %collective-permute-done.51 = bf16[2,128,256]{2,1,0:T(8,128)(2,1)S(1)} collective-permute-done((bf16[2,128,256]{2,1,0:T(8,128)(2,1)S(1)}, bf16[2,128,256]{2,1,0:T(8,128)(2,1)S(1)}, u32[]{:S(2)}, u32[]{:S(2)}) %collective-permute-start.51) | collective-permute-done | bytes 131104 | tf_op jit(solution)/shard_map/ppermute | solution.py:41
  519.9 9.1 %collective-permute-start.52 = (bf16[128,256]{1,0:T(8,128)(2,1)S(1)}, bf16[128,256]{1,0:T(8,128)(2,1)S(1)}, u32[]{:S(2)}, u32[]{:S(2)}) collective-permute-start(bf16[128,256]{1,0:T(8,128)(2,1)S(1)} %fusion.35), channel_id=1, source_target_pairs={{0,2},{2,0},{1,3},{3,1},{4,6},{6,4},{5,7},{7,5},{8,10},{10,8},{9,1... | collective-permute-start | bytes 196616 | tf_op jit(solution)/shard_map/ppermute | solution.py:41
  536.2 4.1 all-to-all-start.3
  543.8 5.6 collective-permute-done.54
  562.7 10.3 %collective-permute-done.57 = f32[6272]{0:T(1024)S(1)} collective-permute-done((f32[6272]{0:T(1024)S(1)}, f32[6272]{0:T(1024)S(1)}, u32[]{:S(2)}, u32[]{:S(2)}) %collective-permute-start.57) | collective-permute-done | bytes 25120 | tf_op jit(solution)/shard_map/ppermute | solution.py:32
  575.3 8.4 %collective-permute-done.69 = bf16[256,1024]{1,0:T(8,128)(2,1)S(1)} collective-permute-done((bf16[256,1024]{1,0:T(8,128)(2,1)S(1)}, bf16[256,1024]{1,0:T(8,128)(2,1)S(1)}, u32[]{:S(2)}, u32[]{:S(2)}) %collective-permute-start.69) | collective-permute-done | bytes 524320 | tf_op jit(solution)/shard_map/ppermute | solution.py:195
  587.1 6.1 collective-permute-done.60
  604.8 9.4 %collective-permute-done.66 = bf16[512,256]{1,0:T(8,128)(2,1)S(1)} collective-permute-done((bf16[512,256]{1,0:T(8,128)(2,1)S(1)}, bf16[512,256]{1,0:T(8,128)(2,1)S(1)}, u32[]{:S(2)}, u32[]{:S(2)}) %collective-permute-start.66) | collective-permute-done | bytes 262176 | tf_op jit(solution)/shard_map/ppermute | solution.py:32
  (451 shorter events, 199.8 us)
Async XLA Ops:
  7.3 238.9 %all-gather.3.cloned.1.call-start = ((), (), s32[]{:S(2)}) async-start(), calls=%async_computation.6 | async-start | bytes 9437184 | tf_op jit(solution)/shard_map/all_gather | solution.py:436
  10.9 29.2 %collective-permute-start.5 = (bf16[512,128]{1,0:T(8,128)(2,1)S(1)}, bf16[512,128]{1,0:T(8,128)(2,1)S(1)}, u32[]{:S(2)}, u32[]{:S(2)}) collective-permute-start(bf16[512,128]{1,0:T(8,128)(2,1)S(1)} %get-tuple-element.188), channel_id=1, source_target_pairs={{0,4},{4,0},{1,5},{5,1},{2,6},{6,2},{3,7},{7,3},{8,12},{12,8},{9,1... | collective-permute-start | bytes 393224 | tf_op jit(solution)/shard_map/ppermute | solution.py:32
  14.7 22.5 %collective-permute-start.11 = (bf16[256]{0:T(256)(128)(2,1)S(1)}, bf16[256]{0:T(256)(128)(2,1)S(1)}, u32[]{:S(2)}, u32[]{:S(2)}) collective-permute-start(bf16[256]{0:T(256)(128)(2,1)S(1)} %pad_maximum_fusion.34), channel_id=1, source_target_pairs={{0,2},{2,0},{1,3},{3,1},{4,6},{6,4},{5,7},{7,5},{8,10},{10,8},{9,1... | collective-permute-start | bytes 1544 | tf_op jit(solution)/shard_map/ppermute | solution.py:32
  17.4 36.1 %all-to-all-start = ((bf16[4,128,512]{2,1,0:T(8,128)(2,1)}), bf16[4,128,512]{2,1,0:T(8,128)(2,1)S(1)}, u32[]{:S(2)}, u32[]{:S(2)}) async-start(bf16[4,128,512]{2,1,0:T(8,128)(2,1)} %bitcast.173), calls=%async_computation | async-start | bytes 1048576 | tf_op jit(solution)/shard_map/all_to_all | solution.py:429
  20.9 237.4 %all-gather.5.cloned.1.call-start = ((), (), s32[]{:S(2)}) async-start(), calls=%async_computation.7 | async-start | bytes 9437184 | tf_op jit(solution)/shard_map/all_gather | solution.py:437
  23.1 22.5 %collective-permute-start.12 = (bf16[512,256]{1,0:T(8,128)(2,1)S(1)}, bf16[512,256]{1,0:T(8,128)(2,1)S(1)}, u32[]{:S(2)}, u32[]{:S(2)}) collective-permute-start(bf16[512,256]{1,0:T(8,128)(2,1)S(1)} %copy-done.37), channel_id=1, source_target_pairs={{0,4},{4,0},{1,5},{5,1},{2,6},{6,2},{3,7},{7,3},{8,12},{12,8},{9,1... | collective-permute-start | bytes 786440 | tf_op jit(solution)/shard_map/ppermute | solution.py:32
  46.4 27.4 %collective-permute-start.13 = (bf16[2,512,256]{2,1,0:T(8,128)(2,1)}, bf16[2,512,256]{2,1,0:T(8,128)(2,1)}, u32[]{:S(2)}, u32[]{:S(2)}) collective-permute-start(bf16[2,512,256]{2,1,0:T(8,128)(2,1)} %pad_maximum_fusion.14), channel_id=1, source_target_pairs={{0,8},{8,0},{1,9},{9,1},{2,10},{10,2},{3,11},{11,3},{4,12},{12,4},... | collective-permute-start | bytes 1572872 | tf_op jit(solution)/shard_map/ppermute | solution.py:32
  48.8 55.2 %collective-permute-start.7 = (bf16[2048,128]{1,0:T(8,128)(2,1)}, bf16[2048,128]{1,0:T(8,128)(2,1)}, u32[]{:S(2)}, u32[]{:S(2)}) collective-permute-start(bf16[2048,128]{1,0:T(8,128)(2,1)} %pad_maximum_fusion.13), channel_id=1, source_target_pairs={{0,16},{16,0},{1,17},{17,1},{2,18},{18,2},{3,19},{19,3},{4,20},{20... | collective-permute-start | bytes 1572872 | tf_op jit(solution)/shard_map/ppermute | solution.py:32
  50.4 33.4 %collective-permute-start.9 = (bf16[1024,128]{1,0:T(8,128)(2,1)}, bf16[1024,128]{1,0:T(8,128)(2,1)}, u32[]{:S(2)}, u32[]{:S(2)}) collective-permute-start(bf16[1024,128]{1,0:T(8,128)(2,1)} %collective-permute-done.8), channel_id=1, source_target_pairs={{0,8},{8,0},{1,9},{9,1},{2,10},{10,2},{3,11},{11,3},{4,12},{12,4},... | collective-permute-start | bytes 786440 | tf_op jit(solution)/shard_map/ppermute | solution.py:41
  53.5 98.8 %all-to-all-start.1 = ((bf16[4,128,512]{2,1,0:T(8,128)(2,1)}), bf16[4,128,512]{2,1,0:T(8,128)(2,1)}, u32[]{:S(2)}, u32[]{:S(2)}) async-start(bf16[4,128,512]{2,1,0:T(8,128)(2,1)} %bitcast.42), calls=%async_computation.1 | async-start | bytes 1048576 | tf_op jit(solution)/shard_map/all_to_all | solution.py:430
  57.6 543.9 %reduce-scatter.3.cloned.1.call-start = ((), (), s32[]{:S(2)}) async-start(), calls=%async_computation.8 | async-start | bytes 9437184 | tf_op jit(solution)/shard_map/reduce_scatter | solution.py:126
  59.1 29.9 %collective-permute-start.4 = (bf16[128,2048]{1,0:T(8,128)(2,1)S(1)}, bf16[128,2048]{1,0:T(8,128)(2,1)S(1)}, u32[]{:S(2)}, u32[]{:S(2)}) collective-permute-start(bf16[128,2048]{1,0:T(8,128)(2,1)S(1)} %add_convert_fusion.3), channel_id=1, source_target_pairs={{0,5},{1,4},{4,1},{5,0},{2,7},{3,6},{6,3},{7,2},{8,13},{9,12},{12,... | collective-permute-start | bytes 1572872 | tf_op jit(solution)/shard_map/ppermute | solution.py:36
  59.7 31.3 %collective-permute-start.3 = (bf16[128,2048]{1,0:T(8,128)(2,1)S(1)}, bf16[128,2048]{1,0:T(8,128)(2,1)S(1)}, u32[]{:S(2)}, u32[]{:S(2)}) collective-permute-start(bf16[128,2048]{1,0:T(8,128)(2,1)S(1)} %add_convert_fusion.3), channel_id=1, source_target_pairs={{0,1},{1,0},{2,3},{3,2},{4,5},{5,4},{6,7},{7,6},{8,9},{9,8},{10,11... | collective-permute-start | bytes 1572872 | tf_op jit(solution)/shard_map/ppermute | solution.py:32
  73.8 28.0 %collective-permute-start.2 = (bf16[128,2048]{1,0:T(8,128)(2,1)S(1)}, bf16[128,2048]{1,0:T(8,128)(2,1)S(1)}, u32[]{:S(2)}, u32[]{:S(2)}) collective-permute-start(bf16[128,2048]{1,0:T(8,128)(2,1)S(1)} %add_convert_fusion.3), channel_id=1, source_target_pairs={{0,4},{4,0},{1,5},{5,1},{2,6},{6,2},{3,7},{7,3},{8,12},{12,8},{9,1... | collective-permute-start | bytes 1572872 | tf_op jit(solution)/shard_map/ppermute | solution.py:32
  110.2 25.0 %collective-permute-start.17 = (bf16[2,2,2,128,256]{4,3,2,1,0:T(8,128)(2,1)S(1)}, bf16[2,2,2,128,256]{4,3,2,1,0:T(8,128)(2,1)S(1)}, u32[]{:S(2)}, u32[]{:S(2)}) collective-permute-start(bf16[2,2,2,128,256]{4,3,2,1,0:T(8,128)(2,1)S(1)} %pad_maximum_fusion.15), channel_id=1, source_target_pairs={{0,4},{4,0},{1,5},{5,1},{2,6},{6,2},{3,7},{7,3},{8,12},{12,8},{9,1... | collective-permute-start | bytes 1572872 | tf_op jit(solution)/shard_map/ppermute | solution.py:32
  148.8 27.3 %collective-permute-start.26 = (bf16[128,2048]{1,0:T(8,128)(2,1)}, bf16[128,2048]{1,0:T(8,128)(2,1)}, u32[]{:S(2)}, u32[]{:S(2)}) collective-permute-start(bf16[128,2048]{1,0:T(8,128)(2,1)} %get-tuple-element.160), channel_id=1, source_target_pairs={{0,5},{1,4},{4,1},{5,0},{2,7},{3,6},{6,3},{7,2},{8,13},{9,12},{12,... | collective-permute-start | bytes 1572872 | tf_op jit(solution)/shard_map/ppermute | solution.py:36
  151.2 35.7 %collective-permute-start.25 = (bf16[128,2048]{1,0:T(8,128)(2,1)}, bf16[128,2048]{1,0:T(8,128)(2,1)}, u32[]{:S(2)}, u32[]{:S(2)}) collective-permute-start(bf16[128,2048]{1,0:T(8,128)(2,1)} %get-tuple-element.161), channel_id=1, source_target_pairs={{0,1},{1,0},{2,3},{3,2},{4,5},{5,4},{6,7},{7,6},{8,9},{9,8},{10,11... | collective-permute-start | bytes 1572872 | tf_op jit(solution)/shard_map/ppermute | solution.py:32
  151.7 35.2 %collective-permute-start.24 = (bf16[128,2048]{1,0:T(8,128)(2,1)}, bf16[128,2048]{1,0:T(8,128)(2,1)}, u32[]{:S(2)}, u32[]{:S(2)}) collective-permute-start(bf16[128,2048]{1,0:T(8,128)(2,1)} %get-tuple-element.159), channel_id=1, source_target_pairs={{0,4},{4,0},{1,5},{5,1},{2,6},{6,2},{3,7},{7,3},{8,12},{12,8},{9,1... | collective-permute-start | bytes 1572872 | tf_op jit(solution)/shard_map/ppermute | solution.py:32
  154.2 40.4 %collective-permute-start.32 = (bf16[128,2048]{1,0:T(8,128)(2,1)}, bf16[128,2048]{1,0:T(8,128)(2,1)S(1)}, u32[]{:S(2)}, u32[]{:S(2)}) collective-permute-start(bf16[128,2048]{1,0:T(8,128)(2,1)} %bitcast.83), channel_id=1, source_target_pairs={{0,2},{2,0},{1,3},{3,1},{4,6},{6,4},{5,7},{7,5},{8,10},{10,8},{9,1... | collective-permute-start | bytes 1572872 | tf_op jit(solution)/shard_map/ppermute | solution.py:32
  191.1 27.0 %collective-permute-start.28 = (bf16[128,2048]{1,0:T(8,128)(2,1)S(1)}, bf16[128,2048]{1,0:T(8,128)(2,1)S(1)}, u32[]{:S(2)}, u32[]{:S(2)}) collective-permute-start(bf16[128,2048]{1,0:T(8,128)(2,1)S(1)} %add_convert_fusion.2), channel_id=1, source_target_pairs={{0,2},{2,0},{1,3},{3,1},{4,6},{6,4},{5,7},{7,5},{8,10},{10,8},{9,1... | collective-permute-start | bytes 1572872 | tf_op jit(solution)/shard_map/ppermute | solution.py:32
  193.9 28.6 %collective-permute-start.33 = (bf16[128,2048]{1,0:T(8,128)(2,1)}, bf16[128,2048]{1,0:T(8,128)(2,1)S(1)}, u32[]{:S(2)}, u32[]{:S(2)}) collective-permute-start(bf16[128,2048]{1,0:T(8,128)(2,1)} %bitcast.83), channel_id=1, source_target_pairs={{1,2},{2,1},{5,6},{6,5},{9,10},{10,9},{13,14},{14,13},{17,18},{18,... | collective-permute-start | bytes 1572872 | tf_op jit(solution)/shard_map/ppermute | solution.py:62
  194.6 35.3 %collective-permute-start.34 = (bf16[128,2048]{1,0:T(8,128)(2,1)S(1)}, bf16[128,2048]{1,0:T(8,128)(2,1)S(1)}, u32[]{:S(2)}, u32[]{:S(2)}) collective-permute-start(bf16[128,2048]{1,0:T(8,128)(2,1)S(1)} %collective-permute-done.32), channel_id=1, source_target_pairs={{1,0},{2,3},{5,4},{6,7},{9,8},{10,11},{13,12},{14,15},{17,16},{18,... | collective-permute-start | bytes 1572872 | tf_op jit(solution)/shard_map/ppermute | solution.py:69
  195.9 34.9 %collective-permute-start.29 = (bf16[128,2048]{1,0:T(8,128)(2,1)S(1)}, bf16[128,2048]{1,0:T(8,128)(2,1)S(1)}, u32[]{:S(2)}, u32[]{:S(2)}) collective-permute-start(bf16[128,2048]{1,0:T(8,128)(2,1)S(1)} %add_convert_fusion.2), channel_id=1, source_target_pairs={{1,2},{2,1},{5,6},{6,5},{9,10},{10,9},{13,14},{14,13},{17,18},{18,... | collective-permute-start | bytes 1572872 | tf_op jit(solution)/shard_map/ppermute | solution.py:62
  219.8 26.4 %collective-permute-start.27 = (bf16[128,2048]{1,0:T(8,128)(2,1)S(1)}, bf16[128,2048]{1,0:T(8,128)(2,1)}, u32[]{:S(2)}, u32[]{:S(2)}) collective-permute-start(bf16[128,2048]{1,0:T(8,128)(2,1)S(1)} %add_convert_fusion.2), channel_id=1, source_target_pairs={{0,1},{1,0},{2,3},{3,2},{4,5},{5,4},{6,7},{7,6},{8,9},{9,8},{10,11... | collective-permute-start | bytes 1572872 | tf_op jit(solution)/shard_map/ppermute | solution.py:32
  222.6 35.7 %collective-permute-start.31 = (bf16[128,2048]{1,0:T(8,128)(2,1)}, bf16[128,2048]{1,0:T(8,128)(2,1)}, u32[]{:S(2)}, u32[]{:S(2)}) collective-permute-start(bf16[128,2048]{1,0:T(8,128)(2,1)} %bitcast.83), channel_id=1, source_target_pairs={{0,1},{1,0},{2,3},{3,2},{4,5},{5,4},{6,7},{7,6},{8,9},{9,8},{10,11... | collective-permute-start | bytes 1572872 | tf_op jit(solution)/shard_map/ppermute | solution.py:32
  289.0 22.9 %collective-permute-start.35 = (bf16[128,2048]{1,0:T(8,128)(2,1)S(1)}, bf16[128,2048]{1,0:T(8,128)(2,1)S(1)}, u32[]{:S(2)}, u32[]{:S(2)}) collective-permute-start(bf16[128,2048]{1,0:T(8,128)(2,1)S(1)} %get-tuple-element.157), channel_id=1, source_target_pairs={{0,1},{1,0},{2,3},{3,2},{4,5},{5,4},{6,7},{7,6},{8,9},{9,8},{10,11... | collective-permute-start | bytes 1572872 | tf_op jit(solution)/shard_map/ppermute | solution.py:32
  300.8 17.2 %collective-permute-start.37 = (bf16[128,2048]{1,0:T(8,128)(2,1)S(1)}, bf16[128,2048]{1,0:T(8,128)(2,1)S(1)}, u32[]{:S(2)}, u32[]{:S(2)}) collective-permute-start(bf16[128,2048]{1,0:T(8,128)(2,1)S(1)} %fusion.16), channel_id=1, source_target_pairs={{0,2},{2,0},{1,3},{3,1},{4,6},{6,4},{5,7},{7,5},{8,10},{10,8},{9,1... | collective-permute-start | bytes 1572872 | tf_op jit(solution)/shard_map/ppermute | solution.py:32
  331.8 20.6 %collective-permute-start.40 = (bf16[128,2048]{1,0:T(8,128)(2,1)}, bf16[128,2048]{1,0:T(8,128)(2,1)}, u32[]{:S(2)}, u32[]{:S(2)}) collective-permute-start(bf16[128,2048]{1,0:T(8,128)(2,1)} %get-tuple-element.156), channel_id=1, source_target_pairs={{0,1},{3,2},{4,5},{7,6},{8,9},{11,10},{12,13},{15,14},{16,17},{19,... | collective-permute-start | bytes 1572872 | tf_op jit(solution)/shard_map/ppermute | solution.py:76
  342.9 20.7 %collective-permute-start.39 = (bf16[128,2048]{1,0:T(8,128)(2,1)}, bf16[128,2048]{1,0:T(8,128)(2,1)S(1)}, u32[]{:S(2)}, u32[]{:S(2)}) collective-permute-start(bf16[128,2048]{1,0:T(8,128)(2,1)} %get-tuple-element.155), channel_id=1, source_target_pairs={{0,1},{1,0},{2,3},{3,2},{4,5},{5,4},{6,7},{7,6},{8,9},{9,8},{10,11... | collective-permute-start | bytes 1572872 | tf_op jit(solution)/shard_map/ppermute | solution.py:32
  353.9 21.9 %collective-permute-start.41 = (bf16[128,2048]{1,0:T(8,128)(2,1)S(1)}, bf16[128,2048]{1,0:T(8,128)(2,1)S(1)}, u32[]{:S(2)}, u32[]{:S(2)}) collective-permute-start(bf16[128,2048]{1,0:T(8,128)(2,1)S(1)} %fusion.11), channel_id=1, source_target_pairs={{0,2},{2,0},{1,3},{3,1},{4,6},{6,4},{5,7},{7,5},{8,10},{10,8},{9,1... | collective-permute-start | bytes 1572872 | tf_op jit(solution)/shard_map/ppermute | solution.py:32
  394.7 36.1 %collective-permute-start.45 = (bf16[128,2048]{1,0:T(8,128)(2,1)}, bf16[128,2048]{1,0:T(8,128)(2,1)}, u32[]{:S(2)}, u32[]{:S(2)}) collective-permute-start(bf16[128,2048]{1,0:T(8,128)(2,1)} %get-tuple-element.123), channel_id=1, source_target_pairs={{0,5},{1,4},{4,1},{5,0},{2,7},{3,6},{6,3},{7,2},{8,13},{9,12},{12,... | collective-permute-start | bytes 1572872 | tf_op jit(solution)/shard_map/ppermute | solution.py:36
  397.2 33.6 %collective-permute-start.44 = (bf16[128,2048]{1,0:T(8,128)(2,1)}, bf16[128,2048]{1,0:T(8,128)(2,1)}, u32[]{:S(2)}, u32[]{:S(2)}) collective-permute-start(bf16[128,2048]{1,0:T(8,128)(2,1)} %get-tuple-element.123), channel_id=1, source_target_pairs={{0,1},{1,0},{2,3},{3,2},{4,5},{5,4},{6,7},{7,6},{8,9},{9,8},{10,11... | collective-permute-start | bytes 1572872 | tf_op jit(solution)/shard_map/ppermute | solution.py:32
  397.5 33.3 %collective-permute-start.43 = (bf16[128,2048]{1,0:T(8,128)(2,1)}, bf16[128,2048]{1,0:T(8,128)(2,1)}, u32[]{:S(2)}, u32[]{:S(2)}) collective-permute-start(bf16[128,2048]{1,0:T(8,128)(2,1)} %get-tuple-element.123), channel_id=1, source_target_pairs={{0,4},{4,0},{1,5},{5,1},{2,6},{6,2},{3,7},{7,3},{8,12},{12,8},{9,1... | collective-permute-start | bytes 1572872 | tf_op jit(solution)/shard_map/ppermute | solution.py:32
  400.1 30.7 %all-to-all-start.2 = ((bf16[128,4,512]{2,0,1:T(8,128)(2,1)}), bf16[128,4,512]{2,0,1:T(8,128)(2,1)}, u32[]{:S(2)}, u32[]{:S(2)}) async-start(bf16[128,4,512]{2,0,1:T(8,128)(2,1)} %bitcast.168), calls=%async_computation.2 | async-start | bytes 1048576 | tf_op jit(solution)/shard_map/all_to_all | solution.py:482
  404.2 213.8 %reduce-scatter.5.cloned.1.call-start = ((), (), s32[]{:S(2)}) async-start(), calls=%async_computation.9 | async-start | bytes 9437184 | tf_op jit(solution)/shard_map/reduce_scatter | solution.py:126
  405.2 23.5 %collective-permute-start.77 = (f32[16384]{0:T(1024)S(1)}, f32[16384]{0:T(1024)}, u32[]{:S(2)}, u32[]{:S(2)}) collective-permute-start(f32[16384]{0:T(1024)S(1)} %add.735), channel_id=1, source_target_pairs={{0,8},{8,0},{1,9},{9,1},{2,10},{10,2},{3,11},{11,3},{4,12},{12,4},... | collective-permute-start | bytes 196616 | tf_op jit(solution)/shard_map/ppermute | solution.py:32
  447.3 84.6 %collective-permute-start.48 = (bf16[128,2048]{1,0:T(8,128)(2,1)}, bf16[128,2048]{1,0:T(8,128)(2,1)}, u32[]{:S(2)}, u32[]{:S(2)}) collective-permute-start(bf16[128,2048]{1,0:T(8,128)(2,1)} %get-tuple-element.149), channel_id=1, source_target_pairs={{0,5},{1,4},{4,1},{5,0},{2,7},{3,6},{6,3},{7,2},{8,13},{9,12},{12,... | collective-permute-start | bytes 1572872 | tf_op jit(solution)/shard_map/ppermute | solution.py:36
  450.0 81.8 %collective-permute-start.47 = (bf16[128,2048]{1,0:T(8,128)(2,1)}, bf16[128,2048]{1,0:T(8,128)(2,1)}, u32[]{:S(2)}, u32[]{:S(2)}) collective-permute-start(bf16[128,2048]{1,0:T(8,128)(2,1)} %get-tuple-element.150), channel_id=1, source_target_pairs={{0,1},{1,0},{2,3},{3,2},{4,5},{5,4},{6,7},{7,6},{8,9},{9,8},{10,11... | collective-permute-start | bytes 1572872 | tf_op jit(solution)/shard_map/ppermute | solution.py:32
  450.1 81.7 %collective-permute-start.46 = (bf16[128,2048]{1,0:T(8,128)(2,1)}, bf16[128,2048]{1,0:T(8,128)(2,1)}, u32[]{:S(2)}, u32[]{:S(2)}) collective-permute-start(bf16[128,2048]{1,0:T(8,128)(2,1)} %get-tuple-element.148), channel_id=1, source_target_pairs={{0,4},{4,0},{1,5},{5,1},{2,6},{6,2},{3,7},{7,3},{8,12},{12,8},{9,1... | collective-permute-start | bytes 1572872 | tf_op jit(solution)/shard_map/ppermute | solution.py:32
  450.8 52.2 %collective-permute-start.49 = (bf16[2,2,2,128,256]{4,3,2,1,0:T(8,128)(2,1)S(1)}, bf16[2,2,2,128,256]{4,3,2,1,0:T(8,128)(2,1)}, u32[]{:S(2)}, u32[]{:S(2)}) collective-permute-start(bf16[2,2,2,128,256]{4,3,2,1,0:T(8,128)(2,1)S(1)} %fusion.24), channel_id=1, source_target_pairs={{0,4},{4,0},{1,5},{5,1},{2,6},{6,2},{3,7},{7,3},{8,12},{12,8},{9,1... | collective-permute-start | bytes 1572872 | tf_op jit(solution)/shard_map/ppermute | solution.py:41
  453.4 102.4 %collective-permute-start.58 = (bf16[2048,256]{0,1:T(8,128)(2,1)}, bf16[2048,256]{0,1:T(8,128)(2,1)}, u32[]{:S(2)}, u32[]{:S(2)}) collective-permute-start(bf16[2048,256]{0,1:T(8,128)(2,1)} %pad_maximum_fusion.11), channel_id=1, source_target_pairs={{0,16},{16,0},{1,17},{17,1},{2,18},{18,2},{3,19},{19,3},{4,20},{20... | collective-permute-start | bytes 3145736 | tf_op jit(solution)/shard_map/ppermute | solution.py:32
  531.8 27.9 %collective-permute-start.68 = (bf16[256,2048]{1,0:T(8,128)(2,1)}, bf16[256,2048]{1,0:T(8,128)(2,1)}, u32[]{:S(2)}, u32[]{:S(2)}) collective-permute-start(bf16[256,2048]{1,0:T(8,128)(2,1)} %pad_maximum_fusion.12), channel_id=1, source_target_pairs={{0,16},{16,0},{1,17},{17,1},{2,18},{18,2},{3,19},{19,3},{4,20},{20... | collective-permute-start | bytes 3145736 | tf_op jit(solution)/shard_map/ppermute | solution.py:32
  536.2 61.8 %all-to-all-start.3 = ((bf16[128,4,512]{2,0,1:T(8,128)(2,1)}), bf16[128,4,512]{2,0,1:T(8,128)(2,1)}, u32[]{:S(2)}, u32[]{:S(2)}) async-start(bf16[128,4,512]{2,0,1:T(8,128)(2,1)} %bitcast.167), calls=%async_computation.3 | async-start | bytes 1048576 | tf_op jit(solution)/shard_map/all_to_all | solution.py:501
  549.5 23.6 %collective-permute-start.63 = (bf16[2,512,256]{2,1,0:T(8,128)(2,1)S(1)}, bf16[2,512,256]{2,1,0:T(8,128)(2,1)S(1)}, u32[]{:S(2)}, u32[]{:S(2)}) collective-permute-start(bf16[2,512,256]{2,1,0:T(8,128)(2,1)S(1)} %fusion.23), channel_id=1, source_target_pairs={{0,4},{4,0},{1,5},{5,1},{2,6},{6,2},{3,7},{7,3},{8,12},{12,8},{9,1... | collective-permute-start | bytes 1572872 | tf_op jit(solution)/shard_map/ppermute | solution.py:41
  557.5 17.3 %collective-permute-start.59 = (bf16[1024,256]{0,1:T(8,128)(2,1)S(1)}, bf16[1024,256]{0,1:T(8,128)(2,1)S(1)}, u32[]{:S(2)}, u32[]{:S(2)}) collective-permute-start(bf16[1024,256]{0,1:T(8,128)(2,1)S(1)} %slice.372), channel_id=1, source_target_pairs={{0,8},{8,0},{1,9},{9,1},{2,10},{10,2},{3,11},{11,3},{4,12},{12,4},... | collective-permute-start | bytes 1572872 | tf_op jit(solution)/shard_map/ppermute | solution.py:195
  561.2 22.5 %collective-permute-start.69 = (bf16[256,1024]{1,0:T(8,128)(2,1)S(1)}, bf16[256,1024]{1,0:T(8,128)(2,1)S(1)}, u32[]{:S(2)}, u32[]{:S(2)}) collective-permute-start(bf16[256,1024]{1,0:T(8,128)(2,1)S(1)} %slice.371), channel_id=1, source_target_pairs={{0,8},{8,0},{1,9},{9,1},{2,10},{10,2},{3,11},{11,3},{4,12},{12,4},... | collective-permute-start | bytes 1572872 | tf_op jit(solution)/shard_map/ppermute | solution.py:195
  574.9 18.3 %collective-permute-start.60 = (bf16[1024,128]{0,1:T(8,128)(2,1)S(1)}, bf16[1024,128]{0,1:T(8,128)(2,1)S(1)}, u32[]{:S(2)}, u32[]{:S(2)}) collective-permute-start(bf16[1024,128]{0,1:T(8,128)(2,1)S(1)} %slice.374), channel_id=1, source_target_pairs={{0,2},{2,0},{1,3},{3,1},{4,6},{6,4},{5,7},{7,5},{8,10},{10,8},{9,1... | collective-permute-start | bytes 786440 | tf_op jit(solution)/shard_map/ppermute | solution.py:32
  601.5 18.7 %collective-permute-start.78 = (bf16[256,2048]{1,0:T(8,128)(2,1)}, bf16[256,2048]{1,0:T(8,128)(2,1)S(1)}, u32[]{:S(2)}, u32[]{:S(2)}) collective-permute-start(bf16[256,2048]{1,0:T(8,128)(2,1)} %bitcast.170), channel_id=1, source_target_pairs={{0,16},{16,0},{1,17},{17,1},{2,18},{18,2},{3,19},{19,3},{4,20},{20... | collective-permute-start | bytes 3145736 | tf_op jit(solution)/shard_map/ppermute | solution.py:32
  (103 other events, 1281.7 us)
Sparse Core Ops, SparseCore 0:
  10.6 90.9 all-gather.2
  103.5 85.7 all-gather.4
  279.0 70.8 reduce-scatter.2
  428.7 101.3 reduce-scatter.4

commit v2 on v1

v2 whole, which is shorter than its diff:
```python
import functools
import math

import jax
import jax.numpy as jnp
from jax import lax
from jax.experimental import pallas as pl
from jax.experimental.pallas import tpu as pltpu
from jax.sharding import Mesh
from jax.sharding import PartitionSpec as P

epsilon = 1e-05
negative = -1e30
log2e = math.log2(math.e)
f32 = jnp.float32
bf16 = jnp.bfloat16


def dot_nn(a, b):
    return lax.dot_general(a, b, (((1,), (0,)), ((), ())), preferred_element_type=f32)


def dot_nt(a, b):
    return lax.dot_general(a, b, (((1,), (1,)), ((), ())), preferred_element_type=f32)


def dot_tn(a, b):
    return lax.dot_general(a, b, (((0,), (0,)), ((), ())), preferred_element_type=f32)


def swap(a, axis):
    return lax.ppermute(a, axis, [(0, 1), (1, 0)])


def fetch(a, axis, step):
    n = lax.axis_size(axis)
    return lax.ppermute(a, axis, [(s, (s - step) % n) for s in range(n)])


def tie(*arrays):
    return jax.tree.unflatten(
        jax.tree.structure(arrays), lax.optimization_barrier(tuple(jax.tree.leaves(arrays)))
    )


def add(u, v):
    return (u.astype(f32) + v.astype(f32)).astype(bf16)


def end_swap(a):
    return lax.ppermute(a, ("ch", "cl"), [(1, 2), (2, 1)])


def line_first(a):
    return swap(a, "ch"), swap(a, "cl"), end_swap(a)


def line_second(a, far, near, mid):
    end = lax.ppermute(far, ("ch", "cl"), [(1, 0), (2, 3)])
    return jnp.concatenate([a, near, far, mid + end], axis=0)


def line_scatter_first(p):
    t = p.shape[0] // 4
    end = lax.ppermute(p[3 * t :], ("ch", "cl"), [(0, 1), (3, 2)])
    return end, swap(p[t : 2 * t], "cl"), end_swap(p[3 * t :])


def line_scatter_second(p, end):
    t = p.shape[0] // 4
    return swap(add(p[2 * t : 3 * t], end), "ch")


def line_total(p, near, mid, far):
    t = p.shape[0] // 4
    return p[:t].astype(f32) + near.astype(f32) + far.astype(f32) + mid.astype(f32)


def gather_axis(a, axis):
    n = lax.axis_size(axis)
    if n == 2:
        b = swap(a, axis)
        first = lax.axis_index(axis) == 0
        return jnp.stack([jnp.where(first, a, b), jnp.where(first, b, a)])
    return lax.all_gather(a, axis, axis=0, tiled=False)


def row_send(a, k, rows):
    n, j, i = rows // 2, k // 2, k % 2
    pairs = [(y * 2 + x, (y + j) % n * 2 + (x ^ i)) for y in range(n) for x in range(2)]
    return lax.ppermute(a, ("ry", "rx"), pairs)


def half_of(w, axis):
    n = w.shape[axis] // 2
    return lax.dynamic_slice_in_dim(w, lax.axis_index("dp") * n, n, axis)


def scatter_row(g, feat):
    return lax.psum_scatter(g, ("ry", "rx", "dp"), scatter_dimension=feat, tiled=True)


class Place:
    def __init__(self):
        self.dp = lax.axis_index("dp")
        self.ry = lax.axis_index("ry")
        self.rx = lax.axis_index("rx")
        self.ch = lax.axis_index("ch")
        self.cl = lax.axis_index("cl")
        self.rows_y = lax.axis_size("ry")
        self.rows = 2 * self.rows_y

    def row_of(self, k):
        return ((self.ry + k // 2) % self.rows_y) * 2 + (self.rx ^ (k % 2))

    def row_from(self, k):
        return ((self.ry - k // 2) % self.rows_y) * 2 + (self.rx ^ (k % 2))

    def slot_from(self, r):
        return ((self.ry - r // 2) % self.rows_y) * 2 + (self.rx ^ (r % 2))

    def both_cores(self, part, feat):
        pair = gather_axis(part, "dp")
        return jnp.concatenate([pair[0], pair[1]], axis=feat).astype(f32)

    def by_tokens(self, got, col, t):
        got = jnp.concatenate(got, axis=0)
        at = lambda c, r: (self.slot_from(r) * 4 + (col ^ c)) * t
        return jnp.concatenate(
            [lax.dynamic_slice_in_dim(got, at(c, r), t, 0) for c in range(4) for r in range(self.rows)], axis=0
        )

    def sum_rows(self, lines):
        pair = lambda y: jnp.concatenate([lines(2 * y), lines(2 * y + 1)], axis=0)
        total = pair(self.ry).astype(f32)
        for j in range(1, self.rows_y):
            total = total + row_send(pair((self.ry + j) % self.rows_y), 2 * j, self.rows).astype(f32)
        n = total.shape[0] // 2
        cut = lambda x: lax.dynamic_slice_in_dim(total, x * n, n, 0)
        return cut(self.rx) + swap(cut(1 - self.rx).astype(bf16), "rx").astype(f32)

    def line_tokens(self, a, col, r, t):
        return jnp.concatenate(
            [lax.dynamic_slice_in_dim(a, ((col ^ k) * self.rows + r) * t, t, 0) for k in range(4)], axis=0
        )

    def exchange(self, *parts):
        got = []
        for k in range(self.rows):
            r = self.row_of(k)
            part = jnp.concatenate([p(r) for p in parts], axis=0) if len(parts) > 1 else parts[0](r)
            got.append(row_send(part, k, self.rows) if k else part)
        return got

    def by_lanes(self, got, lo, hi):
        w = got[0].shape[1]
        got = jnp.concatenate([g[lo:hi] for g in got], axis=1)
        return jnp.concatenate(
            [lax.dynamic_slice_in_dim(got, self.slot_from(r) * w, w, 1) for r in range(self.rows)], axis=1
        )

    def by_rows(self, got, lo, hi):
        n = hi - lo
        got = jnp.concatenate([g[lo:hi] for g in got], axis=0)
        return jnp.concatenate(
            [lax.dynamic_slice_in_dim(got, self.slot_from(r) * n, n, 0) for r in range(self.rows)], axis=0
        )


def multiply(x, w, kind, cost=None):
    def body(x_ref, w_ref, o_ref):
        dot = {"nn": dot_nn, "nt": dot_nt, "tn": dot_tn}[kind]
        o_ref[...] = dot(x_ref[...], w_ref[...]).astype(bf16)

    whole = lambda a: pl.BlockSpec(a.shape, lambda i: (0, 0))
    if kind == "tn":
        m, n, k = x.shape[1], w.shape[1], x.shape[0]
        tile = min(512, m)
        specs = [pl.BlockSpec((k, tile), lambda i: (0, i)), whole(w)]
        out_spec, steps = pl.BlockSpec((tile, n), lambda i: (i, 0)), m // tile
    else:
        m, k = x.shape
        n = w.shape[1] if kind == "nn" else w.shape[0]
        tile = min(512, n)
        by_col, by_row = pl.BlockSpec((k, tile), lambda i: (0, i)), pl.BlockSpec((tile, k), lambda i: (i, 0))
        specs = [whole(x), by_col if kind == "nn" else by_row]
        out_spec, steps = pl.BlockSpec((m, tile), lambda i: (0, i)), n // tile
    return pl.pallas_call(
        body,
        grid=(steps,),
        in_specs=specs,
        out_specs=out_spec,
        out_shape=jax.ShapeDtypeStruct((m, n), bf16),
        compiler_params=pltpu.CompilerParams(
            dimension_semantics=("arbitrary",), vmem_limit_bytes=24 * 1024 * 1024
        ),
        cost_estimate=pl.CostEstimate(
            flops=2 * m * n * k if cost is None else cost,
            bytes_accessed=2 * (m * n + m * k + n * k) if cost is None else cost,
            transcendentals=0,
        ),
    )(x, w)


def feed_forward(x, w, bias, grad_act):
    (m, k), n = x.shape, w.shape[1]
    tile = min(256, n)

    def body(x_ref, w_ref, b_ref, g_ref, a_ref, u_ref):
        u = dot_nn(x_ref[...], w_ref[...]) + b_ref[...]
        square = u * u
        th = jnp.tanh(gelu_a * u * (1.0 + gelu_b * square))
        half = 0.5 * (1.0 + th)
        a_ref[...] = (u * half).astype(bf16)
        slope = half + 0.5 * u * (1.0 - th * th) * (gelu_a + 3.0 * gelu_a * gelu_b * square)
        u_ref[...] = (g_ref[...].astype(f32) * slope).astype(bf16)

    cols = lambda rows: pl.BlockSpec((rows, tile), lambda i: (0, i))
    return pl.pallas_call(
        body,
        grid=(n // tile,),
        in_specs=[pl.BlockSpec((m, k), lambda i: (0, 0)), cols(k), cols(1), cols(m)],
        out_specs=[cols(m), cols(m)],
        out_shape=[jax.ShapeDtypeStruct((m, n), bf16)] * 2,
        compiler_params=pltpu.CompilerParams(
            dimension_semantics=("arbitrary",), vmem_limit_bytes=24 * 1024 * 1024
        ),
        cost_estimate=pl.CostEstimate(
            flops=2 * m * n * k, bytes_accessed=2 * (3 * m * n + m * k + n * k), transcendentals=m * n
        ),
    )(x, w, bias, grad_act)


def stack_heads(a, heads):
    w = a.shape[1] // heads
    return jnp.concatenate([a[:, h * w : (h + 1) * w] for h in range(heads)], axis=0)


def attend_forward(
    bounds, q_ref, k_ref, v_ref, low_ref, pos_ref, o_ref, lse_ref, *, heads, span, scale
):
    chunk = pl.program_id(0)
    rows = stack_heads(q_ref[...], heads)
    n, width = rows.shape
    low = jnp.concatenate([low_ref[0]] * heads, axis=1)
    pos = jnp.concatenate([pos_ref[0]] * heads, axis=1)

    def step(kb, state):
        top, total, acc = state
        start = pl.multiple_of(kb * span, span)
        keys = k_ref[pl.ds(start, span), :]
        values = v_ref[pl.ds(start, span), :]
        s = dot_nt(keys, rows) * scale
        at = start + lax.broadcasted_iota(jnp.int32, (span, n), 0)
        s = jnp.where((at >= low) & (at <= pos), s, negative)
        new = jnp.maximum(top, jnp.max(s, axis=0, keepdims=True))
        p = jnp.exp2(s - new)
        fade = jnp.exp2(top - new)
        total = total * fade + jnp.sum(p, axis=0, keepdims=True)
        acc = acc * fade + dot_tn(values, p.astype(bf16))
        return new, total, acc

    start_state = (
        jnp.full((1, n), negative, f32),
        jnp.zeros((1, n), f32),
        jnp.zeros((width, n), f32),
    )
    top, total, acc = lax.fori_loop(bounds[chunk, 0], bounds[chunk, 1], step, start_state)
    out = (acc / total).T.astype(bf16)
    t = n // heads
    for h in range(heads):
        o_ref[:, h * width : (h + 1) * width] = out[h * t : (h + 1) * t]
    lse_ref[0] = top + jnp.log2(total)


def attend_backward(
    bounds, q_ref, o_ref, g_ref, lse_ref, k_ref, v_ref, low_ref, pos_ref, dq_ref, dkv_ref, *, heads, span, scale, plain
):
    chunk = pl.program_id(0)

    @pl.when(chunk == 0)
    def _():
        dkv_ref[...] = jnp.zeros_like(dkv_ref)

    rows = stack_heads(q_ref[...], heads)
    outs = stack_heads(o_ref[...], heads)
    grads = stack_heads(g_ref[...], heads)
    n, width = rows.shape
    low = jnp.concatenate([low_ref[0]] * heads, axis=1)
    pos = jnp.concatenate([pos_ref[0]] * heads, axis=1)
    lse = lse_ref[0]
    delta = jnp.sum((outs.astype(f32) * grads.astype(f32)).T, axis=0, keepdims=True)

    def step(kb, acc):
        start = pl.multiple_of(kb * span, span)
        keys = k_ref[pl.ds(start, span), :]
        values = v_ref[pl.ds(start, span), :]
        s = dot_nt(keys, rows) * scale
        at = start + lax.broadcasted_iota(jnp.int32, (span, n), 0)
        p = jnp.where((at >= low) & (at <= pos), jnp.exp2(s - lse), 0.0)
        dp = dot_nt(values, grads)
        ds = (p * (dp - delta)).astype(bf16)
        acc = acc + dot_tn(keys, ds)
        dkv_ref[pl.ds(start, span), :width] += dot_nn(ds, rows) * plain
        dkv_ref[pl.ds(start, span), width:] += dot_nn(p.astype(bf16), grads)
        return acc

    acc = lax.fori_loop(bounds[chunk, 0], bounds[chunk, 1], step, jnp.zeros((width, n), f32))
    out = (acc * plain).T.astype(bf16)
    t = n // heads
    for h in range(heads):
        dq_ref[:, h * width : (h + 1) * width] = out[h * t : (h + 1) * t]


class Attention:
    def __init__(self, tokens, chunks, hidden, length, head):
        self.t, self.chunks, self.hidden, self.length, self.head = tokens, chunks, hidden, length, head
        self.heads = hidden // head
        self.span = min(512, length)
        self.plain = head ** (-0.5)
        self.scale = self.plain * log2e
        self.params = pltpu.CompilerParams(
            dimension_semantics=("arbitrary",), vmem_limit_bytes=(20 << 20) + length * 4096
        )
        self.rows_spec = pl.BlockSpec((tokens, hidden), lambda i, b: (i, 0))
        self.kv_spec = pl.BlockSpec((length, head), lambda i, b: (0, 0))
        self.vec_spec = pl.BlockSpec((1, 1, tokens), lambda i, b: (i, 0, 0))
        self.lse_spec = pl.BlockSpec((1, 1, tokens * self.heads), lambda i, b: (i, 0, 0))
        self.cells = tokens * chunks * self.heads * length

    def forward(self, bounds, q, k, v, low, pos):
        body = functools.partial(attend_forward, heads=self.heads, span=self.span, scale=self.scale)
        return pl.pallas_call(
            body,
            grid_spec=pltpu.PrefetchScalarGridSpec(
                num_scalar_prefetch=1,
                grid=(self.chunks,),
                in_specs=[self.rows_spec, self.kv_spec, self.kv_spec, self.vec_spec, self.vec_spec],
                out_specs=[self.rows_spec, self.lse_spec],
            ),
            out_shape=[
                jax.ShapeDtypeStruct(q.shape, bf16),
                jax.ShapeDtypeStruct((self.chunks, 1, self.t * self.heads), f32),
            ],
            compiler_params=self.params,
            cost_estimate=pl.CostEstimate(
                flops=4 * self.cells * self.head, bytes_accessed=4 << 20, transcendentals=self.cells
            ),
        )(bounds, q, k, v, low, pos)

    def backward(self, bounds, q, o, g, lse, k, v, low, pos):
        body = functools.partial(
            attend_backward, heads=self.heads, span=self.span, scale=self.scale, plain=self.plain
        )
        return pl.pallas_call(
            body,
            grid_spec=pltpu.PrefetchScalarGridSpec(
                num_scalar_prefetch=1,
                grid=(self.chunks,),
                in_specs=[self.rows_spec] * 3
                + [self.lse_spec, self.kv_spec, self.kv_spec, self.vec_spec, self.vec_spec],
                out_specs=[
                    self.rows_spec,
                    pl.BlockSpec((self.length, 2 * self.head), lambda i, b: (0, 0)),
                ],
            ),
            out_shape=[
                jax.ShapeDtypeStruct(q.shape, bf16),
                jax.ShapeDtypeStruct((self.length, 2 * self.head), f32),
            ],
            compiler_params=self.params,
            cost_estimate=pl.CostEstimate(
                flops=10 * self.cells * self.head, bytes_accessed=8 << 20, transcendentals=self.cells
            ),
        )(bounds, q, o, g, lse, k, v, low, pos)


def norm_parts(v):
    mean = jnp.mean(v, axis=1, keepdims=True)
    spread = jnp.mean(v * v, axis=1, keepdims=True) - mean * mean
    inv_std = lax.rsqrt(spread + epsilon)
    return (v - mean) * inv_std, inv_std


def norm_back(e, centred, inv_std, gain):
    c = e * gain
    m1 = jnp.mean(c, axis=1, keepdims=True)
    m2 = jnp.mean(c * centred, axis=1, keepdims=True)
    return (c - m1 - centred * m2) * inv_std


gelu_a = math.sqrt(2.0 / math.pi)
gelu_b = 0.044715


def per_device(
    tokens,
    segment_ids,
    ln1_gain,
    ln1_bias,
    w_query,
    b_query,
    w_keyval,
    b_value,
    w_out,
    b_out,
    ln2_gain,
    ln2_bias,
    w_up,
    b_up,
    w_down,
    b_down,
    d_output,
):
    at = Place()
    rows = at.rows
    col_tokens, row_width = tokens.shape
    t = col_tokens // rows
    width = row_width * rows
    head = b_value.shape[0]
    hidden = w_query.shape[1]
    length = segment_ids.shape[1]
    row, col = at.ry * 2 + at.rx, at.ch * 2 + at.cl
    every = ("ry", "rx", "dp")
    rows_of = lambda a, n: lambda r: lax.dynamic_slice_in_dim(a, r * n, n, 0)
    lanes_of = lambda a, n: lambda r: lax.dynamic_slice_in_dim(a, r * n, n, 1)

    gather = lambda w, axis: lax.all_gather(half_of(w, axis), every, axis=axis, tiled=True)
    qkv_weight = gather(jnp.concatenate([w_query, w_keyval], axis=1), 0)
    out_weight = gather(w_out, 1)
    down_weight = gather(w_down, 1)
    up_weight = gather(w_up, 0)

    vectors = jnp.pad(jnp.stack([ln1_gain, ln1_bias, ln2_gain, ln2_bias, b_out, b_down]), ((0, 10), (0, 0)))
    got = at.exchange(rows_of(tokens, t), rows_of(d_output, t), lambda r: vectors)
    got = at.by_lanes(got, 0, got[0].shape[0])
    own, own_grad = got[:t].astype(f32), got[t : 2 * t]
    gain_one, bias_one, gain_two, bias_two, out_bias, down_bias = got[2 * t : 2 * t + 6].astype(f32)[:, None, :]

    segments = segment_ids[0]
    base = jnp.stack([(col ^ k) * col_tokens + row * t for k in range(4)]).astype(jnp.int32)
    pos = base[:, None] + jnp.arange(t, dtype=jnp.int32)[None, :]
    seg_rows = jnp.stack([lax.dynamic_slice_in_dim(segments, base[k], t, 0) for k in range(4)])
    low = jnp.sum((segments[None, None, :] < seg_rows[:, :, None]).astype(jnp.int32), axis=2)
    attention = Attention(t, 4, hidden, length, head)
    span = attention.span
    bounds = jnp.stack([low[:, 0] // span, (base + t - 1) // span + 1], axis=1)
    low, pos = low[:, None, :], pos[:, None, :]

    centred_one, inv_one = norm_parts(own)
    normed_one = (centred_one * gain_one + bias_one).astype(bf16)
    block_one = line_second(normed_one, *line_first(normed_one))
    block_one, own_grad = tie(block_one, own_grad)
    kv_bias = jnp.pad(b_value.astype(f32), (head, 0))
    kv = (dot_nn(block_one, qkv_weight[:, hidden:]) + kv_bias).astype(bf16)
    got = at.exchange(lambda r: kv)
    queries = (dot_nn(block_one, qkv_weight[:, :hidden]) + b_query.astype(f32)).astype(bf16)
    grad_first = line_first(own_grad)
    kv = at.by_tokens(got, col, t)
    keys, values = kv[:, :head], kv[:, head:]
    attended, lse = attention.forward(bounds, queries, keys, values, low, pos)

    part = dot_nn(attended, out_weight).astype(bf16)
    part, grad_first = tie(part, grad_first)
    block_grad = line_second(own_grad, *grad_first)
    end, near, mid = line_scatter_first(part)
    far = line_scatter_second(part, end)
    near, mid, far, block_grad = tie(near, mid, far, block_grad)
    hidden_one = own + out_bias + line_total(part, near, mid, far)
    centred_two, inv_two = norm_parts(hidden_one)
    normed_two = (centred_two * gain_two + bias_two).astype(bf16)
    far, near, mid = line_first(normed_two)
    near, mid, block_grad = tie(near, mid, block_grad)
    grad_act = multiply(block_grad, down_weight, "nt")
    far, grad_act = tie(far, grad_act)
    block_two = line_second(normed_two, far, near, mid)

    activated, grad_upper = feed_forward(block_two, up_weight, b_up.astype(f32)[None, :], grad_act)
    part = multiply(grad_upper, up_weight, "nt")
    part, activated, grad_upper = tie(part, activated, grad_upper)
    end, near, mid = line_scatter_first(part)
    end, mid, activated, grad_upper = tie(end, mid, activated, grad_upper)
    far = line_scatter_second(part, end)
    down_part = multiply(activated, block_grad, "tn", 1)
    up_part = multiply(block_two, grad_upper, "tn", 1)
    near, mid, far, down_part, up_part, activated = tie(near, mid, far, down_part, up_part, activated)
    down_part = scatter_row(down_part, 1)
    up_part = scatter_row(up_part, 0)
    grad_two = line_total(part, near, mid, far)
    grad_hidden = own_grad.astype(f32) + norm_back(grad_two, centred_two, inv_two, gain_two)
    grad_branch = grad_hidden.astype(bf16)
    far, near, mid = line_first(grad_branch)
    near, mid, activated = tie(near, mid, activated)
    final_part = multiply(activated, down_weight, "nn", 1)
    far, final_part = tie(far, final_part)
    block_branch = line_second(grad_branch, far, near, mid)
    grad_att = dot_nt(block_branch, out_weight).astype(bf16)
    grad_att, final_part = tie(grad_att, final_part)
    final_end, final_near, final_mid = line_scatter_first(final_part)
    grad_query, grad_kv = attention.backward(
        bounds, queries, attended, grad_att, lse, keys, values, low, pos
    )

    grad_kv = grad_kv.astype(bf16)
    grad_query, grad_kv, final_end, block_branch, attended = tie(
        grad_query, grad_kv, final_end, block_branch, attended
    )
    part = dot_nt(grad_query, qkv_weight[:, :hidden]).astype(bf16)
    end, near, mid = line_scatter_first(part)
    final_far = line_scatter_second(final_part, final_end)
    kv_grad = at.sum_rows(lambda r: at.line_tokens(grad_kv, col, r, t)).astype(bf16)
    kv_grad, end, grad_query, block_one, down_part, final_far, final_near, final_mid = tie(
        kv_grad, end, grad_query, block_one, down_part, final_far, final_near, final_mid
    )
    far = line_scatter_second(part, end)
    parts = [dot_tn(block_one, grad_query).astype(bf16), dot_tn(block_branch, attended).astype(bf16)]
    shift = lambda a, k: jnp.concatenate([a[(j ^ k) * t : ((j ^ k) + 1) * t] for j in range(4)], axis=0)
    kv_whole = add(kv_grad, shift(swap(kv_grad, "cl"), 1))
    kv_whole = add(kv_whole, shift(swap(kv_whole, "ch"), 2))
    near, mid, far, kv_whole, up_part = tie(near, mid, far, kv_whole, up_part)
    qo_part = scatter_row(jnp.concatenate(parts, axis=1), 0)
    kv_part = dot_tn(kv_whole, block_one).astype(bf16)
    kv_far = swap(lax.dynamic_slice_in_dim(kv_part, (1 - at.dp) * head, head, 0), "dp")
    kv_part = add(half_of(kv_part, 0), kv_far)
    grad_one = line_total(part, near, mid, far) + dot_nt(kv_whole[:t], qkv_weight[:, hidden:])
    grad_own = grad_hidden + norm_back(grad_one, centred_one, inv_one, gain_one)
    final = hidden_one + down_bias + line_total(final_part, final_near, final_mid, final_far)

    sums = lambda a: jnp.sum(a.astype(f32), axis=0)
    tiled = lambda a: jnp.tile(a.reshape(-1, row_width), (1, rows))
    place = lambda a: lax.dynamic_update_slice_in_dim(jnp.zeros((4 * a.shape[0],), f32), a, col * a.shape[0], 0)
    vectors = jnp.stack(
        [
            sums(grad_one * centred_one),
            sums(grad_one),
            sums(grad_two * centred_two),
            sums(grad_two),
            sums(grad_branch),
            sums(own_grad),
        ]
    )
    parts = [
        vectors,
        tiled(jnp.pad(sums(kv_whole[:t, head:]), (0, row_width - head))),
        tiled(place(sums(grad_query))),
        tiled(place(sums(grad_upper))),
    ]
    n = sum(p.shape[0] for p in parts)
    parts.append(jnp.zeros((-n % 16, width), f32))
    packed = jnp.concatenate(parts).astype(bf16)
    n = packed.shape[0]
    got = at.exchange(
        lanes_of(packed, row_width),
        lanes_of(grad_own.astype(bf16), row_width),
        lanes_of(final.astype(bf16), row_width),
        lanes_of(kv_part, row_width),
    )
    total = sum(g[:n].astype(f32) for g in got)
    grad_tokens = at.by_rows(got, n, n + t).astype(f32)
    output = at.by_rows(got, n + t, n + 2 * t)
    kv_part = sum(g[n + 2 * t :].astype(f32) for g in got).astype(bf16)
    grad_w_keyval = gather_axis(kv_part, "dp").reshape(2 * head, row_width).T.astype(f32)
    for axis in ("cl", "ch"):
        total = total.astype(bf16)
        total = total.astype(f32) + swap(total, axis).astype(f32)
    total = total.astype(bf16)
    total = total.astype(f32) + swap(total, "dp").astype(f32)
    grad_w_up = at.both_cores(up_part, 0)
    grad_w_down = at.both_cores(down_part, 1)
    qo_part = at.both_cores(qo_part, 0)
    grad_w_query, grad_w_out = qo_part[:, :hidden], qo_part[:, hidden:].T
    grad_ln1_gain, grad_ln1_bias, grad_ln2_gain, grad_ln2_bias, grad_b_out, grad_b_down = total[:6]
    grad_b_value = total[6, :head]
    of_col = lambda first, n: lax.dynamic_slice_in_dim(
        total[first : first + 4 * n // row_width].reshape(-1), col * n, n, 0
    )
    grad_b_query = of_col(7, hidden)
    grad_b_up = of_col(7 + 4 * hidden // row_width, b_up.shape[0])
    return (
        output,
        grad_tokens,
        grad_ln1_gain,
        grad_ln1_bias,
        grad_w_query,
        grad_b_query,
        grad_w_keyval,
        grad_b_value,
        grad_w_out,
        grad_b_out,
        grad_ln2_gain,
        grad_ln2_bias,
        grad_w_up,
        grad_b_up,
        grad_w_down,
        grad_b_down,
    )


def solution(mesh):
    dp, rows, cols = (mesh.shape[name] for name in ("dp", "row", "col"))
    fine = Mesh(
        mesh.devices.reshape(dp, rows // 2, 2, cols // 2, 2), ("dp", "ry", "rx", "ch", "cl")
    )
    row, col = ("ry", "rx"), ("ch", "cl")
    tok = P(("dp", "ch", "cl"), row)
    in_specs = (
        tok,
        P("dp", None),
        P(row),
        P(row),
        P(row, col),
        P(col),
        P(row, None),
        P(),
        P(col, row),
        P(row),
        P(row),
        P(row),
        P(row, col),
        P(col),
        P(col, row),
        P(row),
        tok,
    )
    out_specs = (
        tok,
        tok,
        P(row),
        P(row),
        P(row, col),
        P(col),
        P(row, None),
        P(),
        P(col, row),
        P(row),
        P(row),
        P(row),
        P(row, col),
        P(col),
        P(col, row),
        P(row),
    )
    return jax.shard_map(
        per_device, mesh=fine, in_specs=in_specs, out_specs=out_specs, check_vma=False
    )
```

time: 639 us -> 498 us (0.78)
  waiting for transfers between devices: 307 us -> 234 us
  matrix products: 71.6 us -> 22.7 us
  starting transfers between devices: 123 us -> 79.2 us
  Pallas kernels: 12.8 us -> 51.1 us
  other arithmetic: 59.2 us -> 42.2 us
    ppermute x56 -> x27, waiting for transfers between devices: 176 us -> 105 us  [swap(): return lax.ppermute(a, axis, [(0, 1), (1, 0)])]
    pallas_call x0 -> x6, Pallas kernels: none -> 36.8 us  [the longest x5 27 us: multiply(): pl.pallas_call(body, grid=(steps,), in_specs=specs, out_specs=out_spec, o...]
    unnamed x135 -> x190, local copies, waits for them, and re-layouts: 9.28 us -> 32.6 us
    ppermute x56 -> x27, starting transfers between devices: 61.5 us -> 42.7 us  [swap(): return lax.ppermute(a, axis, [(0, 1), (1, 0)])]
    dot_general x5 -> x3, matrix products: 24.5 us -> 7.95 us  [dot_nn(): lax.dot_general(a, b, (((1,), (0,)), ((), ())), preferred_element_type=f32)]
    dot_general x5 -> x3, matrix products: 24.6 us -> 8.36 us  [dot_nt(): lax.dot_general(a, b, (((1,), (1,)), ((), ())), preferred_element_type=f32)]
    dot_general x5 -> x3, matrix products: 22.5 us -> 6.37 us  [dot_tn(): lax.dot_general(a, b, (((0,), (0,)), ((), ())), preferred_element_type=f32)]
    all_to_all x4 -> x0, starting transfers between devices: 15.9 us -> none  [the longest x1 4.14 us: per_device(): lax.all_to_all(grad_own.astype(bf16), row_axes, 1, 0, tiled=True)]
  transfers between devices with their start and end apart: 88 -> 60, of which waited for: 41 -> 29; matrix products, arithmetic and copies ran while one was open for 23% -> 16% of each run, Pallas kernels for 2% -> 7%
where the time goes in v2:
time: 498 us; the launch traced here: 496 us
  waiting for transfers between devices  234 us (47%)
  starting transfers between devices  79.2 us (16%)
  Pallas kernels  51.1 us (10%)
  local copies, waits for them, and re-layouts  51 us (10%)
  other arithmetic  42.2 us (8%)
  matrix products  22.7 us (5%)
  between operations  16.5 us (3%)
    ppermute x27, waiting for transfers between devices, swap(): return lax.ppermute(a, axis, [(0, 1), (1, 0)])  105 us
    ppermute x10, waiting for transfers between devices, row_send(): return lax.ppermute(a, ('ry', 'rx'), pairs)  51.2 us
    ppermute x4, waiting for transfers between devices, line_second(): end = lax.ppermute(far, ('ch', 'cl'), [(1, 0), (2, 3)])  43.8 us
    ppermute x27, starting transfers between devices, swap(): return lax.ppermute(a, axis, [(0, 1), (1, 0)])  42.7 us
    unnamed x190, local copies, waits for them, and re-layouts  32.6 us
    ppermute x4, waiting for transfers between devices, line_scatter_first(): end = lax.ppermute(p[3 * t:], ('ch', 'cl'), [(0, 1), (3, 2)])  28.8 us
    pallas_call x5, Pallas kernels, multiply(): pl.pallas_call(body, grid=(steps,), in_specs=specs, out_specs=out_spec, o...  27 us
    ppermute x10, starting transfers between devices, row_send(): return lax.ppermute(a, ('ry', 'rx'), pairs)  13.2 us
  transfers between devices with their start and end apart: 60, of which 29 were waited for; matrix products, arithmetic and copies ran while one was open for 16% of the time, Pallas kernels for 7%

profile of v2, /device:TPU:0, one launch (start us, length us, event | category | flops | bytes accessed | tf_op | source)
XLA Modules:
  0.0 496.2 jit_solution(10474432825801028790)
XLA Ops:
  15.1 3.0 collective-permute-start
  19.8 9.2 %collective-permute-done = bf16[272,512]{1,0:T(8,128)(2,1)S(1)} collective-permute-done((bf16[272,512]{1,0:T(8,128)(2,1)S(1)}, bf16[272,512]{1,0:T(8,128)(2,1)S(1)}, u32[]{:S(2)}, u32[]{:S(2)}) %collective-permute-start) | collective-permute-done | bytes 278560 | tf_op jit(solution)/shard_map/ppermute | solution.py:91
  29.1 6.4 %collective-permute-done.1 = bf16[272,512]{1,0:T(8,128)(2,1)S(1)} collective-permute-done((bf16[272,512]{1,0:T(8,128)(2,1)S(1)}, bf16[272,512]{1,0:T(8,128)(2,1)S(1)}, u32[]{:S(2)}, u32[]{:S(2)}) %collective-permute-start.1) | collective-permute-done | bytes 278560 | tf_op jit(solution)/shard_map/ppermute | solution.py:91
  44.8 18.9 %collective-permute-done.4 = bf16[128,2048]{1,0:T(8,128)(2,1)} collective-permute-done((bf16[128,2048]{1,0:T(8,128)(2,1)S(1)}, bf16[128,2048]{1,0:T(8,128)(2,1)}, u32[]{:S(2)}, u32[]{:S(2)}) %collective-permute-start.4) | collective-permute-done | bytes 524320 | tf_op jit(solution)/shard_map/ppermute | solution.py:32
  66.0 11.4 %collective-permute-done.6 = bf16[128,2048]{1,0:T(8,128)(2,1)S(1)} collective-permute-done((bf16[128,2048]{1,0:T(8,128)(2,1)}, bf16[128,2048]{1,0:T(8,128)(2,1)S(1)}, u32[]{:S(2)}, u32[]{:S(2)}) %collective-permute-start.6) | collective-permute-done | bytes 524320 | tf_op jit(solution)/shard_map/ppermute | solution.py:59
  80.2 3.8 collective-permute-start.11
  92.6 3.8 collective-permute-done.9
  101.3 5.9 %shard_map.288 = (bf16[512,512]{1,0:T(8,128)(2,1)S(1)}, f32[4,1,512]{2,1,0:T(1,128)S(1)}) custom-call(s32[4,2]{1,0:T(4,128)S(1)} %pad_add_fusion.1.bounds, bf16[512,512]{1,0:T(8,128)(2,1)S(1)} %fusion.6.q_ref, bf16[2048,128]{1,0:T(8,128)(2,1)S(1)} %get-tuple-element.242.k_ref, bf16[2048,128]{1,0:T(8,128)(2,1)S(1)} %get-tuple-element.241.v_ref, ...), custom_call_target="tpu_custom_call" | custom-call | flops 2147483648 | bytes 4194304 | tf_op jit(solution)/shard_map/pallas_call | solution.py:333
  107.3 3.0 convolution_convert_fusion.3
  110.4 7.3 %collective-permute-done.10 = bf16[128,2048]{1,0:T(8,128)(2,1)S(1)} collective-permute-done((bf16[128,2048]{1,0:T(8,128)(2,1)}, bf16[128,2048]{1,0:T(8,128)(2,1)S(1)}, u32[]{:S(2)}, u32[]{:S(2)}) %collective-permute-start.10) | collective-permute-done | bytes 524320 | tf_op jit(solution)/shard_map/ppermute | solution.py:32
  124.0 7.6 %collective-permute-done.15 = bf16[128,2048]{1,0:T(8,128)(2,1)S(1)} collective-permute-done((bf16[128,2048]{1,0:T(8,128)(2,1)S(1)}, bf16[128,2048]{1,0:T(8,128)(2,1)S(1)}, u32[]{:S(2)}, u32[]{:S(2)}) %collective-permute-start.15) | collective-permute-done | bytes 524320 | tf_op jit(solution)/shard_map/ppermute | solution.py:65
  131.7 3.2 collective-permute-start.16
  134.9 12.7 %collective-permute-done.17 = bf16[128,2048]{1,0:T(8,128)(2,1)S(1)} collective-permute-done((bf16[128,2048]{1,0:T(8,128)(2,1)S(1)}, bf16[128,2048]{1,0:T(8,128)(2,1)S(1)}, u32[]{:S(2)}, u32[]{:S(2)}) %collective-permute-start.17) | collective-permute-done | bytes 524320 | tf_op jit(solution)/shard_map/ppermute | solution.py:59
  150.4 6.6 %collective-permute-done.13 = bf16[128,2048]{1,0:T(8,128)(2,1)S(1)} collective-permute-done((bf16[128,2048]{1,0:T(8,128)(2,1)S(1)}, bf16[128,2048]{1,0:T(8,128)(2,1)S(1)}, u32[]{:S(2)}, u32[]{:S(2)}) %collective-permute-start.13) | collective-permute-done | bytes 524320 | tf_op jit(solution)/shard_map/ppermute | solution.py:32
  163.9 10.9 %collective-permute-done.18 = bf16[128,2048]{1,0:T(8,128)(2,1)} collective-permute-done((bf16[128,2048]{1,0:T(8,128)(2,1)S(1)}, bf16[128,2048]{1,0:T(8,128)(2,1)}, u32[]{:S(2)}, u32[]{:S(2)}) %collective-permute-start.18) | collective-permute-done | bytes 524320 | tf_op jit(solution)/shard_map/ppermute | solution.py:32
  174.8 3.4 copy-done.4
  178.1 5.3 %shard_map.289.g_ref = bf16[512,2048]{1,0:T(8,128)(2,1)S(1)} custom-call(bf16[512,2048]{1,0:T(8,128)(2,1)S(1)} %pad_maximum_fusion.2.x_ref.w_ref, bf16[2048,2048]{1,0:T(8,128)(2,1)S(1)} %copy-done.4), custom_call_target="tpu_custom_call" | custom-call | flops 4294967296 | bytes 12582912 | tf_op jit(solution)/shard_map/pallas_call | solution.py:188
  184.7 10.1 %collective-permute-done.20 = bf16[128,2048]{1,0:T(8,128)(2,1)} collective-permute-done((bf16[128,2048]{1,0:T(8,128)(2,1)S(1)}, bf16[128,2048]{1,0:T(8,128)(2,1)}, u32[]{:S(2)}, u32[]{:S(2)}) %collective-permute-start.20) | collective-permute-done | bytes 524320 | tf_op jit(solution)/shard_map/ppermute | solution.py:32
  196.3 11.1 %collective-permute-done.21 = bf16[128,2048]{1,0:T(8,128)(2,1)S(1)} collective-permute-done((bf16[128,2048]{1,0:T(8,128)(2,1)}, bf16[128,2048]{1,0:T(8,128)(2,1)S(1)}, u32[]{:S(2)}, u32[]{:S(2)}) %collective-permute-start.21) | collective-permute-done | bytes 524320 | tf_op jit(solution)/shard_map/ppermute | solution.py:59
  207.6 3.1 pad_maximum_fusion.3.x_ref
  212.3 3.4 copy-done.18
  215.6 9.7 %shard_map.290 = (bf16[512,2048]{1,0:T(8,128)(2,1)S(1)}, bf16[512,2048]{1,0:T(8,128)(2,1)S(1)}) custom-call(bf16[512,2048]{1,0:T(8,128)(2,1)S(1)} %copy-done.11, bf16[2048,2048]{1,0:T(8,128)(2,1)S(1)} %copy-done.18, f32[1,2048]{1,0:T(1,128)S(1)} %bitcast.62, bf16[512,2048]{1,0:T(8,128)(2,1)S(1)} %copy-done.20), custom_call_target="tpu_custom_call" | custom-call | flops 4294967296 | bytes 16777216 | tf_op jit(solution)/shard_map/pallas_call | solution.py:219
  225.4 5.3 %shard_map.291 = bf16[512,2048]{1,0:T(8,128)(2,1)S(1)} custom-call(bf16[512,2048]{1,0:T(8,128)(2,1)S(1)} %get-tuple-element.99.x_ref.w_ref, bf16[2048,2048]{1,0:T(8,128)(2,1)S(1)} %copy-done.18), custom_call_target="tpu_custom_call" | custom-call | flops 4294967296 | bytes 12582912 | tf_op jit(solution)/shard_map/pallas_call | solution.py:188
  232.4 3.4 collective-permute-start.23
  236.0 12.2 %collective-permute-done.23 = bf16[128,2048]{1,0:T(8,128)(2,1)S(1)} collective-permute-done((bf16[128,2048]{1,0:T(8,128)(2,1)S(1)}, bf16[128,2048]{1,0:T(8,128)(2,1)S(1)}, u32[]{:S(2)}, u32[]{:S(2)}) %collective-permute-start.23) | collective-permute-done | bytes 524320 | tf_op jit(solution)/shard_map/ppermute | solution.py:65
  248.3 3.4 collective-permute-start.25
  251.7 5.3 %shard_map.293 = bf16[2048,2048]{1,0:T(8,128)(2,1)S(1)} custom-call(bf16[512,2048]{1,0:T(8,128)(2,1)S(1)} %copy-done.11, bf16[512,2048]{1,0:T(8,128)(2,1)S(1)} %get-tuple-element.99.x_ref.w_ref), custom_call_target="tpu_custom_call" | custom-call | flops 1 | bytes 1 | tf_op jit(solution)/shard_map/pallas_call | solution.py:188
  257.1 3.3 copy-done.2
  263.6 5.3 %shard_map.292 = bf16[2048,2048]{1,0:T(8,128)(2,1)S(1)} custom-call(bf16[512,2048]{1,0:T(8,128)(2,1)S(1)} %copy-done.13, bf16[512,2048]{1,0:T(8,128)(2,1)S(1)} %copy-done.10), custom_call_target="tpu_custom_call" | custom-call | flops 1 | bytes 1 | tf_op jit(solution)/shard_map/pallas_call | solution.py:188
  269.0 3.3 copy-done.3
  275.9 3.0 fusion.39
  282.7 9.6 %collective-permute-done.26 = bf16[128,2048]{1,0:T(8,128)(2,1)} collective-permute-done((bf16[128,2048]{1,0:T(8,128)(2,1)S(1)}, bf16[128,2048]{1,0:T(8,128)(2,1)}, u32[]{:S(2)}, u32[]{:S(2)}) %collective-permute-start.26) | collective-permute-done | bytes 524320 | tf_op jit(solution)/shard_map/ppermute | solution.py:32
  292.3 3.4 copy-done.5
  295.7 5.8 %shard_map.294 = bf16[512,2048]{1,0:T(8,128)(2,1)S(1)} custom-call(bf16[512,2048]{1,0:T(8,128)(2,1)S(1)} %copy-done.14, bf16[2048,2048]{1,0:T(8,128)(2,1)S(1)} %copy-done.5), custom_call_target="tpu_custom_call" | custom-call | flops 1 | bytes 1 | tf_op jit(solution)/shard_map/pallas_call | solution.py:188
  311.6 8.6 %collective-permute-done.29 = bf16[128,2048]{1,0:T(8,128)(2,1)S(1)} collective-permute-done((bf16[128,2048]{1,0:T(8,128)(2,1)}, bf16[128,2048]{1,0:T(8,128)(2,1)S(1)}, u32[]{:S(2)}, u32[]{:S(2)}) %collective-permute-start.29) | collective-permute-done | bytes 524320 | tf_op jit(solution)/shard_map/ppermute | solution.py:59
  320.4 3.4 convolution_convert_fusion.5.g_ref
  328.0 8.4 %shard_map.295 = (bf16[512,512]{1,0:T(8,128)(2,1)S(1)}, f32[2048,256]{1,0:T(8,128)S(1)}) custom-call(s32[4,2]{1,0:T(4,128)S(1)} %pad_add_fusion.1.bounds, bf16[512,512]{1,0:T(8,128)(2,1)S(1)} %copy-done.24, bf16[512,512]{1,0:T(8,128)(2,1)S(1)} %copy-done.22, bf16[512,512]{1,0:T(8,128)(2,1)S(1)} %convolution_convert_fusion.5.g_ref, ...), custom_call_target="tpu_custom_call" | custom-call | flops 5368709120 | bytes 8388608 | tf_op jit(solution)/shard_map/pallas_call | solution.py:355
  339.1 3.5 collective-permute-start.34
  348.1 3.9 collective-permute-done.31
  363.3 9.0 %collective-permute-done.33 = bf16[128,2048]{1,0:T(8,128)(2,1)} collective-permute-done((bf16[128,2048]{1,0:T(8,128)(2,1)}, bf16[128,2048]{1,0:T(8,128)(2,1)}, u32[]{:S(2)}, u32[]{:S(2)}) %collective-permute-start.33) | collective-permute-done | bytes 524320 | tf_op jit(solution)/shard_map/ppermute | solution.py:65
  386.7 3.3 collective-permute-start.41
  390.7 30.8 %collective-permute-done.41 = bf16[512,256]{1,0:T(8,128)(2,1)S(1)} collective-permute-done((bf16[512,256]{1,0:T(8,128)(2,1)S(1)}, bf16[512,256]{1,0:T(8,128)(2,1)S(1)}, u32[]{:S(2)}, u32[]{:S(2)}) %collective-permute-start.41) | collective-permute-done | bytes 262176 | tf_op jit(solution)/shard_map/ppermute | solution.py:32
  424.3 3.7 fusion.18
  434.0 3.8 collective-permute-start.45
  442.5 18.5 %collective-permute-done.44 = bf16[416,512]{1,0:T(8,128)(2,1)S(1)} collective-permute-done((bf16[416,512]{1,0:T(8,128)(2,1)S(1)}, bf16[416,512]{1,0:T(8,128)(2,1)S(1)}, u32[]{:S(2)}, u32[]{:S(2)}) %collective-permute-start.44) | collective-permute-done | bytes 426016 | tf_op jit(solution)/shard_map/ppermute | solution.py:91
  460.9 5.6 %collective-permute-done.43 = bf16[416,512]{1,0:T(8,128)(2,1)S(1)} collective-permute-done((bf16[416,512]{1,0:T(8,128)(2,1)S(1)}, bf16[416,512]{1,0:T(8,128)(2,1)S(1)}, u32[]{:S(2)}, u32[]{:S(2)}) %collective-permute-start.43) | collective-permute-done | bytes 426016 | tf_op jit(solution)/shard_map/ppermute | solution.py:91
  471.4 4.0 collective-permute-done.47
  480.6 3.7 reduce-scatter.8.cloned.1.call-done
  (418 shorter events, 146.3 us)
Async XLA Ops:
  7.2 76.9 %all-gather.5.cloned.1.call-start = ((), (), s32[]{:S(2)}) async-start(), calls=%async_computation.3 | async-start | bytes 3538944 | tf_op jit(solution)/shard_map/all_gather | solution.py:428
  9.2 98.1 %all-gather.7.cloned.1.call-start = ((), (), s32[]{:S(2)}) async-start(), calls=%async_computation.4 | async-start | bytes 2359296 | tf_op jit(solution)/shard_map/all_gather | solution.py:428
  10.9 163.8 %all-gather.9.cloned.1.call-start = ((), (), s32[]{:S(2)}) async-start(), calls=%async_computation.5 | async-start | bytes 9437184 | tf_op jit(solution)/shard_map/all_gather | solution.py:428
  12.1 198.5 %all-gather.11.cloned.1.call-start = ((), (), s32[]{:S(2)}) async-start(), calls=%async_computation.6 | async-start | bytes 9437184 | tf_op jit(solution)/shard_map/all_gather | solution.py:428
  14.6 357.7 %reduce-scatter.4.cloned.1.call-start = ((), (), s32[]{:S(2)}) async-start(), calls=%async_computation.7 | async-start | bytes 9437184 | tf_op jit(solution)/shard_map/reduce_scatter | solution.py:100
  15.1 13.9 %collective-permute-start = (bf16[272,512]{1,0:T(8,128)(2,1)S(1)}, bf16[272,512]{1,0:T(8,128)(2,1)S(1)}, u32[]{:S(2)}, u32[]{:S(2)}) collective-permute-start(bf16[272,512]{1,0:T(8,128)(2,1)S(1)} %get-tuple-element.294), channel_id=1, source_target_pairs={{0,4},{4,0},{8,12},{12,8},{1,5},{5,1},{9,13},{13,9},{2,6},{6,2},{1... | collective-permute-start | bytes 835592 | tf_op jit(solution)/shard_map/ppermute | solution.py:91
  18.1 17.3 %collective-permute-start.1 = (bf16[272,512]{1,0:T(8,128)(2,1)S(1)}, bf16[272,512]{1,0:T(8,128)(2,1)S(1)}, u32[]{:S(2)}, u32[]{:S(2)}) collective-permute-start(bf16[272,512]{1,0:T(8,128)(2,1)S(1)} %get-tuple-element.295), channel_id=1, source_target_pairs={{0,8},{4,12},{8,0},{12,4},{1,9},{5,13},{9,1},{13,5},{2,10},{6,14},... | collective-permute-start | bytes 835592 | tf_op jit(solution)/shard_map/ppermute | solution.py:91
  19.6 16.6 %collective-permute-start.2 = (bf16[272,512]{1,0:T(8,128)(2,1)S(1)}, bf16[272,512]{1,0:T(8,128)(2,1)S(1)}, u32[]{:S(2)}, u32[]{:S(2)}) collective-permute-start(bf16[272,512]{1,0:T(8,128)(2,1)S(1)} %get-tuple-element.296), channel_id=1, source_target_pairs={{0,12},{4,8},{8,4},{12,0},{1,13},{5,9},{9,5},{13,1},{2,14},{6,10},... | collective-permute-start | bytes 835592 | tf_op jit(solution)/shard_map/ppermute | solution.py:91
  37.4 26.3 %collective-permute-start.4 = (bf16[128,2048]{1,0:T(8,128)(2,1)S(1)}, bf16[128,2048]{1,0:T(8,128)(2,1)}, u32[]{:S(2)}, u32[]{:S(2)}) collective-permute-start(bf16[128,2048]{1,0:T(8,128)(2,1)S(1)} %fusion.17), channel_id=1, source_target_pairs={{0,2},{2,0},{1,3},{3,1},{4,6},{6,4},{5,7},{7,5},{8,10},{10,8},{9,1... | collective-permute-start | bytes 1572872 | tf_op jit(solution)/shard_map/ppermute | solution.py:32
  41.2 24.8 %collective-permute-start.5 = (bf16[128,2048]{1,0:T(8,128)(2,1)S(1)}, bf16[128,2048]{1,0:T(8,128)(2,1)S(1)}, u32[]{:S(2)}, u32[]{:S(2)}) collective-permute-start(bf16[128,2048]{1,0:T(8,128)(2,1)S(1)} %fusion.17), channel_id=1, source_target_pairs={{1,2},{2,1},{5,6},{6,5},{9,10},{10,9},{13,14},{14,13},{17,18},{18,... | collective-permute-start | bytes 1572872 | tf_op jit(solution)/shard_map/ppermute | solution.py:51
  41.9 35.6 %collective-permute-start.3 = (bf16[128,2048]{1,0:T(8,128)(2,1)S(1)}, bf16[128,2048]{1,0:T(8,128)(2,1)S(1)}, u32[]{:S(2)}, u32[]{:S(2)}) collective-permute-start(bf16[128,2048]{1,0:T(8,128)(2,1)S(1)} %fusion.17), channel_id=1, source_target_pairs={{0,1},{1,0},{2,3},{3,2},{4,5},{5,4},{6,7},{7,6},{8,9},{9,8},{10,11... | collective-permute-start | bytes 1572872 | tf_op jit(solution)/shard_map/ppermute | solution.py:32
  63.7 13.7 %collective-permute-start.6 = (bf16[128,2048]{1,0:T(8,128)(2,1)}, bf16[128,2048]{1,0:T(8,128)(2,1)S(1)}, u32[]{:S(2)}, u32[]{:S(2)}) collective-permute-start(bf16[128,2048]{1,0:T(8,128)(2,1)} %collective-permute-done.4), channel_id=1, source_target_pairs={{1,0},{2,3},{5,4},{6,7},{9,8},{10,11},{13,12},{14,15},{17,16},{18,... | collective-permute-start | bytes 1572872 | tf_op jit(solution)/shard_map/ppermute | solution.py:59
  78.8 31.6 %collective-permute-start.12 = (bf16[128,2048]{1,0:T(8,128)(2,1)}, bf16[128,2048]{1,0:T(8,128)(2,1)}, u32[]{:S(2)}, u32[]{:S(2)}) collective-permute-start(bf16[128,2048]{1,0:T(8,128)(2,1)} %pad_maximum_fusion.8), channel_id=1, source_target_pairs={{1,2},{2,1},{5,6},{6,5},{9,10},{10,9},{13,14},{14,13},{17,18},{18,... | collective-permute-start | bytes 1572872 | tf_op jit(solution)/shard_map/ppermute | solution.py:51
  80.2 30.1 %collective-permute-start.11 = (bf16[128,2048]{1,0:T(8,128)(2,1)}, bf16[128,2048]{1,0:T(8,128)(2,1)}, u32[]{:S(2)}, u32[]{:S(2)}) collective-permute-start(bf16[128,2048]{1,0:T(8,128)(2,1)} %pad_maximum_fusion.8), channel_id=1, source_target_pairs={{0,1},{1,0},{2,3},{3,2},{4,5},{5,4},{6,7},{7,6},{8,9},{9,8},{10,11... | collective-permute-start | bytes 1572872 | tf_op jit(solution)/shard_map/ppermute | solution.py:32
  87.7 12.6 %collective-permute-start.8 = (bf16[512,256]{1,0:T(8,128)(2,1)S(1)}, bf16[512,256]{1,0:T(8,128)(2,1)S(1)}, u32[]{:S(2)}, u32[]{:S(2)}) collective-permute-start(bf16[512,256]{1,0:T(8,128)(2,1)S(1)} %fusion.9), channel_id=1, source_target_pairs={{0,8},{4,12},{8,0},{12,4},{1,9},{5,13},{9,1},{13,5},{2,10},{6,14},... | collective-permute-start | bytes 786440 | tf_op jit(solution)/shard_map/ppermute | solution.py:91
  96.4 21.3 %collective-permute-start.10 = (bf16[128,2048]{1,0:T(8,128)(2,1)}, bf16[128,2048]{1,0:T(8,128)(2,1)S(1)}, u32[]{:S(2)}, u32[]{:S(2)}) collective-permute-start(bf16[128,2048]{1,0:T(8,128)(2,1)} %pad_maximum_fusion.8), channel_id=1, source_target_pairs={{0,2},{2,0},{1,3},{3,1},{4,6},{6,4},{5,7},{7,5},{8,10},{10,8},{9,1... | collective-permute-start | bytes 1572872 | tf_op jit(solution)/shard_map/ppermute | solution.py:32
  117.8 13.8 %collective-permute-start.15 = (bf16[128,2048]{1,0:T(8,128)(2,1)S(1)}, bf16[128,2048]{1,0:T(8,128)(2,1)S(1)}, u32[]{:S(2)}, u32[]{:S(2)}) collective-permute-start(bf16[128,2048]{1,0:T(8,128)(2,1)S(1)} %get-tuple-element.211), channel_id=1, source_target_pairs={{0,1},{3,2},{4,5},{7,6},{8,9},{11,10},{12,13},{15,14},{16,17},{19,... | collective-permute-start | bytes 1572872 | tf_op jit(solution)/shard_map/ppermute | solution.py:65
  119.2 37.8 %collective-permute-start.14 = (bf16[128,2048]{1,0:T(8,128)(2,1)S(1)}, bf16[128,2048]{1,0:T(8,128)(2,1)S(1)}, u32[]{:S(2)}, u32[]{:S(2)}) collective-permute-start(bf16[128,2048]{1,0:T(8,128)(2,1)S(1)} %get-tuple-element.211), channel_id=1, source_target_pairs={{1,2},{2,1},{5,6},{6,5},{9,10},{10,9},{13,14},{14,13},{17,18},{18,... | collective-permute-start | bytes 1572872 | tf_op jit(solution)/shard_map/ppermute | solution.py:51
  119.9 27.7 %collective-permute-start.17 = (bf16[128,2048]{1,0:T(8,128)(2,1)S(1)}, bf16[128,2048]{1,0:T(8,128)(2,1)S(1)}, u32[]{:S(2)}, u32[]{:S(2)}) collective-permute-start(bf16[128,2048]{1,0:T(8,128)(2,1)S(1)} %collective-permute-done.10), channel_id=1, source_target_pairs={{1,0},{2,3},{5,4},{6,7},{9,8},{10,11},{13,12},{14,15},{17,16},{18,... | collective-permute-start | bytes 1572872 | tf_op jit(solution)/shard_map/ppermute | solution.py:59
  121.2 35.8 %collective-permute-start.13 = (bf16[128,2048]{1,0:T(8,128)(2,1)S(1)}, bf16[128,2048]{1,0:T(8,128)(2,1)S(1)}, u32[]{:S(2)}, u32[]{:S(2)}) collective-permute-start(bf16[128,2048]{1,0:T(8,128)(2,1)S(1)} %get-tuple-element.212), channel_id=1, source_target_pairs={{0,1},{1,0},{2,3},{3,2},{4,5},{5,4},{6,7},{7,6},{8,9},{9,8},{10,11... | collective-permute-start | bytes 1572872 | tf_op jit(solution)/shard_map/ppermute | solution.py:32
  131.7 25.3 %collective-permute-start.16 = (bf16[128,2048]{1,0:T(8,128)(2,1)S(1)}, bf16[128,2048]{1,0:T(8,128)(2,1)S(1)}, u32[]{:S(2)}, u32[]{:S(2)}) collective-permute-start(bf16[128,2048]{1,0:T(8,128)(2,1)S(1)} %add_convert_fusion.6), channel_id=1, source_target_pairs={{0,2},{2,0},{1,3},{3,1},{4,6},{6,4},{5,7},{7,5},{8,10},{10,8},{9,1... | collective-permute-start | bytes 1572872 | tf_op jit(solution)/shard_map/ppermute | solution.py:32
  160.6 14.2 %collective-permute-start.18 = (bf16[128,2048]{1,0:T(8,128)(2,1)S(1)}, bf16[128,2048]{1,0:T(8,128)(2,1)}, u32[]{:S(2)}, u32[]{:S(2)}) collective-permute-start(bf16[128,2048]{1,0:T(8,128)(2,1)S(1)} %add_convert_fusion.5), channel_id=1, source_target_pairs={{0,1},{1,0},{2,3},{3,2},{4,5},{5,4},{6,7},{7,6},{8,9},{9,8},{10,11... | collective-permute-start | bytes 1572872 | tf_op jit(solution)/shard_map/ppermute | solution.py:32
  162.4 32.5 %collective-permute-start.20 = (bf16[128,2048]{1,0:T(8,128)(2,1)S(1)}, bf16[128,2048]{1,0:T(8,128)(2,1)}, u32[]{:S(2)}, u32[]{:S(2)}) collective-permute-start(bf16[128,2048]{1,0:T(8,128)(2,1)S(1)} %add_convert_fusion.5), channel_id=1, source_target_pairs={{0,2},{2,0},{1,3},{3,1},{4,6},{6,4},{5,7},{7,5},{8,10},{10,8},{9,1... | collective-permute-start | bytes 1572872 | tf_op jit(solution)/shard_map/ppermute | solution.py:32
  194.8 12.6 %collective-permute-start.21 = (bf16[128,2048]{1,0:T(8,128)(2,1)}, bf16[128,2048]{1,0:T(8,128)(2,1)S(1)}, u32[]{:S(2)}, u32[]{:S(2)}) collective-permute-start(bf16[128,2048]{1,0:T(8,128)(2,1)} %collective-permute-done.20), channel_id=1, source_target_pairs={{1,0},{2,3},{5,4},{6,7},{9,8},{10,11},{13,12},{14,15},{17,16},{18,... | collective-permute-start | bytes 1572872 | tf_op jit(solution)/shard_map/ppermute | solution.py:59
  232.4 15.8 %collective-permute-start.23 = (bf16[128,2048]{1,0:T(8,128)(2,1)S(1)}, bf16[128,2048]{1,0:T(8,128)(2,1)S(1)}, u32[]{:S(2)}, u32[]{:S(2)}) collective-permute-start(bf16[128,2048]{1,0:T(8,128)(2,1)S(1)} %get-tuple-element.209), channel_id=1, source_target_pairs={{0,1},{3,2},{4,5},{7,6},{8,9},{11,10},{12,13},{15,14},{16,17},{19,... | collective-permute-start | bytes 1572872 | tf_op jit(solution)/shard_map/ppermute | solution.py:65
  235.9 36.4 %collective-permute-start.22 = (bf16[128,2048]{1,0:T(8,128)(2,1)}, bf16[128,2048]{1,0:T(8,128)(2,1)}, u32[]{:S(2)}, u32[]{:S(2)}) collective-permute-start(bf16[128,2048]{1,0:T(8,128)(2,1)} %get-tuple-element.210), channel_id=1, source_target_pairs={{0,1},{1,0},{2,3},{3,2},{4,5},{5,4},{6,7},{7,6},{8,9},{9,8},{10,11... | collective-permute-start | bytes 1572872 | tf_op jit(solution)/shard_map/ppermute | solution.py:32
  248.3 24.0 %collective-permute-start.25 = (bf16[128,2048]{1,0:T(8,128)(2,1)S(1)}, bf16[128,2048]{1,0:T(8,128)(2,1)}, u32[]{:S(2)}, u32[]{:S(2)}) collective-permute-start(bf16[128,2048]{1,0:T(8,128)(2,1)S(1)} %add_convert_fusion.4), channel_id=1, source_target_pairs={{0,2},{2,0},{1,3},{3,1},{4,6},{6,4},{5,7},{7,5},{8,10},{10,8},{9,1... | collective-permute-start | bytes 1572872 | tf_op jit(solution)/shard_map/ppermute | solution.py:32
  272.4 149.3 %reduce-scatter.6.cloned.1.call-start = ((), (), s32[]{:S(2)}) async-start(), calls=%async_computation.8 | async-start | bytes 9437184 | tf_op jit(solution)/shard_map/reduce_scatter | solution.py:100
  272.9 211.4 %reduce-scatter.8.cloned.1.call-start = ((), (), s32[]{:S(2)}) async-start(), calls=%async_computation.9 | async-start | bytes 4718592 | tf_op jit(solution)/shard_map/reduce_scatter | solution.py:100
  279.6 12.7 %collective-permute-start.26 = (bf16[128,2048]{1,0:T(8,128)(2,1)S(1)}, bf16[128,2048]{1,0:T(8,128)(2,1)}, u32[]{:S(2)}, u32[]{:S(2)}) collective-permute-start(bf16[128,2048]{1,0:T(8,128)(2,1)S(1)} %get-tuple-element.195), channel_id=1, source_target_pairs={{0,1},{1,0},{2,3},{3,2},{4,5},{5,4},{6,7},{7,6},{8,9},{9,8},{10,11... | collective-permute-start | bytes 1572872 | tf_op jit(solution)/shard_map/ppermute | solution.py:32
  281.4 23.9 %collective-permute-start.28 = (bf16[128,2048]{1,0:T(8,128)(2,1)S(1)}, bf16[128,2048]{1,0:T(8,128)(2,1)}, u32[]{:S(2)}, u32[]{:S(2)}) collective-permute-start(bf16[128,2048]{1,0:T(8,128)(2,1)S(1)} %get-tuple-element.195), channel_id=1, source_target_pairs={{0,2},{2,0},{1,3},{3,1},{4,6},{6,4},{5,7},{7,5},{8,10},{10,8},{9,1... | collective-permute-start | bytes 1572872 | tf_op jit(solution)/shard_map/ppermute | solution.py:32
  305.3 14.9 %collective-permute-start.29 = (bf16[128,2048]{1,0:T(8,128)(2,1)}, bf16[128,2048]{1,0:T(8,128)(2,1)S(1)}, u32[]{:S(2)}, u32[]{:S(2)}) collective-permute-start(bf16[128,2048]{1,0:T(8,128)(2,1)} %collective-permute-done.28), channel_id=1, source_target_pairs={{1,0},{2,3},{5,4},{6,7},{9,8},{10,11},{13,12},{14,15},{17,16},{18,... | collective-permute-start | bytes 1572872 | tf_op jit(solution)/shard_map/ppermute | solution.py:59
  323.9 39.4 %collective-permute-start.36 = (bf16[128,2048]{1,0:T(8,128)(2,1)S(1)}, bf16[128,2048]{1,0:T(8,128)(2,1)}, u32[]{:S(2)}, u32[]{:S(2)}) collective-permute-start(bf16[128,2048]{1,0:T(8,128)(2,1)S(1)} %get-tuple-element.206), channel_id=1, source_target_pairs={{1,2},{2,1},{5,6},{6,5},{9,10},{10,9},{13,14},{14,13},{17,18},{18,... | collective-permute-start | bytes 1572872 | tf_op jit(solution)/shard_map/ppermute | solution.py:51
  325.5 13.4 %collective-permute-start.30 = (bf16[128,2048]{1,0:T(8,128)(2,1)S(1)}, bf16[128,2048]{1,0:T(8,128)(2,1)S(1)}, u32[]{:S(2)}, u32[]{:S(2)}) collective-permute-start(bf16[128,2048]{1,0:T(8,128)(2,1)S(1)} %get-tuple-element.206), channel_id=1, source_target_pairs={{0,1},{3,2},{4,5},{7,6},{8,9},{11,10},{12,13},{15,14},{16,17},{19,... | collective-permute-start | bytes 1572872 | tf_op jit(solution)/shard_map/ppermute | solution.py:65
  336.6 24.0 %collective-permute-start.35 = (bf16[128,2048]{1,0:T(8,128)(2,1)S(1)}, bf16[128,2048]{1,0:T(8,128)(2,1)S(1)}, u32[]{:S(2)}, u32[]{:S(2)}) collective-permute-start(bf16[128,2048]{1,0:T(8,128)(2,1)S(1)} %get-tuple-element.205), channel_id=1, source_target_pairs={{0,1},{1,0},{2,3},{3,2},{4,5},{5,4},{6,7},{7,6},{8,9},{9,8},{10,11... | collective-permute-start | bytes 1572872 | tf_op jit(solution)/shard_map/ppermute | solution.py:32
  339.1 24.2 %collective-permute-start.34 = (bf16[128,2048]{1,0:T(8,128)(2,1)S(1)}, bf16[128,2048]{1,0:T(8,128)(2,1)}, u32[]{:S(2)}, u32[]{:S(2)}) collective-permute-start(bf16[128,2048]{1,0:T(8,128)(2,1)S(1)} %add_convert_fusion.3), channel_id=1, source_target_pairs={{0,2},{2,0},{1,3},{3,1},{4,6},{6,4},{5,7},{7,5},{8,10},{10,8},{9,1... | collective-permute-start | bytes 1572872 | tf_op jit(solution)/shard_map/ppermute | solution.py:32
  345.6 26.8 %collective-permute-start.33 = (bf16[128,2048]{1,0:T(8,128)(2,1)}, bf16[128,2048]{1,0:T(8,128)(2,1)}, u32[]{:S(2)}, u32[]{:S(2)}) collective-permute-start(bf16[128,2048]{1,0:T(8,128)(2,1)} %get-tuple-element.207), channel_id=1, source_target_pairs={{0,1},{3,2},{4,5},{7,6},{8,9},{11,10},{12,13},{15,14},{16,17},{19,... | collective-permute-start | bytes 1572872 | tf_op jit(solution)/shard_map/ppermute | solution.py:65
  359.0 62.6 %collective-permute-start.38 = (bf16[128,2048]{1,0:T(8,128)(2,1)}, bf16[128,2048]{1,0:T(8,128)(2,1)}, u32[]{:S(2)}, u32[]{:S(2)}) collective-permute-start(bf16[128,2048]{1,0:T(8,128)(2,1)} %get-tuple-element.207), channel_id=1, source_target_pairs={{1,2},{2,1},{5,6},{6,5},{9,10},{10,9},{13,14},{14,13},{17,18},{18,... | collective-permute-start | bytes 1572872 | tf_op jit(solution)/shard_map/ppermute | solution.py:51
  360.6 61.1 %collective-permute-start.37 = (bf16[128,2048]{1,0:T(8,128)(2,1)}, bf16[128,2048]{1,0:T(8,128)(2,1)}, u32[]{:S(2)}, u32[]{:S(2)}) collective-permute-start(bf16[128,2048]{1,0:T(8,128)(2,1)} %get-tuple-element.208), channel_id=1, source_target_pairs={{0,1},{1,0},{2,3},{3,2},{4,5},{5,4},{6,7},{7,6},{8,9},{9,8},{10,11... | collective-permute-start | bytes 1572872 | tf_op jit(solution)/shard_map/ppermute | solution.py:32
  372.8 12.8 %collective-permute-start.40 = (bf16[512,256]{1,0:T(8,128)(2,1)S(1)}, bf16[512,256]{1,0:T(8,128)(2,1)}, u32[]{:S(2)}, u32[]{:S(2)}) collective-permute-start(bf16[512,256]{1,0:T(8,128)(2,1)S(1)} %add_convert_fusion.9), channel_id=1, source_target_pairs={{0,1},{1,0},{2,3},{3,2},{4,5},{5,4},{6,7},{7,6},{8,9},{9,8},{10,11... | collective-permute-start | bytes 786440 | tf_op jit(solution)/shard_map/ppermute | solution.py:32
  375.3 63.2 %collective-permute-start.52 = (bf16[2048,256]{1,0:T(8,128)(2,1)}, bf16[2048,256]{1,0:T(8,128)(2,1)}, u32[]{:S(2)}, u32[]{:S(2)}) collective-permute-start(bf16[2048,256]{1,0:T(8,128)(2,1)} %reduce-scatter.4.cloned.1.call-done), channel_id=1, source_target_pairs={{0,16},{16,0},{1,17},{17,1},{2,18},{18,2},{3,19},{19,3},{4,20},{20... | collective-permute-start | bytes 3145736 | tf_op jit(solution)/shard_map/ppermute | solution.py:32
  383.6 38.1 %collective-permute-start.39 = (bf16[128,2048]{1,0:T(8,128)(2,1)S(1)}, bf16[128,2048]{1,0:T(8,128)(2,1)}, u32[]{:S(2)}, u32[]{:S(2)}) collective-permute-start(bf16[128,2048]{1,0:T(8,128)(2,1)S(1)} %add_convert_fusion.1), channel_id=1, source_target_pairs={{0,2},{2,0},{1,3},{3,1},{4,6},{6,4},{5,7},{7,5},{8,10},{10,8},{9,1... | collective-permute-start | bytes 1572872 | tf_op jit(solution)/shard_map/ppermute | solution.py:32
  386.7 34.8 %collective-permute-start.41 = (bf16[512,256]{1,0:T(8,128)(2,1)S(1)}, bf16[512,256]{1,0:T(8,128)(2,1)S(1)}, u32[]{:S(2)}, u32[]{:S(2)}) collective-permute-start(bf16[512,256]{1,0:T(8,128)(2,1)S(1)} %add_convert_fusion.8), channel_id=1, source_target_pairs={{0,2},{2,0},{1,3},{3,1},{4,6},{6,4},{5,7},{7,5},{8,10},{10,8},{9,1... | collective-permute-start | bytes 786440 | tf_op jit(solution)/shard_map/ppermute | solution.py:32
  431.6 43.9 %collective-permute-start.51 = (bf16[256,2048]{1,0:T(8,128)(2,1)S(1)}, bf16[256,2048]{1,0:T(8,128)(2,1)S(1)}, u32[]{:S(2)}, u32[]{:S(2)}) collective-permute-start(bf16[256,2048]{1,0:T(8,128)(2,1)S(1)} %copy-done.44), channel_id=1, source_target_pairs={{0,16},{16,0},{1,17},{17,1},{2,18},{18,2},{3,19},{19,3},{4,20},{20... | collective-permute-start | bytes 3145736 | tf_op jit(solution)/shard_map/ppermute | solution.py:32
  433.6 27.3 %collective-permute-start.44 = (bf16[416,512]{1,0:T(8,128)(2,1)S(1)}, bf16[416,512]{1,0:T(8,128)(2,1)S(1)}, u32[]{:S(2)}, u32[]{:S(2)}) collective-permute-start(bf16[416,512]{1,0:T(8,128)(2,1)S(1)} %pad_maximum_fusion.16), channel_id=1, source_target_pairs={{0,8},{4,12},{8,0},{12,4},{1,9},{5,13},{9,1},{13,5},{2,10},{6,14},... | collective-permute-start | bytes 1277960 | tf_op jit(solution)/shard_map/ppermute | solution.py:91
  434.0 26.9 %collective-permute-start.45 = (bf16[416,512]{1,0:T(8,128)(2,1)S(1)}, bf16[416,512]{1,0:T(8,128)(2,1)S(1)}, u32[]{:S(2)}, u32[]{:S(2)}) collective-permute-start(bf16[416,512]{1,0:T(8,128)(2,1)S(1)} %pad_maximum_fusion.17), channel_id=1, source_target_pairs={{0,12},{4,8},{8,4},{12,0},{1,13},{5,9},{9,5},{13,1},{2,14},{6,10},... | collective-permute-start | bytes 1277960 | tf_op jit(solution)/shard_map/ppermute | solution.py:91
  437.8 28.7 %collective-permute-start.43 = (bf16[416,512]{1,0:T(8,128)(2,1)S(1)}, bf16[416,512]{1,0:T(8,128)(2,1)S(1)}, u32[]{:S(2)}, u32[]{:S(2)}) collective-permute-start(bf16[416,512]{1,0:T(8,128)(2,1)S(1)} %pad_maximum_fusion.15), channel_id=1, source_target_pairs={{0,4},{4,0},{8,12},{12,8},{1,5},{5,1},{9,13},{13,9},{2,6},{6,2},{1... | collective-permute-start | bytes 1277960 | tf_op jit(solution)/shard_map/ppermute | solution.py:91
  466.7 17.7 %collective-permute-start.50 = (bf16[128,512]{1,0:T(8,128)(2,1)S(1)}, bf16[128,512]{1,0:T(8,128)(2,1)S(1)}, u32[]{:S(2)}, u32[]{:S(2)}) collective-permute-start(bf16[128,512]{1,0:T(8,128)(2,1)S(1)} %add_convert_fusion.10), channel_id=1, source_target_pairs={{0,16},{16,0},{1,17},{17,1},{2,18},{18,2},{3,19},{19,3},{4,20},{20... | collective-permute-start | bytes 393224 | tf_op jit(solution)/shard_map/ppermute | solution.py:32
  (91 other events, 795.5 us)
Sparse Core Ops, SparseCore 0:
  10.5 43.9 all-gather.4
  56.9 28.1 all-gather.6
  87.6 55.9 all-gather.8
  145.9 54.3 all-gather.10
  272.5 71.2 reduce-scatter.3
  347.4 72.7 reduce-scatter.5
  423.6 60.7 reduce-scatter.7

commit v3 on v2

--- a/solution.py
+++ b/solution.py
@@ -47,23 +47,17 @@
     return (u.astype(f32) + v.astype(f32)).astype(bf16)
 
 
-def end_swap(a):
-    return lax.ppermute(a, ("ch", "cl"), [(1, 2), (2, 1)])
-
-
 def line_first(a):
-    return swap(a, "ch"), swap(a, "cl"), end_swap(a)
-
-
-def line_second(a, far, near, mid):
-    end = lax.ppermute(far, ("ch", "cl"), [(1, 0), (2, 3)])
-    return jnp.concatenate([a, near, far, mid + end], axis=0)
+    return swap(a, "ch"), swap(a, "cl")
+
+
+def line_second(a, far, near):
+    return jnp.concatenate([a, near, far, swap(far, "cl")], axis=0)
 
 
 def line_scatter_first(p):
     t = p.shape[0] // 4
-    end = lax.ppermute(p[3 * t :], ("ch", "cl"), [(0, 1), (3, 2)])
-    return end, swap(p[t : 2 * t], "cl"), end_swap(p[3 * t :])
+    return swap(p[3 * t :], "cl"), swap(p[t : 2 * t], "cl")
 
 
 def line_scatter_second(p, end):
@@ -71,9 +65,8 @@
     return swap(add(p[2 * t : 3 * t], end), "ch")
 
 
-def line_total(p, near, mid, far):
-    t = p.shape[0] // 4
-    return p[:t].astype(f32) + near.astype(f32) + far.astype(f32) + mid.astype(f32)
+def line_total(p, near, far):
+    return p[: near.shape[0]].astype(f32) + near.astype(f32) + far.astype(f32)
 
 
 def gather_axis(a, axis):
@@ -97,7 +90,7 @@
 
 
 def scatter_row(g, feat):
-    return lax.psum_scatter(g, ("ry", "rx", "dp"), scatter_dimension=feat, tiled=True)
+    return lax.psum_scatter(g, ("ry", "rx"), scatter_dimension=feat, tiled=True)
 
 
 class Place:
@@ -151,6 +144,34 @@
             part = jnp.concatenate([p(r) for p in parts], axis=0) if len(parts) > 1 else parts[0](r)
             got.append(row_send(part, k, self.rows) if k else part)
         return got
+
+    def to_tokens(self, a):
+        n, w = a.shape[0] // self.rows, a.shape[1]
+        cut = lambda y: lax.dynamic_slice_in_dim(a, y * 2 * n, 2 * n, 0)
+        got = [cut(self.ry)]
+        got += [row_send(cut((self.ry + j) % self.rows_y), 2 * j, self.rows) for j in range(1, self.rows_y)]
+        got = jnp.concatenate(got, axis=1)
+        part = lambda x: lax.dynamic_slice_in_dim(got, x * n, n, 0)
+        got = jnp.concatenate([part(self.rx), swap(part(1 - self.rx), "rx")], axis=1)
+        slot = lambda r: ((r % 2) ^ self.rx) * self.rows_y + (self.ry - r // 2) % self.rows_y
+        return jnp.concatenate(
+            [lax.dynamic_slice_in_dim(got, slot(r) * w, w, 1) for r in range(self.rows)], axis=1
+        )
+
+    def to_home(self, a):
+        n, w = a.shape[0], a.shape[1] // self.rows
+        lanes = lambda x: jnp.concatenate(
+            [lax.dynamic_slice_in_dim(a, (2 * y + x) * w, w, 1) for y in range(self.rows_y)], axis=1
+        )
+        got = jnp.concatenate([lanes(self.rx), swap(lanes(1 - self.rx), "rx")], axis=0)
+        cut = lambda y: lax.dynamic_slice_in_dim(got, y * w, w, 1)
+        out = [cut(self.ry)]
+        out += [row_send(cut((self.ry + j) % self.rows_y), 2 * j, self.rows) for j in range(1, self.rows_y)]
+        out = jnp.concatenate(out, axis=0)
+        slot = lambda r: (self.ry - r // 2) % self.rows_y * 2 + ((r % 2) ^ self.rx)
+        return jnp.concatenate(
+            [lax.dynamic_slice_in_dim(out, slot(r) * n, n, 0) for r in range(self.rows)], axis=0
+        )
 
     def by_lanes(self, got, lo, hi):
         w = got[0].shape[1]
@@ -229,6 +250,39 @@
             flops=2 * m * n * k, bytes_accessed=2 * (3 * m * n + m * k + n * k), transcendentals=m * n
         ),
     )(x, w, bias, grad_act)
+
+
+def outer(half, x, y, split, more=None):
+    k, m, n = x.shape[0], x.shape[1], y.shape[1]
+    m, n = (m // 2, n) if split == 0 else (m, n // 2)
+    tile = min(512, m)
+    steps = m // tile
+
+    def body(half_ref, x_ref, y_ref, *refs):
+        total = dot_tn(x_ref[...], y_ref[...])
+        if more is not None:
+            total = total + refs[0][...].astype(f32)
+        refs[-1][...] = total.astype(bf16)
+
+    out = pl.BlockSpec((tile, n), lambda i, half: (i, 0))
+    first = (lambda i, half: (0, half[0] * steps + i)) if split == 0 else (lambda i, half: (0, i))
+    second = (lambda i, half: (0, 0)) if split == 0 else (lambda i, half: (0, half[0]))
+    args = (x, y) if more is None else (x, y, more)
+    return pl.pallas_call(
+        body,
+        grid_spec=pltpu.PrefetchScalarGridSpec(
+            num_scalar_prefetch=1,
+            grid=(steps,),
+            in_specs=[pl.BlockSpec((k, tile), first), pl.BlockSpec((k, n), second)]
+            + [out] * (more is not None),
+            out_specs=out,
+        ),
+        out_shape=jax.ShapeDtypeStruct((m, n), bf16),
+        compiler_params=pltpu.CompilerParams(
+            dimension_semantics=("arbitrary",), vmem_limit_bytes=24 * 1024 * 1024
+        ),
+        cost_estimate=pl.CostEstimate(flops=1, bytes_accessed=1, transcendentals=0),
+    )(half, *args)
 
 
 def stack_heads(a, heads):
@@ -426,16 +480,18 @@
     lanes_of = lambda a, n: lambda r: lax.dynamic_slice_in_dim(a, r * n, n, 1)
 
     gather = lambda w, axis: lax.all_gather(half_of(w, axis), every, axis=axis, tiled=True)
-    qkv_weight = gather(jnp.concatenate([w_query, w_keyval], axis=1), 0)
-    out_weight = gather(w_out, 1)
+    qkvo_weight = gather(jnp.concatenate([w_query, w_keyval, w_out.T], axis=1), 0)
+    qkv_weight, out_weight = qkvo_weight[:, : hidden + 2 * head], qkvo_weight[:, hidden + 2 * head :]
     down_weight = gather(w_down, 1)
     up_weight = gather(w_up, 0)
 
     vectors = jnp.pad(jnp.stack([ln1_gain, ln1_bias, ln2_gain, ln2_bias, b_out, b_down]), ((0, 10), (0, 0)))
-    got = at.exchange(rows_of(tokens, t), rows_of(d_output, t), lambda r: vectors)
+    got = at.exchange(rows_of(tokens, t), lambda r: vectors)
     got = at.by_lanes(got, 0, got[0].shape[0])
-    own, own_grad = got[:t].astype(f32), got[t : 2 * t]
-    gain_one, bias_one, gain_two, bias_two, out_bias, down_bias = got[2 * t : 2 * t + 6].astype(f32)[:, None, :]
+    got, d_output = tie(got, d_output)
+    own = got[:t].astype(f32)
+    gain_one, bias_one, gain_two, bias_two, out_bias, down_bias = got[t : t + 6].astype(f32)[:, None, :]
+    own_grad = at.to_tokens(d_output)
 
     segments = segment_ids[0]
     base = jnp.stack([(col ^ k) * col_tokens + row * t for k in range(4)]).astype(jnp.int32)
@@ -449,7 +505,7 @@
 
     centred_one, inv_one = norm_parts(own)
     normed_one = (centred_one * gain_one + bias_one).astype(bf16)
-    block_one = line_second(normed_one, *line_first(normed_one))
+    block_one = line_second(normed_one, *tie(*line_first(normed_one)))
     block_one, own_grad = tie(block_one, own_grad)
     kv_bias = jnp.pad(b_value.astype(f32), (head, 0))
     kv = (dot_nn(block_one, qkv_weight[:, hidden:]) + kv_bias).astype(bf16)
@@ -460,71 +516,74 @@
     keys, values = kv[:, :head], kv[:, head:]
     attended, lse = attention.forward(bounds, queries, keys, values, low, pos)
 
-    part = dot_nn(attended, out_weight).astype(bf16)
+    part = dot_nt(attended, out_weight).astype(bf16)
     part, grad_first = tie(part, grad_first)
     block_grad = line_second(own_grad, *grad_first)
-    end, near, mid = line_scatter_first(part)
+    end, near = line_scatter_first(part)
     far = line_scatter_second(part, end)
-    near, mid, far, block_grad = tie(near, mid, far, block_grad)
-    hidden_one = own + out_bias + line_total(part, near, mid, far)
+    near, far, block_grad = tie(near, far, block_grad)
+    hidden_one = own + out_bias + line_total(part, near, far)
     centred_two, inv_two = norm_parts(hidden_one)
     normed_two = (centred_two * gain_two + bias_two).astype(bf16)
-    far, near, mid = line_first(normed_two)
-    near, mid, block_grad = tie(near, mid, block_grad)
+    far, near = line_first(normed_two)
     grad_act = multiply(block_grad, down_weight, "nt")
-    far, grad_act = tie(far, grad_act)
-    block_two = line_second(normed_two, far, near, mid)
-
+    far, near, grad_act = tie(far, near, grad_act)
+    block_two = line_second(normed_two, far, near)
+
+    core = at.dp.astype(jnp.int32).reshape(1)
     activated, grad_upper = feed_forward(block_two, up_weight, b_up.astype(f32)[None, :], grad_act)
     part = multiply(grad_upper, up_weight, "nt")
     part, activated, grad_upper = tie(part, activated, grad_upper)
-    end, near, mid = line_scatter_first(part)
-    end, mid, activated, grad_upper = tie(end, mid, activated, grad_upper)
+    end, near = line_scatter_first(part)
+    down_part = outer(1 - core, activated, block_grad, 0)
+    up_part = outer(1 - core, block_two, grad_upper, 1)
+    end, down_part, up_part, activated, grad_upper = tie(end, down_part, up_part, activated, grad_upper)
     far = line_scatter_second(part, end)
-    down_part = multiply(activated, block_grad, "tn", 1)
-    up_part = multiply(block_two, grad_upper, "tn", 1)
-    near, mid, far, down_part, up_part, activated = tie(near, mid, far, down_part, up_part, activated)
+    down_part, up_part = swap(down_part, "dp"), swap(up_part, "dp")
+    down_part = outer(core, activated, block_grad, 0, down_part)
+    up_part = outer(core, block_two, grad_upper, 1, up_part)
+    near, far, down_part, up_part, activated = tie(near, far, down_part, up_part, activated)
     down_part = scatter_row(down_part, 1)
     up_part = scatter_row(up_part, 0)
-    grad_two = line_total(part, near, mid, far)
+    grad_two = line_total(part, near, far)
     grad_hidden = own_grad.astype(f32) + norm_back(grad_two, centred_two, inv_two, gain_two)
     grad_branch = grad_hidden.astype(bf16)
-    far, near, mid = line_first(grad_branch)
-    near, mid, activated = tie(near, mid, activated)
-    final_part = multiply(activated, down_weight, "nn", 1)
-    far, final_part = tie(far, final_part)
-    block_branch = line_second(grad_branch, far, near, mid)
-    grad_att = dot_nt(block_branch, out_weight).astype(bf16)
-    grad_att, final_part = tie(grad_att, final_part)
-    final_end, final_near, final_mid = line_scatter_first(final_part)
+    far, near = line_first(grad_branch)
+    far, near, activated = tie(far, near, activated)
+    block_branch = line_second(grad_branch, far, near)
+    grad_att = dot_nn(block_branch, out_weight).astype(bf16)
     grad_query, grad_kv = attention.backward(
         bounds, queries, attended, grad_att, lse, keys, values, low, pos
     )
 
     grad_kv = grad_kv.astype(bf16)
-    grad_query, grad_kv, final_end, block_branch, attended = tie(
-        grad_query, grad_kv, final_end, block_branch, attended
-    )
+    grad_query, grad_kv, block_branch, attended, activated = tie(
+        grad_query, grad_kv, block_branch, attended, activated
+    )
+    final_part = multiply(activated, down_weight, "nn", 1)
     part = dot_nt(grad_query, qkv_weight[:, :hidden]).astype(bf16)
-    end, near, mid = line_scatter_first(part)
-    final_far = line_scatter_second(final_part, final_end)
+    end, near = line_scatter_first(part)
     kv_grad = at.sum_rows(lambda r: at.line_tokens(grad_kv, col, r, t)).astype(bf16)
-    kv_grad, end, grad_query, block_one, down_part, final_far, final_near, final_mid = tie(
-        kv_grad, end, grad_query, block_one, down_part, final_far, final_near, final_mid
-    )
     far = line_scatter_second(part, end)
+    kv_grad, grad_query, block_one, down_part = tie(kv_grad, grad_query, block_one, down_part)
     parts = [dot_tn(block_one, grad_query).astype(bf16), dot_tn(block_branch, attended).astype(bf16)]
-    shift = lambda a, k: jnp.concatenate([a[(j ^ k) * t : ((j ^ k) + 1) * t] for j in range(4)], axis=0)
-    kv_whole = add(kv_grad, shift(swap(kv_grad, "cl"), 1))
-    kv_whole = add(kv_whole, shift(swap(kv_whole, "ch"), 2))
-    near, mid, far, kv_whole, up_part = tie(near, mid, far, kv_whole, up_part)
-    qo_part = scatter_row(jnp.concatenate(parts, axis=1), 0)
-    kv_part = dot_tn(kv_whole, block_one).astype(bf16)
+    qo_part = jnp.concatenate(parts, axis=1)
+    cut = lambda k: kv_grad[k * t : (k + 1) * t]
+    got = swap(jnp.concatenate([cut(1), cut(3)], axis=0), "cl")
+    got, final_part = tie(got, final_part)
+    kv_own = add(add(cut(0), got[:t]), swap(add(cut(2), got[t:]), "ch"))
+    final_end, final_near = line_scatter_first(final_part)
+    grad_w_down = at.both_cores(down_part, 0)
+    kv_part = dot_tn(kv_own, normed_one).astype(bf16)
     kv_far = swap(lax.dynamic_slice_in_dim(kv_part, (1 - at.dp) * head, head, 0), "dp")
     kv_part = add(half_of(kv_part, 0), kv_far)
-    grad_one = line_total(part, near, mid, far) + dot_nt(kv_whole[:t], qkv_weight[:, hidden:])
+    near, far, kv_own, kv_part, up_part, qo_part, final_end, grad_w_down = tie(
+        near, far, kv_own, kv_part, up_part, qo_part, final_end, grad_w_down
+    )
+    final_far = line_scatter_second(final_part, final_end)
+    qo_part = lax.psum_scatter(qo_part, ("ry", "rx", "dp"), scatter_dimension=0, tiled=True)
+    grad_one = line_total(part, near, far) + dot_nt(kv_own, qkv_weight[:, hidden:])
     grad_own = grad_hidden + norm_back(grad_one, centred_one, inv_one, gain_one)
-    final = hidden_one + down_bias + line_total(final_part, final_near, final_mid, final_far)
 
     sums = lambda a: jnp.sum(a.astype(f32), axis=0)
     tiled = lambda a: jnp.tile(a.reshape(-1, row_width), (1, rows))
@@ -541,7 +600,7 @@
     )
     parts = [
         vectors,
-        tiled(jnp.pad(sums(kv_whole[:t, head:]), (0, row_width - head))),
+        tiled(jnp.pad(sums(kv_own[:, head:]), (0, row_width - head))),
         tiled(place(sums(grad_query))),
         tiled(place(sums(grad_upper))),
     ]
@@ -549,26 +608,22 @@
     parts.append(jnp.zeros((-n % 16, width), f32))
     packed = jnp.concatenate(parts).astype(bf16)
     n = packed.shape[0]
-    got = at.exchange(
-        lanes_of(packed, row_width),
-        lanes_of(grad_own.astype(bf16), row_width),
-        lanes_of(final.astype(bf16), row_width),
-        lanes_of(kv_part, row_width),
-    )
-    total = sum(g[:n].astype(f32) for g in got)
-    grad_tokens = at.by_rows(got, n, n + t).astype(f32)
-    output = at.by_rows(got, n + t, n + 2 * t)
-    kv_part = sum(g[n + 2 * t :].astype(f32) for g in got).astype(bf16)
-    grad_w_keyval = gather_axis(kv_part, "dp").reshape(2 * head, row_width).T.astype(f32)
+    packed = jnp.concatenate([packed, kv_part], axis=0)
+    got = at.exchange(lanes_of(packed, row_width), lanes_of(grad_own.astype(bf16), row_width))
+    total = sum(g[: n + head].astype(f32) for g in got)
+    grad_tokens = at.by_rows(got, n + head, n + head + t).astype(f32)
+    total, final_near, final_far = tie(total, final_near, final_far)
+    final = hidden_one + down_bias + line_total(final_part, final_near, final_far)
+    output = at.to_home(final.astype(bf16))
     for axis in ("cl", "ch"):
         total = total.astype(bf16)
         total = total.astype(f32) + swap(total, axis).astype(f32)
-    total = total.astype(bf16)
-    total = total.astype(f32) + swap(total, "dp").astype(f32)
-    grad_w_up = at.both_cores(up_part, 0)
-    grad_w_down = at.both_cores(down_part, 1)
+    total = gather_axis(total.astype(bf16), "dp").astype(f32)
+    grad_w_keyval = total[:, n:].reshape(2 * head, row_width).T
+    total = total[0, :n] + total[1, :n]
     qo_part = at.both_cores(qo_part, 0)
     grad_w_query, grad_w_out = qo_part[:, :hidden], qo_part[:, hidden:].T
+    grad_w_up = at.both_cores(up_part, 1)
     grad_ln1_gain, grad_ln1_bias, grad_ln2_gain, grad_ln2_bias, grad_b_out, grad_b_down = total[:6]
     grad_b_value = total[6, :head]
     of_col = lambda first, n: lax.dynamic_slice_in_dim(

time: 498 us -> 490 us (0.984)
  starting transfers between devices: 79.2 us -> 58.9 us
  other arithmetic: 42.2 us -> 50 us
    ppermute x27 -> x38, waiting for transfers between devices: 105 us -> 183 us  [swap(): return lax.ppermute(a, axis, [(0, 1), (1, 0)])]
    ppermute x16 -> x0, waiting for transfers between devices: 72.6 us -> none  [the longest x4 43.8 us: line_second(): end = lax.ppermute(far, ('ch', 'cl'), [(1, 0), (2, 3)])]
    ppermute x16 -> x0, starting transfers between devices: 23.1 us -> none  [the longest x4 9.8 us: line_scatter_first(): end = lax.ppermute(p[3 * t:], ('ch', 'cl'), [(0, 1), (3, 2)])]
    pallas_call x0 -> x4, Pallas kernels: none -> 14.7 us  [outer(): pl.pallas_call(body, grid_spec=pltpu.PrefetchScalarGridSpec(num_scalar_pr...]
    pallas_call x5 -> x3, Pallas kernels: 27 us -> 16.3 us  [multiply(): pl.pallas_call(body, grid=(steps,), in_specs=specs, out_specs=out_spec, o...]
    unnamed x190 -> x182, local copies, waits for them, and re-layouts: 32.6 us -> 25.5 us
    ppermute x10 -> x12, waiting for transfers between devices: 51.2 us -> 47.3 us  [row_send(): return lax.ppermute(a, ('ry', 'rx'), pairs)]
    concatenate x7 -> x14, other arithmetic: 12.7 us -> 16.3 us  [the longest x4 8.42 us: line_second(): return jnp.concatenate([a, near, far, swap(far, 'cl')], axis=0)]
  transfers between devices with their start and end apart: 60 -> 56, of which waited for: 29 -> 32; matrix products, arithmetic and copies ran while one was open for 16% -> 19% of each run, Pallas kernels for 7% -> 8%
where the time goes in v3:
time: 490 us; the launch traced here: 484 us
  waiting for transfers between devices  230 us (47%)
  starting transfers between devices  58.9 us (12%)
  Pallas kernels  55.3 us (11%)
  other arithmetic  50 us (10%)
  local copies, waits for them, and re-layouts  47.7 us (10%)
  matrix products  25.1 us (5%)
  between operations  16.4 us (3%)
    ppermute x38, waiting for transfers between devices, swap(): return lax.ppermute(a, axis, [(0, 1), (1, 0)])  183 us
    ppermute x12, waiting for transfers between devices, row_send(): return lax.ppermute(a, ('ry', 'rx'), pairs)  47.3 us
    ppermute x38, starting transfers between devices, swap(): return lax.ppermute(a, axis, [(0, 1), (1, 0)])  43.2 us
    unnamed x182, local copies, waits for them, and re-layouts  25.5 us
    pallas_call x3, Pallas kernels, multiply(): pl.pallas_call(body, grid=(steps,), in_specs=specs, out_specs=out_spec, o...  16.3 us
    ppermute x12, starting transfers between devices, row_send(): return lax.ppermute(a, ('ry', 'rx'), pairs)  15.2 us
    pallas_call x4, Pallas kernels, outer(): pl.pallas_call(body, grid_spec=pltpu.PrefetchScalarGridSpec(num_scalar_pr...  14.7 us
    dot_general x3, matrix products, dot_nt(): lax.dot_general(a, b, (((1,), (1,)), ((), ())), preferred_element_type=f32)  10 us
  transfers between devices with their start and end apart: 56, of which 32 were waited for; matrix products, arithmetic and copies ran while one was open for 19% of the time, Pallas kernels for 8%

profile of v3, /device:TPU:0, one launch (start us, length us, event | category | flops | bytes accessed | tf_op | source)
XLA Modules:
  0.0 483.6 jit_solution(4199836176051521246)
XLA Ops:
  15.7 4.0 collective-permute-start.2
  21.2 4.0 collective-permute-done.2
  25.1 3.3 collective-permute-done.1
  36.3 3.0 collective-permute-done.6
  41.2 16.6 %collective-permute-done.3 = bf16[128,2048]{1,0:T(8,128)(2,1)S(1)} collective-permute-done((bf16[128,2048]{1,0:T(8,128)(2,1)S(1)}, bf16[128,2048]{1,0:T(8,128)(2,1)S(1)}, u32[]{:S(2)}, u32[]{:S(2)}) %collective-permute-start.3) | collective-permute-done | bytes 524320 | tf_op jit(solution)/shard_map/ppermute | solution.py:32
  60.1 10.6 %collective-permute-done.5 = bf16[128,2048]{1,0:T(8,128)(2,1)} collective-permute-done((bf16[128,2048]{1,0:T(8,128)(2,1)S(1)}, bf16[128,2048]{1,0:T(8,128)(2,1)}, u32[]{:S(2)}, u32[]{:S(2)}) %collective-permute-start.5) | collective-permute-done | bytes 524320 | tf_op jit(solution)/shard_map/ppermute | solution.py:32
  73.5 3.3 collective-permute-start.11
  84.9 2.9 fusion.12.q_ref
  87.7 7.6 %collective-permute-done.10 = bf16[512,256]{1,0:T(8,128)(2,1)S(1)} collective-permute-done((bf16[512,256]{1,0:T(8,128)(2,1)S(1)}, bf16[512,256]{1,0:T(8,128)(2,1)S(1)}, u32[]{:S(2)}, u32[]{:S(2)}) %collective-permute-start.10) | collective-permute-done | bytes 262176 | tf_op jit(solution)/shard_map/ppermute | solution.py:84
  95.4 4.5 collective-permute-done.9
  100.4 6.1 %shard_map.288 = (bf16[512,512]{1,0:T(8,128)(2,1)S(1)}, f32[4,1,512]{2,1,0:T(1,128)S(1)}) custom-call(s32[4,2]{1,0:T(4,128)S(1)} %pad_add_fusion.1.bounds, bf16[512,512]{1,0:T(8,128)(2,1)S(1)} %fusion.12.q_ref, bf16[2048,128]{1,0:T(8,128)(2,1)S(1)} %get-tuple-element.231.k_ref, bf16[2048,128]{1,0:T(8,128)(2,1)S(1)} %get-tuple-element.230.v_ref, ...), custom_call_target="tpu_custom_call" | custom-call | flops 2147483648 | bytes 4194304 | tf_op jit(solution)/shard_map/pallas_call | solution.py:387
  106.5 3.1 convolution_convert_fusion.3
  113.3 11.3 %collective-permute-done.14 = bf16[128,2048]{1,0:T(8,128)(2,1)S(1)} collective-permute-done((bf16[128,2048]{1,0:T(8,128)(2,1)S(1)}, bf16[128,2048]{1,0:T(8,128)(2,1)S(1)}, u32[]{:S(2)}, u32[]{:S(2)}) %collective-permute-start.14) | collective-permute-done | bytes 524320 | tf_op jit(solution)/shard_map/ppermute | solution.py:32
  126.7 30.3 %collective-permute-done.16 = bf16[128,2048]{1,0:T(8,128)(2,1)S(1)} collective-permute-done((bf16[128,2048]{1,0:T(8,128)(2,1)}, bf16[128,2048]{1,0:T(8,128)(2,1)S(1)}, u32[]{:S(2)}, u32[]{:S(2)}) %collective-permute-start.16) | collective-permute-done | bytes 524320 | tf_op jit(solution)/shard_map/ppermute | solution.py:32
  165.1 3.4 copy-done.11
  168.5 5.3 %shard_map.289.g_ref = bf16[512,2048]{1,0:T(8,128)(2,1)S(1)} custom-call(bf16[512,2048]{1,0:T(8,128)(2,1)S(1)} %pad_maximum_fusion.2.x_ref.y_ref, bf16[2048,2048]{1,0:T(8,128)(2,1)S(1)} %copy-done.11), custom_call_target="tpu_custom_call" | custom-call | flops 4294967296 | bytes 12582912 | tf_op jit(solution)/shard_map/pallas_call | solution.py:209
  175.1 11.4 %collective-permute-done.17 = bf16[128,2048]{1,0:T(8,128)(2,1)} collective-permute-done((bf16[128,2048]{1,0:T(8,128)(2,1)S(1)}, bf16[128,2048]{1,0:T(8,128)(2,1)}, u32[]{:S(2)}, u32[]{:S(2)}) %collective-permute-start.17) | collective-permute-done | bytes 524320 | tf_op jit(solution)/shard_map/ppermute | solution.py:32
  186.9 12.8 %collective-permute-done.19 = bf16[128,2048]{1,0:T(8,128)(2,1)S(1)} collective-permute-done((bf16[128,2048]{1,0:T(8,128)(2,1)}, bf16[128,2048]{1,0:T(8,128)(2,1)S(1)}, u32[]{:S(2)}, u32[]{:S(2)}) %collective-permute-start.19) | collective-permute-done | bytes 524320 | tf_op jit(solution)/shard_map/ppermute | solution.py:32
  199.7 2.9 pad_maximum_fusion.3.x_ref
  204.2 3.4 copy-done.17
  209.2 9.7 %shard_map.290 = (bf16[512,2048]{1,0:T(8,128)(2,1)S(1)}, bf16[512,2048]{1,0:T(8,128)(2,1)S(1)}) custom-call(bf16[512,2048]{1,0:T(8,128)(2,1)S(1)} %copy-done.4, bf16[2048,2048]{1,0:T(8,128)(2,1)S(1)} %copy-done.17, f32[1,2048]{1,0:T(1,128)S(1)} %bitcast.64, bf16[512,2048]{1,0:T(8,128)(2,1)S(1)} %copy-done.19), custom_call_target="tpu_custom_call" | custom-call | flops 4294967296 | bytes 16777216 | tf_op jit(solution)/shard_map/pallas_call | solution.py:240
  218.9 5.3 %shard_map.291 = bf16[512,2048]{1,0:T(8,128)(2,1)S(1)} custom-call(bf16[512,2048]{1,0:T(8,128)(2,1)S(1)} %get-tuple-element.99.x_ref.y_ref, bf16[2048,2048]{1,0:T(8,128)(2,1)S(1)} %copy-done.17), custom_call_target="tpu_custom_call" | custom-call | flops 4294967296 | bytes 12582912 | tf_op jit(solution)/shard_map/pallas_call | solution.py:209
  229.5 4.4 shard_map.293
  233.9 3.3 collective-permute-done.21
  238.9 4.2 collective-permute-start.22
  243.1 7.2 %collective-permute-done.23.refs_0_ = bf16[1024,2048]{1,0:T(8,128)(2,1)S(1)} collective-permute-done((bf16[1024,2048]{1,0:T(8,128)(2,1)S(1)}, bf16[1024,2048]{1,0:T(8,128)(2,1)S(1)}, u32[]{:S(2)}, u32[]{:S(2)}) %collective-permute-start.23) | collective-permute-done | bytes 4194336 | tf_op jit(solution)/shard_map/ppermute | solution.py:32
  256.6 4.9 %shard_map.295 = bf16[2048,1024]{1,0:T(8,128)(2,1)S(1)} custom-call(s32[1]{0:T(128)} %bitcast.18.half_ref, bf16[512,2048]{1,0:T(8,128)(2,1)S(1)} %copy-done.6, bf16[512,2048]{1,0:T(8,128)(2,1)S(1)} %get-tuple-element.99.x_ref.y_ref, bf16[2048,1024]{1,0:T(8,128)(2,1)} %collective-permute-done.24.refs_0_), custom_call_target="tpu_custom_call" | custom-call | flops 1 | bytes 1 | tf_op jit(solution)/shard_map/pallas_call | solution.py:271
  263.6 2.9 collective-permute-done.22
  269.0 3.2 fusion.56
  275.1 22.4 %collective-permute-done.25 = bf16[128,2048]{1,0:T(8,128)(2,1)} collective-permute-done((bf16[128,2048]{1,0:T(8,128)(2,1)S(1)}, bf16[128,2048]{1,0:T(8,128)(2,1)}, u32[]{:S(2)}, u32[]{:S(2)}) %collective-permute-start.25) | collective-permute-done | bytes 524320 | tf_op jit(solution)/shard_map/ppermute | solution.py:32
  302.4 9.8 %collective-permute-done.27 = bf16[128,2048]{1,0:T(8,128)(2,1)} collective-permute-done((bf16[128,2048]{1,0:T(8,128)(2,1)}, bf16[128,2048]{1,0:T(8,128)(2,1)}, u32[]{:S(2)}, u32[]{:S(2)}) %collective-permute-start.27) | collective-permute-done | bytes 524320 | tf_op jit(solution)/shard_map/ppermute | solution.py:32
  312.2 3.3 fusion.9.g_ref
  315.5 8.5 %shard_map.296 = (bf16[512,512]{1,0:T(8,128)(2,1)S(1)}, f32[2048,256]{1,0:T(8,128)S(1)}) custom-call(s32[4,2]{1,0:T(4,128)S(1)} %pad_add_fusion.1.bounds, bf16[512,512]{1,0:T(8,128)(2,1)S(1)} %copy-done.23, bf16[512,512]{1,0:T(8,128)(2,1)S(1)} %copy-done.21, bf16[512,512]{1,0:T(8,128)(2,1)S(1)} %fusion.9.g_ref, f32[4,1,512]{2,1,0:T(1,128)S(1)} %get-tuple-element.106.lse_ref, ...), custom_call_target="tpu_custom_call" | custom-call | flops 5368709120 | bytes 8388608 | tf_op jit(solution)/shard_map/pallas_call | solution.py:409
  328.4 3.0 convolution_convert_fusion.2
  337.0 5.8 %shard_map.297 = bf16[512,2048]{1,0:T(8,128)(2,1)S(1)} custom-call(bf16[512,2048]{1,0:T(8,128)(2,1)S(1)} %copy-done.8, bf16[2048,2048]{1,0:T(8,128)(2,1)S(1)} %bitcast.63), custom_call_target="tpu_custom_call" | custom-call | flops 1 | bytes 1 | tf_op jit(solution)/shard_map/pallas_call | solution.py:209
  342.8 8.0 %collective-permute-done.28 = bf16[1024,256]{1,0:T(8,128)(2,1)S(1)} collective-permute-done((bf16[1024,256]{1,0:T(8,128)(2,1)S(1)}, bf16[1024,256]{1,0:T(8,128)(2,1)S(1)}, u32[]{:S(2)}, u32[]{:S(2)}) %collective-permute-start.28) | collective-permute-done | bytes 524320 | tf_op jit(solution)/shard_map/ppermute | solution.py:84
  352.7 3.8 collective-permute-done.32
  362.0 3.1 convolution_convert_fusion.1
  367.7 3.8 collective-permute-done.30
  376.0 8.2 %collective-permute-done.34 = bf16[128,256]{1,0:T(8,128)(2,1)} collective-permute-done((bf16[128,256]{1,0:T(8,128)(2,1)S(1)}, bf16[128,256]{1,0:T(8,128)(2,1)}, u32[]{:S(2)}, u32[]{:S(2)}) %collective-permute-start.34) | collective-permute-done | bytes 65568 | tf_op jit(solution)/shard_map/ppermute | solution.py:32
  393.7 8.0 %collective-permute-done.36 = bf16[128,2048]{1,0:T(8,128)(2,1)S(1)} collective-permute-done((bf16[128,2048]{1,0:T(8,128)(2,1)}, bf16[128,2048]{1,0:T(8,128)(2,1)S(1)}, u32[]{:S(2)}, u32[]{:S(2)}) %collective-permute-start.36) | collective-permute-done | bytes 524320 | tf_op jit(solution)/shard_map/ppermute | solution.py:32
  402.5 3.9 fusion.24
  406.6 3.3 concatenate.133
  419.4 5.0 %collective-permute-done.40 = bf16[288,512]{1,0:T(8,128)(2,1)} collective-permute-done((bf16[288,512]{1,0:T(8,128)(2,1)}, bf16[288,512]{1,0:T(8,128)(2,1)}, u32[]{:S(2)}, u32[]{:S(2)}) %collective-permute-start.40) | collective-permute-done | bytes 294944 | tf_op jit(solution)/shard_map/ppermute | solution.py:84
  425.3 7.5 %collective-permute-done.39 = bf16[288,512]{1,0:T(8,128)(2,1)} collective-permute-done((bf16[288,512]{1,0:T(8,128)(2,1)}, bf16[288,512]{1,0:T(8,128)(2,1)}, u32[]{:S(2)}, u32[]{:S(2)}) %collective-permute-start.39) | collective-permute-done | bytes 294944 | tf_op jit(solution)/shard_map/ppermute | solution.py:84
  435.9 6.9 %collective-permute-done.42 = bf16[128,2048]{1,0:T(8,128)(2,1)} collective-permute-done((bf16[128,2048]{1,0:T(8,128)(2,1)S(1)}, bf16[128,2048]{1,0:T(8,128)(2,1)}, u32[]{:S(2)}, u32[]{:S(2)}) %collective-permute-start.42) | collective-permute-done | bytes 524320 | tf_op jit(solution)/shard_map/ppermute | solution.py:32
  444.6 4.2 collective-permute-done.45
  452.4 6.2 %collective-permute-done.46 = bf16[160,512]{1,0:T(8,128)(2,1)S(1)} collective-permute-done((bf16[160,512]{1,0:T(8,128)(2,1)S(1)}, bf16[160,512]{1,0:T(8,128)(2,1)S(1)}, u32[]{:S(2)}, u32[]{:S(2)}) %collective-permute-start.46) | collective-permute-done | bytes 163872 | tf_op jit(solution)/shard_map/ppermute | solution.py:32
  (401 shorter events, 147.9 us)
Async XLA Ops:
  7.2 71.3 %all-gather.4.cloned.1.call-start = ((), (), s32[]{:S(2)}) async-start(), calls=%async_computation.3 | async-start | bytes 5898240 | tf_op jit(solution)/shard_map/all_gather | solution.py:482
  11.6 153.5 %all-gather.6.cloned.1.call-start = ((), (), s32[]{:S(2)}) async-start(), calls=%async_computation.4 | async-start | bytes 9437184 | tf_op jit(solution)/shard_map/all_gather | solution.py:482
  12.8 189.8 %all-gather.8.cloned.1.call-start = ((), (), s32[]{:S(2)}) async-start(), calls=%async_computation.5 | async-start | bytes 9437184 | tf_op jit(solution)/shard_map/all_gather | solution.py:482
  15.3 346.0 %reduce-scatter.4.cloned.1.call-start = ((), (), s32[]{:S(2)}) async-start(), calls=%async_computation.6 | async-start | bytes 5242880 | tf_op jit(solution)/shard_map/reduce_scatter | solution.py:93
  15.7 9.5 %collective-permute-start.2 = (bf16[144,512]{1,0:T(8,128)(2,1)S(1)}, bf16[144,512]{1,0:T(8,128)(2,1)S(1)}, u32[]{:S(2)}, u32[]{:S(2)}) collective-permute-start(bf16[144,512]{1,0:T(8,128)(2,1)S(1)} %get-tuple-element.288), channel_id=1, source_target_pairs={{0,12},{4,8},{8,4},{12,0},{1,13},{5,9},{9,5},{13,1},{2,14},{6,10},... | collective-permute-start | bytes 442376 | tf_op jit(solution)/shard_map/ppermute | solution.py:84
  20.2 10.2 %collective-permute-start = (bf16[144,512]{1,0:T(8,128)(2,1)S(1)}, bf16[144,512]{1,0:T(8,128)(2,1)S(1)}, u32[]{:S(2)}, u32[]{:S(2)}) collective-permute-start(bf16[144,512]{1,0:T(8,128)(2,1)S(1)} %get-tuple-element.286), channel_id=1, source_target_pairs={{0,4},{4,0},{8,12},{12,8},{1,5},{5,1},{9,13},{13,9},{2,6},{6,2},{1... | collective-permute-start | bytes 442376 | tf_op jit(solution)/shard_map/ppermute | solution.py:84
  32.0 25.8 %collective-permute-start.3 = (bf16[128,2048]{1,0:T(8,128)(2,1)S(1)}, bf16[128,2048]{1,0:T(8,128)(2,1)S(1)}, u32[]{:S(2)}, u32[]{:S(2)}) collective-permute-start(bf16[128,2048]{1,0:T(8,128)(2,1)S(1)} %fusion.23), channel_id=1, source_target_pairs={{0,2},{2,0},{1,3},{3,1},{4,6},{6,4},{5,7},{7,5},{8,10},{10,8},{9,1... | collective-permute-start | bytes 1572872 | tf_op jit(solution)/shard_map/ppermute | solution.py:32
  34.7 23.4 %collective-permute-start.4 = (bf16[128,2048]{1,0:T(8,128)(2,1)S(1)}, bf16[128,2048]{1,0:T(8,128)(2,1)S(1)}, u32[]{:S(2)}, u32[]{:S(2)}) collective-permute-start(bf16[128,2048]{1,0:T(8,128)(2,1)S(1)} %fusion.23), channel_id=1, source_target_pairs={{0,1},{1,0},{2,3},{3,2},{4,5},{5,4},{6,7},{7,6},{8,9},{9,8},{10,11... | collective-permute-start | bytes 1572872 | tf_op jit(solution)/shard_map/ppermute | solution.py:32
  39.4 20.3 %collective-permute-start.7 = (bf16[128,1024]{1,0:T(8,128)(2,1)S(1)}, bf16[128,1024]{1,0:T(8,128)(2,1)S(1)}, u32[]{:S(2)}, u32[]{:S(2)}) collective-permute-start(bf16[128,1024]{1,0:T(8,128)(2,1)S(1)} %get-tuple-element.262), channel_id=1, source_target_pairs={{0,4},{4,0},{1,5},{5,1},{2,6},{6,2},{3,7},{7,3},{8,12},{12,8},{9,1... | collective-permute-start | bytes 786440 | tf_op jit(solution)/shard_map/ppermute | solution.py:32
  58.0 12.7 %collective-permute-start.5 = (bf16[128,2048]{1,0:T(8,128)(2,1)S(1)}, bf16[128,2048]{1,0:T(8,128)(2,1)}, u32[]{:S(2)}, u32[]{:S(2)}) collective-permute-start(bf16[128,2048]{1,0:T(8,128)(2,1)S(1)} %collective-permute-done.3), channel_id=1, source_target_pairs={{0,1},{1,0},{2,3},{3,2},{4,5},{5,4},{6,7},{7,6},{8,9},{9,8},{10,11... | collective-permute-start | bytes 1572872 | tf_op jit(solution)/shard_map/ppermute | solution.py:32
  73.5 36.1 %collective-permute-start.11 = (bf16[128,2048]{1,0:T(8,128)(2,1)S(1)}, bf16[128,2048]{1,0:T(8,128)(2,1)}, u32[]{:S(2)}, u32[]{:S(2)}) collective-permute-start(bf16[128,2048]{1,0:T(8,128)(2,1)S(1)} %pad_maximum_fusion.8), channel_id=1, source_target_pairs={{0,2},{2,0},{1,3},{3,1},{4,6},{6,4},{5,7},{7,5},{8,10},{10,8},{9,1... | collective-permute-start | bytes 1572872 | tf_op jit(solution)/shard_map/ppermute | solution.py:32
  76.8 32.9 %collective-permute-start.12 = (bf16[128,2048]{1,0:T(8,128)(2,1)S(1)}, bf16[128,2048]{1,0:T(8,128)(2,1)S(1)}, u32[]{:S(2)}, u32[]{:S(2)}) collective-permute-start(bf16[128,2048]{1,0:T(8,128)(2,1)S(1)} %pad_maximum_fusion.8), channel_id=1, source_target_pairs={{0,1},{1,0},{2,3},{3,2},{4,5},{5,4},{6,7},{7,6},{8,9},{9,8},{10,11... | collective-permute-start | bytes 1572872 | tf_op jit(solution)/shard_map/ppermute | solution.py:32
  81.3 14.1 %collective-permute-start.10 = (bf16[512,256]{1,0:T(8,128)(2,1)S(1)}, bf16[512,256]{1,0:T(8,128)(2,1)S(1)}, u32[]{:S(2)}, u32[]{:S(2)}) collective-permute-start(bf16[512,256]{1,0:T(8,128)(2,1)S(1)} %fusion.15), channel_id=1, source_target_pairs={{0,12},{4,8},{8,4},{12,0},{1,13},{5,9},{9,5},{13,1},{2,14},{6,10},... | collective-permute-start | bytes 786440 | tf_op jit(solution)/shard_map/ppermute | solution.py:84
  82.2 17.6 %collective-permute-start.9 = (bf16[512,256]{1,0:T(8,128)(2,1)S(1)}, bf16[512,256]{1,0:T(8,128)(2,1)S(1)}, u32[]{:S(2)}, u32[]{:S(2)}) collective-permute-start(bf16[512,256]{1,0:T(8,128)(2,1)S(1)} %fusion.15), channel_id=1, source_target_pairs={{0,8},{4,12},{8,0},{12,4},{1,9},{5,13},{9,1},{13,5},{2,10},{6,14},... | collective-permute-start | bytes 786440 | tf_op jit(solution)/shard_map/ppermute | solution.py:84
  82.5 17.3 %collective-permute-start.8 = (bf16[512,256]{1,0:T(8,128)(2,1)S(1)}, bf16[512,256]{1,0:T(8,128)(2,1)S(1)}, u32[]{:S(2)}, u32[]{:S(2)}) collective-permute-start(bf16[512,256]{1,0:T(8,128)(2,1)S(1)} %fusion.15), channel_id=1, source_target_pairs={{0,4},{4,0},{8,12},{12,8},{1,5},{5,1},{9,13},{13,9},{2,6},{6,2},{1... | collective-permute-start | bytes 786440 | tf_op jit(solution)/shard_map/ppermute | solution.py:84
  109.8 14.9 %collective-permute-start.14 = (bf16[128,2048]{1,0:T(8,128)(2,1)S(1)}, bf16[128,2048]{1,0:T(8,128)(2,1)S(1)}, u32[]{:S(2)}, u32[]{:S(2)}) collective-permute-start(bf16[128,2048]{1,0:T(8,128)(2,1)S(1)} %get-tuple-element.210), channel_id=1, source_target_pairs={{0,1},{1,0},{2,3},{3,2},{4,5},{5,4},{6,7},{7,6},{8,9},{9,8},{10,11... | collective-permute-start | bytes 1572872 | tf_op jit(solution)/shard_map/ppermute | solution.py:32
  111.3 46.9 %collective-permute-start.13 = (bf16[128,2048]{1,0:T(8,128)(2,1)S(1)}, bf16[128,2048]{1,0:T(8,128)(2,1)S(1)}, u32[]{:S(2)}, u32[]{:S(2)}) collective-permute-start(bf16[128,2048]{1,0:T(8,128)(2,1)S(1)} %get-tuple-element.211), channel_id=1, source_target_pairs={{0,1},{1,0},{2,3},{3,2},{4,5},{5,4},{6,7},{7,6},{8,9},{9,8},{10,11... | collective-permute-start | bytes 1572872 | tf_op jit(solution)/shard_map/ppermute | solution.py:32
  111.9 45.1 %collective-permute-start.16 = (bf16[128,2048]{1,0:T(8,128)(2,1)}, bf16[128,2048]{1,0:T(8,128)(2,1)S(1)}, u32[]{:S(2)}, u32[]{:S(2)}) collective-permute-start(bf16[128,2048]{1,0:T(8,128)(2,1)} %collective-permute-done.11), channel_id=1, source_target_pairs={{0,1},{1,0},{2,3},{3,2},{4,5},{5,4},{6,7},{7,6},{8,9},{9,8},{10,11... | collective-permute-start | bytes 1572872 | tf_op jit(solution)/shard_map/ppermute | solution.py:32
  124.8 33.4 %collective-permute-start.15 = (bf16[128,2048]{1,0:T(8,128)(2,1)S(1)}, bf16[128,2048]{1,0:T(8,128)(2,1)S(1)}, u32[]{:S(2)}, u32[]{:S(2)}) collective-permute-start(bf16[128,2048]{1,0:T(8,128)(2,1)S(1)} %add_convert_fusion.6), channel_id=1, source_target_pairs={{0,2},{2,0},{1,3},{3,1},{4,6},{6,4},{5,7},{7,5},{8,10},{10,8},{9,1... | collective-permute-start | bytes 1572872 | tf_op jit(solution)/shard_map/ppermute | solution.py:32
  161.4 25.0 %collective-permute-start.17 = (bf16[128,2048]{1,0:T(8,128)(2,1)S(1)}, bf16[128,2048]{1,0:T(8,128)(2,1)}, u32[]{:S(2)}, u32[]{:S(2)}) collective-permute-start(bf16[128,2048]{1,0:T(8,128)(2,1)S(1)} %add_convert_fusion.5), channel_id=1, source_target_pairs={{0,2},{2,0},{1,3},{3,1},{4,6},{6,4},{5,7},{7,5},{8,10},{10,8},{9,1... | collective-permute-start | bytes 1572872 | tf_op jit(solution)/shard_map/ppermute | solution.py:32
  162.7 23.8 %collective-permute-start.18 = (bf16[128,2048]{1,0:T(8,128)(2,1)S(1)}, bf16[128,2048]{1,0:T(8,128)(2,1)}, u32[]{:S(2)}, u32[]{:S(2)}) collective-permute-start(bf16[128,2048]{1,0:T(8,128)(2,1)S(1)} %add_convert_fusion.5), channel_id=1, source_target_pairs={{0,1},{1,0},{2,3},{3,2},{4,5},{5,4},{6,7},{7,6},{8,9},{9,8},{10,11... | collective-permute-start | bytes 1572872 | tf_op jit(solution)/shard_map/ppermute | solution.py:32
  186.5 13.2 %collective-permute-start.19 = (bf16[128,2048]{1,0:T(8,128)(2,1)}, bf16[128,2048]{1,0:T(8,128)(2,1)S(1)}, u32[]{:S(2)}, u32[]{:S(2)}) collective-permute-start(bf16[128,2048]{1,0:T(8,128)(2,1)} %collective-permute-done.17), channel_id=1, source_target_pairs={{0,1},{1,0},{2,3},{3,2},{4,5},{5,4},{6,7},{7,6},{8,9},{9,8},{10,11... | collective-permute-start | bytes 1572872 | tf_op jit(solution)/shard_map/ppermute | solution.py:32
  225.1 12.0 %collective-permute-start.21 = (bf16[128,2048]{1,0:T(8,128)(2,1)S(1)}, bf16[128,2048]{1,0:T(8,128)(2,1)S(1)}, u32[]{:S(2)}, u32[]{:S(2)}) collective-permute-start(bf16[128,2048]{1,0:T(8,128)(2,1)S(1)} %get-tuple-element.208), channel_id=1, source_target_pairs={{0,1},{1,0},{2,3},{3,2},{4,5},{5,4},{6,7},{7,6},{8,9},{9,8},{10,11... | collective-permute-start | bytes 1572872 | tf_op jit(solution)/shard_map/ppermute | solution.py:32
  237.2 13.1 %collective-permute-start.23 = (bf16[1024,2048]{1,0:T(8,128)(2,1)S(1)}, bf16[1024,2048]{1,0:T(8,128)(2,1)S(1)}, u32[]{:S(2)}, u32[]{:S(2)}) collective-permute-start(bf16[1024,2048]{1,0:T(8,128)(2,1)S(1)} %shard_map.292), channel_id=1, source_target_pairs={{0,16},{16,0},{1,17},{17,1},{2,18},{18,2},{3,19},{19,3},{4,20},{20... | collective-permute-start | bytes 12582920 | tf_op jit(solution)/shard_map/ppermute | solution.py:32
  237.2 17.8 %collective-permute-start.24 = (bf16[2048,1024]{1,0:T(8,128)(2,1)}, bf16[2048,1024]{1,0:T(8,128)(2,1)}, u32[]{:S(2)}, u32[]{:S(2)}) collective-permute-start(bf16[2048,1024]{1,0:T(8,128)(2,1)} %shard_map.293), channel_id=1, source_target_pairs={{0,16},{16,0},{1,17},{17,1},{2,18},{18,2},{3,19},{19,3},{4,20},{20... | collective-permute-start | bytes 12582920 | tf_op jit(solution)/shard_map/ppermute | solution.py:32
  237.7 25.9 %collective-permute-start.20 = (bf16[128,2048]{1,0:T(8,128)(2,1)}, bf16[128,2048]{1,0:T(8,128)(2,1)S(1)}, u32[]{:S(2)}, u32[]{:S(2)}) collective-permute-start(bf16[128,2048]{1,0:T(8,128)(2,1)} %get-tuple-element.209), channel_id=1, source_target_pairs={{0,1},{1,0},{2,3},{3,2},{4,5},{5,4},{6,7},{7,6},{8,9},{9,8},{10,11... | collective-permute-start | bytes 1572872 | tf_op jit(solution)/shard_map/ppermute | solution.py:32
  238.9 27.6 %collective-permute-start.22 = (bf16[128,2048]{1,0:T(8,128)(2,1)}, bf16[128,2048]{1,0:T(8,128)(2,1)}, u32[]{:S(2)}, u32[]{:S(2)}) collective-permute-start(bf16[128,2048]{1,0:T(8,128)(2,1)} %add_convert_fusion.4), channel_id=1, source_target_pairs={{0,2},{2,0},{1,3},{3,1},{4,6},{6,4},{5,7},{7,5},{8,10},{10,8},{9,1... | collective-permute-start | bytes 1572872 | tf_op jit(solution)/shard_map/ppermute | solution.py:32
  266.5 127.2 %reduce-scatter.6.cloned.1.call-start = ((), (), s32[]{:S(2)}) async-start(), calls=%async_computation.7 | async-start | bytes 5242880 | tf_op jit(solution)/shard_map/reduce_scatter | solution.py:93
  272.2 25.3 %collective-permute-start.25 = (bf16[128,2048]{1,0:T(8,128)(2,1)S(1)}, bf16[128,2048]{1,0:T(8,128)(2,1)}, u32[]{:S(2)}, u32[]{:S(2)}) collective-permute-start(bf16[128,2048]{1,0:T(8,128)(2,1)S(1)} %get-tuple-element.195), channel_id=1, source_target_pairs={{0,2},{2,0},{1,3},{3,1},{4,6},{6,4},{5,7},{7,5},{8,10},{10,8},{9,1... | collective-permute-start | bytes 1572872 | tf_op jit(solution)/shard_map/ppermute | solution.py:32
  273.0 24.6 %collective-permute-start.26 = (bf16[128,2048]{1,0:T(8,128)(2,1)S(1)}, bf16[128,2048]{1,0:T(8,128)(2,1)S(1)}, u32[]{:S(2)}, u32[]{:S(2)}) collective-permute-start(bf16[128,2048]{1,0:T(8,128)(2,1)S(1)} %get-tuple-element.195), channel_id=1, source_target_pairs={{0,1},{1,0},{2,3},{3,2},{4,5},{5,4},{6,7},{7,6},{8,9},{9,8},{10,11... | collective-permute-start | bytes 1572872 | tf_op jit(solution)/shard_map/ppermute | solution.py:32
  298.3 13.9 %collective-permute-start.27 = (bf16[128,2048]{1,0:T(8,128)(2,1)}, bf16[128,2048]{1,0:T(8,128)(2,1)}, u32[]{:S(2)}, u32[]{:S(2)}) collective-permute-start(bf16[128,2048]{1,0:T(8,128)(2,1)} %collective-permute-done.25), channel_id=1, source_target_pairs={{0,1},{1,0},{2,3},{3,2},{4,5},{5,4},{6,7},{7,6},{8,9},{9,8},{10,11... | collective-permute-start | bytes 1572872 | tf_op jit(solution)/shard_map/ppermute | solution.py:32
  302.1 163.9 %reduce-scatter.8.cloned.1.call-start = ((), (), s32[]{:S(2)}) async-start(), calls=%async_computation.8 | async-start | bytes 4718592 | tf_op jit(solution)/shard_map/reduce_scatter | solution.py:584
  326.8 24.0 %collective-permute-start.28 = (bf16[1024,256]{1,0:T(8,128)(2,1)S(1)}, bf16[1024,256]{1,0:T(8,128)(2,1)S(1)}, u32[]{:S(2)}, u32[]{:S(2)}) collective-permute-start(bf16[1024,256]{1,0:T(8,128)(2,1)S(1)} %get-tuple-element.215), channel_id=1, source_target_pairs={{0,8},{4,12},{8,0},{12,4},{1,9},{5,13},{9,1},{13,5},{2,10},{6,14},... | collective-permute-start | bytes 1572872 | tf_op jit(solution)/shard_map/ppermute | solution.py:84
  332.3 61.4 %collective-permute-start.31 = (bf16[128,2048]{1,0:T(8,128)(2,1)}, bf16[128,2048]{1,0:T(8,128)(2,1)}, u32[]{:S(2)}, u32[]{:S(2)}) collective-permute-start(bf16[128,2048]{1,0:T(8,128)(2,1)} %get-tuple-element.207), channel_id=1, source_target_pairs={{0,1},{1,0},{2,3},{3,2},{4,5},{5,4},{6,7},{7,6},{8,9},{9,8},{10,11... | collective-permute-start | bytes 1572872 | tf_op jit(solution)/shard_map/ppermute | solution.py:32
  333.0 23.6 %collective-permute-start.32 = (bf16[128,2048]{1,0:T(8,128)(2,1)S(1)}, bf16[128,2048]{1,0:T(8,128)(2,1)S(1)}, u32[]{:S(2)}, u32[]{:S(2)}) collective-permute-start(bf16[128,2048]{1,0:T(8,128)(2,1)S(1)} %get-tuple-element.206), channel_id=1, source_target_pairs={{0,1},{1,0},{2,3},{3,2},{4,5},{5,4},{6,7},{7,6},{8,9},{9,8},{10,11... | collective-permute-start | bytes 1572872 | tf_op jit(solution)/shard_map/ppermute | solution.py:32
  351.0 10.2 %collective-permute-start.29 = (bf16[512,256]{1,0:T(8,128)(2,1)S(1)}, bf16[512,256]{1,0:T(8,128)(2,1)S(1)}, u32[]{:S(2)}, u32[]{:S(2)}) collective-permute-start(bf16[512,256]{1,0:T(8,128)(2,1)S(1)} %dynamic-slice_convert_fusion), channel_id=1, source_target_pairs={{0,4},{4,0},{1,5},{5,1},{2,6},{6,2},{3,7},{7,3},{8,12},{12,8},{9,1... | collective-permute-start | bytes 786440 | tf_op jit(solution)/shard_map/ppermute | solution.py:32
  357.5 36.2 %collective-permute-start.33 = (bf16[128,2048]{1,0:T(8,128)(2,1)}, bf16[128,2048]{1,0:T(8,128)(2,1)}, u32[]{:S(2)}, u32[]{:S(2)}) collective-permute-start(bf16[128,2048]{1,0:T(8,128)(2,1)} %add_convert_fusion.3), channel_id=1, source_target_pairs={{0,2},{2,0},{1,3},{3,1},{4,6},{6,4},{5,7},{7,5},{8,10},{10,8},{9,1... | collective-permute-start | bytes 1572872 | tf_op jit(solution)/shard_map/ppermute | solution.py:32
  362.0 9.5 %collective-permute-start.30 = (bf16[256,256]{1,0:T(8,128)(2,1)}, bf16[256,256]{1,0:T(8,128)(2,1)}, u32[]{:S(2)}, u32[]{:S(2)}) collective-permute-start(bf16[256,256]{1,0:T(8,128)(2,1)} %pad_maximum_fusion.20), channel_id=1, source_target_pairs={{0,1},{1,0},{2,3},{3,2},{4,5},{5,4},{6,7},{7,6},{8,9},{9,8},{10,11... | collective-permute-start | bytes 393224 | tf_op jit(solution)/shard_map/ppermute | solution.py:32
  362.0 27.7 %collective-permute-start.37 = (bf16[1024,512]{1,0:T(8,128)(2,1)}, bf16[1024,512]{1,0:T(8,128)(2,1)}, u32[]{:S(2)}, u32[]{:S(2)}) collective-permute-start(bf16[1024,512]{1,0:T(8,128)(2,1)} %reduce-scatter.4.cloned.1.call-done), channel_id=1, source_target_pairs={{0,16},{16,0},{1,17},{17,1},{2,18},{18,2},{3,19},{19,3},{4,20},{20... | collective-permute-start | bytes 3145736 | tf_op jit(solution)/shard_map/ppermute | solution.py:32
  372.3 11.8 %collective-permute-start.34 = (bf16[128,256]{1,0:T(8,128)(2,1)S(1)}, bf16[128,256]{1,0:T(8,128)(2,1)}, u32[]{:S(2)}, u32[]{:S(2)}) collective-permute-start(bf16[128,256]{1,0:T(8,128)(2,1)S(1)} %add_convert_fusion.11), channel_id=1, source_target_pairs={{0,2},{2,0},{1,3},{3,1},{4,6},{6,4},{5,7},{7,5},{8,10},{10,8},{9,1... | collective-permute-start | bytes 196616 | tf_op jit(solution)/shard_map/ppermute | solution.py:32
  386.8 14.9 %collective-permute-start.36 = (bf16[128,2048]{1,0:T(8,128)(2,1)}, bf16[128,2048]{1,0:T(8,128)(2,1)S(1)}, u32[]{:S(2)}, u32[]{:S(2)}) collective-permute-start(bf16[128,2048]{1,0:T(8,128)(2,1)} %get-tuple-element.203), channel_id=1, source_target_pairs={{0,1},{1,0},{2,3},{3,2},{4,5},{5,4},{6,7},{7,6},{8,9},{9,8},{10,11... | collective-permute-start | bytes 1572872 | tf_op jit(solution)/shard_map/ppermute | solution.py:32
  387.5 48.3 %collective-permute-start.41 = (bf16[128,2048]{1,0:T(8,128)(2,1)}, bf16[128,2048]{1,0:T(8,128)(2,1)}, u32[]{:S(2)}, u32[]{:S(2)}) collective-permute-start(bf16[128,2048]{1,0:T(8,128)(2,1)} %get-tuple-element.202), channel_id=1, source_target_pairs={{0,1},{1,0},{2,3},{3,2},{4,5},{5,4},{6,7},{7,6},{8,9},{9,8},{10,11... | collective-permute-start | bytes 1572872 | tf_op jit(solution)/shard_map/ppermute | solution.py:32
  413.1 11.2 %collective-permute-start.40 = (bf16[288,512]{1,0:T(8,128)(2,1)}, bf16[288,512]{1,0:T(8,128)(2,1)}, u32[]{:S(2)}, u32[]{:S(2)}) collective-permute-start(bf16[288,512]{1,0:T(8,128)(2,1)} %pad_maximum_fusion.14), channel_id=1, source_target_pairs={{0,12},{4,8},{8,4},{12,0},{1,13},{5,9},{9,5},{13,1},{2,14},{6,10},... | collective-permute-start | bytes 884744 | tf_op jit(solution)/shard_map/ppermute | solution.py:84
  415.0 17.7 %collective-permute-start.39 = (bf16[288,512]{1,0:T(8,128)(2,1)}, bf16[288,512]{1,0:T(8,128)(2,1)}, u32[]{:S(2)}, u32[]{:S(2)}) collective-permute-start(bf16[288,512]{1,0:T(8,128)(2,1)} %pad_maximum_fusion.13), channel_id=1, source_target_pairs={{0,8},{4,12},{8,0},{12,4},{1,9},{5,13},{9,1},{13,5},{2,10},{6,14},... | collective-permute-start | bytes 884744 | tf_op jit(solution)/shard_map/ppermute | solution.py:84
  417.3 16.4 %collective-permute-start.38 = (bf16[288,512]{1,0:T(8,128)(2,1)}, bf16[288,512]{1,0:T(8,128)(2,1)}, u32[]{:S(2)}, u32[]{:S(2)}) collective-permute-start(bf16[288,512]{1,0:T(8,128)(2,1)} %pad_maximum_fusion.12), channel_id=1, source_target_pairs={{0,4},{4,0},{8,12},{12,8},{1,5},{5,1},{9,13},{13,9},{2,6},{6,2},{1... | collective-permute-start | bytes 884744 | tf_op jit(solution)/shard_map/ppermute | solution.py:84
  418.2 24.5 %collective-permute-start.42 = (bf16[128,2048]{1,0:T(8,128)(2,1)S(1)}, bf16[128,2048]{1,0:T(8,128)(2,1)}, u32[]{:S(2)}, u32[]{:S(2)}) collective-permute-start(bf16[128,2048]{1,0:T(8,128)(2,1)S(1)} %add_convert_fusion.1), channel_id=1, source_target_pairs={{0,2},{2,0},{1,3},{3,1},{4,6},{6,4},{5,7},{7,5},{8,10},{10,8},{9,1... | collective-permute-start | bytes 1572872 | tf_op jit(solution)/shard_map/ppermute | solution.py:32
  424.3 40.2 %collective-permute-start.49 = (bf16[512,1024]{1,0:T(8,128)(2,1)}, bf16[512,1024]{1,0:T(8,128)(2,1)}, u32[]{:S(2)}, u32[]{:S(2)}) collective-permute-start(bf16[512,1024]{1,0:T(8,128)(2,1)} %reduce-scatter.6.cloned.1.call-done), channel_id=1, source_target_pairs={{0,16},{16,0},{1,17},{17,1},{2,18},{18,2},{3,19},{19,3},{4,20},{20... | collective-permute-start | bytes 3145736 | tf_op jit(solution)/shard_map/ppermute | solution.py:32
  448.9 9.8 %collective-permute-start.46 = (bf16[160,512]{1,0:T(8,128)(2,1)S(1)}, bf16[160,512]{1,0:T(8,128)(2,1)S(1)}, u32[]{:S(2)}, u32[]{:S(2)}) collective-permute-start(bf16[160,512]{1,0:T(8,128)(2,1)S(1)} %add_convert_fusion.9), channel_id=1, source_target_pairs={{0,2},{2,0},{1,3},{3,1},{4,6},{6,4},{5,7},{7,5},{8,10},{10,8},{9,1... | collective-permute-start | bytes 491528 | tf_op jit(solution)/shard_map/ppermute | solution.py:32
  (82 other events, 768.6 us)
Sparse Core Ops, SparseCore 0:
  11.7 51.2 all-gather.3
  65.4 68.0 all-gather.5
  136.0 54.3 all-gather.7
  266.6 51.7 reduce-scatter.3
  321.5 61.7 reduce-scatter.5
  401.8 52.9 reduce-scatter.7

commit v4 on v3

--- a/solution.py
+++ b/solution.py
@@ -156,21 +156,6 @@
         slot = lambda r: ((r % 2) ^ self.rx) * self.rows_y + (self.ry - r // 2) % self.rows_y
         return jnp.concatenate(
             [lax.dynamic_slice_in_dim(got, slot(r) * w, w, 1) for r in range(self.rows)], axis=1
-        )
-
-    def to_home(self, a):
-        n, w = a.shape[0], a.shape[1] // self.rows
-        lanes = lambda x: jnp.concatenate(
-            [lax.dynamic_slice_in_dim(a, (2 * y + x) * w, w, 1) for y in range(self.rows_y)], axis=1
-        )
-        got = jnp.concatenate([lanes(self.rx), swap(lanes(1 - self.rx), "rx")], axis=0)
-        cut = lambda y: lax.dynamic_slice_in_dim(got, y * w, w, 1)
-        out = [cut(self.ry)]
-        out += [row_send(cut((self.ry + j) % self.rows_y), 2 * j, self.rows) for j in range(1, self.rows_y)]
-        out = jnp.concatenate(out, axis=0)
-        slot = lambda r: (self.ry - r // 2) % self.rows_y * 2 + ((r % 2) ^ self.rx)
-        return jnp.concatenate(
-            [lax.dynamic_slice_in_dim(out, slot(r) * n, n, 0) for r in range(self.rows)], axis=0
         )
 
     def by_lanes(self, got, lo, hi):
@@ -436,11 +421,45 @@
     return (v - mean) * inv_std, inv_std
 
 
-def norm_back(e, centred, inv_std, gain):
-    c = e * gain
-    m1 = jnp.mean(c, axis=1, keepdims=True)
-    m2 = jnp.mean(c * centred, axis=1, keepdims=True)
-    return (c - m1 - centred * m2) * inv_std
+def norm_back(part, near, far, base, centred, inv_std, gain, kv=None, weight=None):
+    t, width = near.shape
+    more = () if kv is None else (kv, weight)
+
+    def body(p_ref, n_ref, f_ref, b_ref, c_ref, i_ref, g_ref, *refs):
+        e = p_ref[...].astype(f32) + n_ref[...].astype(f32) + f_ref[...].astype(f32)
+        if more:
+            e = e + dot_nt(refs[0][...], refs[1][...])
+        grad_ref, low_ref, sum_ref = refs[-3:]
+        centre = c_ref[...]
+        c = e * g_ref[...]
+        m1 = jnp.sum(c, axis=1, keepdims=True) * (1.0 / width)
+        m2 = jnp.sum(c * centre, axis=1, keepdims=True) * (1.0 / width)
+        grad = b_ref[...].astype(f32) + (c - m1 - centre * m2) * i_ref[...]
+        low = grad.astype(bf16)
+        grad_ref[...] = grad
+        low_ref[...] = low
+        total = lambda a: jnp.sum(a, axis=0, keepdims=True)
+        sums = [total(e * centre), total(e), total(low.astype(f32)), jnp.zeros((5, width), f32)]
+        sum_ref[...] = jnp.concatenate(sums, axis=0)
+
+    whole = lambda a: pl.BlockSpec(a.shape, lambda i: (0, 0))
+    args = (part, near, far, base, centred, inv_std, gain, *more)
+    shapes = [
+        jax.ShapeDtypeStruct((t, width), f32),
+        jax.ShapeDtypeStruct((t, width), bf16),
+        jax.ShapeDtypeStruct((8, width), f32),
+    ]
+    return pl.pallas_call(
+        body,
+        grid=(1,),
+        in_specs=[pl.BlockSpec((t, width), lambda i: (0, 0))] + [whole(a) for a in args[1:]],
+        out_specs=[whole(a) for a in shapes],
+        out_shape=shapes,
+        compiler_params=pltpu.CompilerParams(
+            dimension_semantics=("arbitrary",), vmem_limit_bytes=32 * 1024 * 1024
+        ),
+        cost_estimate=pl.CostEstimate(flops=20 * t * width, bytes_accessed=20 * t * width, transcendentals=0),
+    )(*args)
 
 
 gelu_a = math.sqrt(2.0 / math.pi)
@@ -545,9 +564,9 @@
     near, far, down_part, up_part, activated = tie(near, far, down_part, up_part, activated)
     down_part = scatter_row(down_part, 1)
     up_part = scatter_row(up_part, 0)
-    grad_two = line_total(part, near, far)
-    grad_hidden = own_grad.astype(f32) + norm_back(grad_two, centred_two, inv_two, gain_two)
-    grad_branch = grad_hidden.astype(bf16)
+    grad_hidden, grad_branch, sums_two = norm_back(
+        part, near, far, own_grad, centred_two, inv_two, gain_two
+    )
     far, near = line_first(grad_branch)
     far, near, activated = tie(far, near, activated)
     block_branch = line_second(grad_branch, far, near)
@@ -570,36 +589,25 @@
     qo_part = jnp.concatenate(parts, axis=1)
     cut = lambda k: kv_grad[k * t : (k + 1) * t]
     got = swap(jnp.concatenate([cut(1), cut(3)], axis=0), "cl")
-    got, final_part = tie(got, final_part)
+    got, final_part, qo_part = tie(got, final_part, qo_part)
     kv_own = add(add(cut(0), got[:t]), swap(add(cut(2), got[t:]), "ch"))
     final_end, final_near = line_scatter_first(final_part)
-    grad_w_down = at.both_cores(down_part, 0)
+    near, far, kv_own, up_part = tie(near, far, kv_own, up_part)
+    qo_part = lax.psum_scatter(qo_part, ("ry", "rx", "dp"), scatter_dimension=0, tiled=True)
+    unused, grad_own, sums_one = norm_back(
+        part, near, far, grad_hidden, centred_one, inv_one, gain_one, kv_own, qkv_weight[:, hidden : hidden + 2 * head]
+    )
+
     kv_part = dot_tn(kv_own, normed_one).astype(bf16)
     kv_far = swap(lax.dynamic_slice_in_dim(kv_part, (1 - at.dp) * head, head, 0), "dp")
     kv_part = add(half_of(kv_part, 0), kv_far)
-    near, far, kv_own, kv_part, up_part, qo_part, final_end, grad_w_down = tie(
-        near, far, kv_own, kv_part, up_part, qo_part, final_end, grad_w_down
-    )
-    final_far = line_scatter_second(final_part, final_end)
-    qo_part = lax.psum_scatter(qo_part, ("ry", "rx", "dp"), scatter_dimension=0, tiled=True)
-    grad_one = line_total(part, near, far) + dot_nt(kv_own, qkv_weight[:, hidden:])
-    grad_own = grad_hidden + norm_back(grad_one, centred_one, inv_one, gain_one)
 
     sums = lambda a: jnp.sum(a.astype(f32), axis=0)
     tiled = lambda a: jnp.tile(a.reshape(-1, row_width), (1, rows))
     place = lambda a: lax.dynamic_update_slice_in_dim(jnp.zeros((4 * a.shape[0],), f32), a, col * a.shape[0], 0)
-    vectors = jnp.stack(
-        [
-            sums(grad_one * centred_one),
-            sums(grad_one),
-            sums(grad_two * centred_two),
-            sums(grad_two),
-            sums(grad_branch),
-            sums(own_grad),
-        ]
-    )
     parts = [
-        vectors,
+        sums_two[:3],
+        sums(own_grad)[None],
         tiled(jnp.pad(sums(kv_own[:, head:]), (0, row_width - head))),
         tiled(place(sums(grad_query))),
         tiled(place(sums(grad_upper))),
@@ -608,29 +616,36 @@
     parts.append(jnp.zeros((-n % 16, width), f32))
     packed = jnp.concatenate(parts).astype(bf16)
     n = packed.shape[0]
-    packed = jnp.concatenate([packed, kv_part], axis=0)
-    got = at.exchange(lanes_of(packed, row_width), lanes_of(grad_own.astype(bf16), row_width))
+    late = jnp.pad(sums_one, ((0, 8), (0, 0))).astype(bf16)
+    grad_own, final_end, down_part = tie(grad_own, final_end, down_part)
+    final_far = line_scatter_second(final_part, final_end)
+    grad_w_down = at.both_cores(down_part, 0)
+    got = at.exchange(*(lanes_of(a, row_width) for a in (packed, late, kv_part, grad_own)))
+    n = n + 16
     total = sum(g[: n + head].astype(f32) for g in got)
     grad_tokens = at.by_rows(got, n + head, n + head + t).astype(f32)
     total, final_near, final_far = tie(total, final_near, final_far)
     final = hidden_one + down_bias + line_total(final_part, final_near, final_far)
-    output = at.to_home(final.astype(bf16))
-    for axis in ("cl", "ch"):
-        total = total.astype(bf16)
-        total = total.astype(f32) + swap(total, axis).astype(f32)
+    output = at.by_rows(at.exchange(lanes_of(final.astype(bf16), row_width)), 0, t)
+    total = total.astype(bf16)
+    both = lax.ppermute(total, ("ch", "cl"), [(0, 3), (3, 0), (1, 2), (2, 1)])
+    sides = [total, swap(total, "ch"), swap(total, "cl"), both]
+    lower = (sides[0].astype(f32) + sides[1].astype(f32)) + (sides[2].astype(f32) + sides[3].astype(f32))
+    total = lower
     total = gather_axis(total.astype(bf16), "dp").astype(f32)
     grad_w_keyval = total[:, n:].reshape(2 * head, row_width).T
     total = total[0, :n] + total[1, :n]
     qo_part = at.both_cores(qo_part, 0)
     grad_w_query, grad_w_out = qo_part[:, :hidden], qo_part[:, hidden:].T
     grad_w_up = at.both_cores(up_part, 1)
-    grad_ln1_gain, grad_ln1_bias, grad_ln2_gain, grad_ln2_bias, grad_b_out, grad_b_down = total[:6]
-    grad_b_value = total[6, :head]
+    grad_ln2_gain, grad_ln2_bias, grad_b_out, grad_b_down = total[:4]
+    grad_ln1_gain, grad_ln1_bias = total[n - 16], total[n - 15]
+    grad_b_value = total[4, :head]
     of_col = lambda first, n: lax.dynamic_slice_in_dim(
         total[first : first + 4 * n // row_width].reshape(-1), col * n, n, 0
     )
-    grad_b_query = of_col(7, hidden)
-    grad_b_up = of_col(7 + 4 * hidden // row_width, b_up.shape[0])
+    grad_b_query = of_col(5, hidden)
+    grad_b_up = of_col(5 + 4 * hidden // row_width, b_up.shape[0])
     return (
         output,
         grad_tokens,

time: 490 us -> 468 us (0.955)
  waiting for transfers between devices: 230 us -> 214 us
  other arithmetic: 50 us -> 36.4 us
  Pallas kernels: 55.3 us -> 61.5 us
  starting transfers between devices: 58.9 us -> 64.1 us
    ppermute x38 -> x37, waiting for transfers between devices: 183 us -> 170 us  [swap(): return lax.ppermute(a, axis, [(0, 1), (1, 0)])]
    unnamed x182 -> x164, local copies, waits for them, and re-layouts: 25.5 us -> 34.4 us
    pallas_call x0 -> x2, Pallas kernels: none -> 6.18 us  [norm_back(): pl.pallas_call(body, grid=(1,), in_specs=[pl.BlockSpec((t, width), lambda...]
    reduce_sum x5 -> x4, other arithmetic: 6.64 us -> 0.62 us  [per_device(): sums = lambda a: jnp.sum(a.astype(f32), axis=0)]
    ppermute x12 -> x14, waiting for transfers between devices: 47.3 us -> 43.3 us  [row_send(): return lax.ppermute(a, ('ry', 'rx'), pairs)]
    dot_general x3 -> x2, matrix products: 10 us -> 6.18 us  [dot_nt(): lax.dot_general(a, b, (((1,), (1,)), ((), ())), preferred_element_type=f32)]
    ppermute x12 -> x14, starting transfers between devices: 15.2 us -> 18.2 us  [row_send(): return lax.ppermute(a, ('ry', 'rx'), pairs)]
    ppermute x38 -> x37, starting transfers between devices: 43.2 us -> 43.7 us  [swap(): return lax.ppermute(a, axis, [(0, 1), (1, 0)])]
  transfers between devices with their start and end apart: 56 -> 58, of which waited for: 32 -> 31; matrix products, arithmetic and copies ran while one was open for 19% -> 17% of each run, Pallas kernels for 8% -> 10%
where the time goes in v4:
time: 468 us; the launch traced here: 466 us
  waiting for transfers between devices  214 us (46%)
  starting transfers between devices  64.1 us (14%)
  Pallas kernels  61.5 us (13%)
  local copies, waits for them, and re-layouts  52.6 us (11%)
  other arithmetic  36.4 us (8%)
  matrix products  21.9 us (5%)
  between operations  15.8 us (3%)
    ppermute x37, waiting for transfers between devices, swap(): return lax.ppermute(a, axis, [(0, 1), (1, 0)])  170 us
    ppermute x37, starting transfers between devices, swap(): return lax.ppermute(a, axis, [(0, 1), (1, 0)])  43.7 us
    ppermute x14, waiting for transfers between devices, row_send(): return lax.ppermute(a, ('ry', 'rx'), pairs)  43.3 us
    unnamed x164, local copies, waits for them, and re-layouts  34.4 us
    ppermute x14, starting transfers between devices, row_send(): return lax.ppermute(a, ('ry', 'rx'), pairs)  18.2 us
    pallas_call x3, Pallas kernels, multiply(): pl.pallas_call(body, grid=(steps,), in_specs=specs, out_specs=out_spec, o...  16.3 us
    pallas_call x4, Pallas kernels, outer(): pl.pallas_call(body, grid_spec=pltpu.PrefetchScalarGridSpec(num_scalar_pr...  14.7 us
    pallas_call x1, Pallas kernels, feed_forward(): pl.pallas_call(body, grid=(n // tile,), in_specs=[pl.BlockSpec((m, k), la...  9.73 us
  transfers between devices with their start and end apart: 58, of which 31 were waited for; matrix products, arithmetic and copies ran while one was open for 17% of the time, Pallas kernels for 10%

profile of v4, /device:TPU:0, one launch (start us, length us, event | category | flops | bytes accessed | tf_op | source)
XLA Modules:
  0.0 466.4 jit_solution(10011645606922533260)
XLA Ops:
  14.6 4.0 collective-permute-start.2
  20.1 4.0 collective-permute-done.2
  24.1 3.3 collective-permute-done.1
  40.1 17.5 %collective-permute-done.3 = bf16[128,2048]{1,0:T(8,128)(2,1)S(1)} collective-permute-done((bf16[128,2048]{1,0:T(8,128)(2,1)S(1)}, bf16[128,2048]{1,0:T(8,128)(2,1)S(1)}, u32[]{:S(2)}, u32[]{:S(2)}) %collective-permute-start.3) | collective-permute-done | bytes 524320 | tf_op jit(solution)/shard_map/ppermute | solution.py:32
  59.8 10.7 %collective-permute-done.5 = bf16[128,2048]{1,0:T(8,128)(2,1)} collective-permute-done((bf16[128,2048]{1,0:T(8,128)(2,1)S(1)}, bf16[128,2048]{1,0:T(8,128)(2,1)}, u32[]{:S(2)}, u32[]{:S(2)}) %collective-permute-start.5) | collective-permute-done | bytes 524320 | tf_op jit(solution)/shard_map/ppermute | solution.py:32
  70.5 2.7 pad_maximum_fusion.1
  73.3 3.2 collective-permute-start.11
  78.3 2.7 fusion.15
  84.5 2.9 fusion.12.q_ref
  87.4 6.6 %collective-permute-done.10 = bf16[512,256]{1,0:T(8,128)(2,1)S(1)} collective-permute-done((bf16[512,256]{1,0:T(8,128)(2,1)S(1)}, bf16[512,256]{1,0:T(8,128)(2,1)S(1)}, u32[]{:S(2)}, u32[]{:S(2)}) %collective-permute-start.10) | collective-permute-done | bytes 262176 | tf_op jit(solution)/shard_map/ppermute | solution.py:84
  94.0 4.5 collective-permute-done.9
  99.0 6.1 %shard_map.288 = (bf16[512,512]{1,0:T(8,128)(2,1)S(1)}, f32[4,1,512]{2,1,0:T(1,128)S(1)}) custom-call(s32[4,2]{1,0:T(4,128)S(1)} %pad_add_fusion.1.bounds, bf16[512,512]{1,0:T(8,128)(2,1)S(1)} %fusion.12.q_ref, bf16[2048,128]{1,0:T(8,128)(2,1)S(1)} %get-tuple-element.232.k_ref, bf16[2048,128]{1,0:T(8,128)(2,1)S(1)} %get-tuple-element.231.v_ref, ...), custom_call_target="tpu_custom_call" | custom-call | flops 2147483648 | bytes 4194304 | tf_op jit(solution)/shard_map/pallas_call | solution.py:372
  105.1 3.2 convolution_convert_fusion.3
  112.0 11.3 %collective-permute-done.14 = bf16[128,2048]{1,0:T(8,128)(2,1)S(1)} collective-permute-done((bf16[128,2048]{1,0:T(8,128)(2,1)S(1)}, bf16[128,2048]{1,0:T(8,128)(2,1)S(1)}, u32[]{:S(2)}, u32[]{:S(2)}) %collective-permute-start.14) | collective-permute-done | bytes 524320 | tf_op jit(solution)/shard_map/ppermute | solution.py:32
  126.0 29.7 %collective-permute-done.16 = bf16[128,2048]{1,0:T(8,128)(2,1)S(1)} collective-permute-done((bf16[128,2048]{1,0:T(8,128)(2,1)}, bf16[128,2048]{1,0:T(8,128)(2,1)S(1)}, u32[]{:S(2)}, u32[]{:S(2)}) %collective-permute-start.16) | collective-permute-done | bytes 524320 | tf_op jit(solution)/shard_map/ppermute | solution.py:32
  163.5 3.4 copy-done.11
  166.9 5.3 %shard_map.289.g_ref = bf16[512,2048]{1,0:T(8,128)(2,1)S(1)} custom-call(bf16[512,2048]{1,0:T(8,128)(2,1)S(1)} %pad_maximum_fusion.2.x_ref.y_ref, bf16[2048,2048]{1,0:T(8,128)(2,1)S(1)} %copy-done.11), custom_call_target="tpu_custom_call" | custom-call | flops 4294967296 | bytes 12582912 | tf_op jit(solution)/shard_map/pallas_call | solution.py:194
  173.5 11.4 %collective-permute-done.17 = bf16[128,2048]{1,0:T(8,128)(2,1)} collective-permute-done((bf16[128,2048]{1,0:T(8,128)(2,1)S(1)}, bf16[128,2048]{1,0:T(8,128)(2,1)}, u32[]{:S(2)}, u32[]{:S(2)}) %collective-permute-start.17) | collective-permute-done | bytes 524320 | tf_op jit(solution)/shard_map/ppermute | solution.py:32
  185.3 13.0 %collective-permute-done.19 = bf16[128,2048]{1,0:T(8,128)(2,1)S(1)} collective-permute-done((bf16[128,2048]{1,0:T(8,128)(2,1)}, bf16[128,2048]{1,0:T(8,128)(2,1)S(1)}, u32[]{:S(2)}, u32[]{:S(2)}) %collective-permute-start.19) | collective-permute-done | bytes 524320 | tf_op jit(solution)/shard_map/ppermute | solution.py:32
  198.3 2.7 pad_maximum_fusion.3.x_ref
  202.6 3.4 copy-done.30
  207.6 9.7 %shard_map.290 = (bf16[512,2048]{1,0:T(8,128)(2,1)S(1)}, bf16[512,2048]{1,0:T(8,128)(2,1)S(1)}) custom-call(bf16[512,2048]{1,0:T(8,128)(2,1)S(1)} %copy-done.4, bf16[2048,2048]{1,0:T(8,128)(2,1)S(1)} %copy-done.30, f32[1,2048]{1,0:T(1,128)S(1)} %bitcast.68, bf16[512,2048]{1,0:T(8,128)(2,1)S(1)} %copy-done.32), custom_call_target="tpu_custom_call" | custom-call | flops 4294967296 | bytes 16777216 | tf_op jit(solution)/shard_map/pallas_call | solution.py:225
  217.3 5.3 %shard_map.291.p_ref = bf16[512,2048]{1,0:T(8,128)(2,1)S(1)} custom-call(bf16[512,2048]{1,0:T(8,128)(2,1)S(1)} %get-tuple-element.104.x_ref.y_ref, bf16[2048,2048]{1,0:T(8,128)(2,1)S(1)} %copy-done.30), custom_call_target="tpu_custom_call" | custom-call | flops 4294967296 | bytes 12582912 | tf_op jit(solution)/shard_map/pallas_call | solution.py:194
  225.2 2.7 shard_map.292
  227.9 4.4 shard_map.293
  232.3 3.4 collective-permute-done.21
  237.4 4.0 collective-permute-start.22
  241.3 7.4 %collective-permute-done.23.refs_0_ = bf16[1024,2048]{1,0:T(8,128)(2,1)S(1)} collective-permute-done((bf16[1024,2048]{1,0:T(8,128)(2,1)S(1)}, bf16[1024,2048]{1,0:T(8,128)(2,1)S(1)}, u32[]{:S(2)}, u32[]{:S(2)}) %collective-permute-start.23) | collective-permute-done | bytes 4194336 | tf_op jit(solution)/shard_map/ppermute | solution.py:32
  248.8 2.7 shard_map.294
  255.2 4.9 %shard_map.295 = bf16[2048,1024]{1,0:T(8,128)(2,1)S(1)} custom-call(s32[1]{0:T(128)} %bitcast.18.half_ref, bf16[512,2048]{1,0:T(8,128)(2,1)S(1)} %copy-done.6, bf16[512,2048]{1,0:T(8,128)(2,1)S(1)} %get-tuple-element.104.x_ref.y_ref, bf16[2048,1024]{1,0:T(8,128)(2,1)} %collective-permute-done.24.refs_0_), custom_call_target="tpu_custom_call" | custom-call | flops 1 | bytes 1 | tf_op jit(solution)/shard_map/pallas_call | solution.py:256
  268.3 2.8 shard_map.296
  272.1 2.9 collective-permute-start.26
  278.7 18.4 %collective-permute-done.25 = bf16[128,2048]{1,0:T(8,128)(2,1)} collective-permute-done((bf16[128,2048]{1,0:T(8,128)(2,1)}, bf16[128,2048]{1,0:T(8,128)(2,1)}, u32[]{:S(2)}, u32[]{:S(2)}) %collective-permute-start.25) | collective-permute-done | bytes 524320 | tf_op jit(solution)/shard_map/ppermute | solution.py:32
  301.4 9.7 %collective-permute-done.27 = bf16[128,2048]{1,0:T(8,128)(2,1)S(1)} collective-permute-done((bf16[128,2048]{1,0:T(8,128)(2,1)}, bf16[128,2048]{1,0:T(8,128)(2,1)S(1)}, u32[]{:S(2)}, u32[]{:S(2)}) %collective-permute-start.27) | collective-permute-done | bytes 524320 | tf_op jit(solution)/shard_map/ppermute | solution.py:32
  311.2 3.1 fusion.9.g_ref
  314.3 8.4 %shard_map.297 = (bf16[512,512]{1,0:T(8,128)(2,1)S(1)}, f32[2048,256]{1,0:T(8,128)S(1)}) custom-call(s32[4,2]{1,0:T(4,128)S(1)} %pad_add_fusion.1.bounds, bf16[512,512]{1,0:T(8,128)(2,1)S(1)} %copy-done.36, bf16[512,512]{1,0:T(8,128)(2,1)S(1)} %copy-done.34, bf16[512,512]{1,0:T(8,128)(2,1)S(1)} %fusion.9.g_ref, f32[4,1,512]{2,1,0:T(1,128)S(1)} %get-tuple-element.112.lse_ref, ...), custom_call_target="tpu_custom_call" | custom-call | flops 5368709120 | bytes 8388608 | tf_op jit(solution)/shard_map/pallas_call | solution.py:394
  324.7 3.0 convolution_convert_fusion.p_ref
  330.6 2.6 convolution_convert_fusion.1
  333.3 5.8 %shard_map.298 = bf16[512,2048]{1,0:T(8,128)(2,1)S(1)} custom-call(bf16[512,2048]{1,0:T(8,128)(2,1)S(1)} %copy-done.8, bf16[2048,2048]{1,0:T(8,128)(2,1)S(1)} %bitcast.65), custom_call_target="tpu_custom_call" | custom-call | flops 1 | bytes 1 | tf_op jit(solution)/shard_map/pallas_call | solution.py:194
  339.1 5.1 %collective-permute-done.28 = bf16[1024,256]{1,0:T(8,128)(2,1)S(1)} collective-permute-done((bf16[1024,256]{1,0:T(8,128)(2,1)S(1)}, bf16[1024,256]{1,0:T(8,128)(2,1)S(1)}, u32[]{:S(2)}, u32[]{:S(2)}) %collective-permute-start.28) | collective-permute-done | bytes 524320 | tf_op jit(solution)/shard_map/ppermute | solution.py:84
  345.6 6.9 %collective-permute-done.32 = bf16[128,2048]{1,0:T(8,128)(2,1)S(1)} collective-permute-done((bf16[128,2048]{1,0:T(8,128)(2,1)S(1)}, bf16[128,2048]{1,0:T(8,128)(2,1)S(1)}, u32[]{:S(2)}, u32[]{:S(2)}) %collective-permute-start.32) | collective-permute-done | bytes 524320 | tf_op jit(solution)/shard_map/ppermute | solution.py:32
  358.1 3.0 convolution_convert_fusion.2
  364.4 3.8 collective-permute-done.30
  374.1 6.4 %collective-permute-done.34 = bf16[128,256]{1,0:T(8,128)(2,1)} collective-permute-done((bf16[128,256]{1,0:T(8,128)(2,1)S(1)}, bf16[128,256]{1,0:T(8,128)(2,1)}, u32[]{:S(2)}, u32[]{:S(2)}) %collective-permute-start.34) | collective-permute-done | bytes 65568 | tf_op jit(solution)/shard_map/ppermute | solution.py:32
  386.6 3.3 shard_map.299
  399.6 6.3 %collective-permute-done.39 = bf16[304,512]{1,0:T(8,128)(2,1)S(1)} collective-permute-done((bf16[304,512]{1,0:T(8,128)(2,1)S(1)}, bf16[304,512]{1,0:T(8,128)(2,1)S(1)}, u32[]{:S(2)}, u32[]{:S(2)}) %collective-permute-start.39) | collective-permute-done | bytes 311328 | tf_op jit(solution)/shard_map/ppermute | solution.py:84
  407.1 7.0 %collective-permute-done.38 = bf16[304,512]{1,0:T(8,128)(2,1)S(1)} collective-permute-done((bf16[304,512]{1,0:T(8,128)(2,1)S(1)}, bf16[304,512]{1,0:T(8,128)(2,1)S(1)}, u32[]{:S(2)}, u32[]{:S(2)}) %collective-permute-start.38) | collective-permute-done | bytes 311328 | tf_op jit(solution)/shard_map/ppermute | solution.py:84
  415.5 14.9 %collective-permute-done.41 = bf16[128,2048]{1,0:T(8,128)(2,1)S(1)} collective-permute-done((bf16[128,2048]{1,0:T(8,128)(2,1)S(1)}, bf16[128,2048]{1,0:T(8,128)(2,1)S(1)}, u32[]{:S(2)}, u32[]{:S(2)}) %collective-permute-start.41) | collective-permute-done | bytes 524320 | tf_op jit(solution)/shard_map/ppermute | solution.py:32
  (381 shorter events, 141.1 us)
Async XLA Ops:
  7.2 71.1 %all-gather.4.cloned.1.call-start = ((), (), s32[]{:S(2)}) async-start(), calls=%async_computation.3 | async-start | bytes 5898240 | tf_op jit(solution)/shard_map/all_gather | solution.py:501
  10.5 153.0 %all-gather.6.cloned.1.call-start = ((), (), s32[]{:S(2)}) async-start(), calls=%async_computation.4 | async-start | bytes 9437184 | tf_op jit(solution)/shard_map/all_gather | solution.py:501
  11.7 189.3 %all-gather.8.cloned.1.call-start = ((), (), s32[]{:S(2)}) async-start(), calls=%async_computation.5 | async-start | bytes 9437184 | tf_op jit(solution)/shard_map/all_gather | solution.py:501
  14.2 342.8 %reduce-scatter.4.cloned.1.call-start = ((), (), s32[]{:S(2)}) async-start(), calls=%async_computation.6 | async-start | bytes 5242880 | tf_op jit(solution)/shard_map/reduce_scatter | solution.py:93
  19.1 10.2 %collective-permute-start = (bf16[144,512]{1,0:T(8,128)(2,1)S(1)}, bf16[144,512]{1,0:T(8,128)(2,1)S(1)}, u32[]{:S(2)}, u32[]{:S(2)}) collective-permute-start(bf16[144,512]{1,0:T(8,128)(2,1)S(1)} %get-tuple-element.295), channel_id=1, source_target_pairs={{0,4},{4,0},{8,12},{12,8},{1,5},{5,1},{9,13},{13,9},{2,6},{6,2},{1... | collective-permute-start | bytes 442376 | tf_op jit(solution)/shard_map/ppermute | solution.py:84
  31.9 25.7 %collective-permute-start.3 = (bf16[128,2048]{1,0:T(8,128)(2,1)S(1)}, bf16[128,2048]{1,0:T(8,128)(2,1)S(1)}, u32[]{:S(2)}, u32[]{:S(2)}) collective-permute-start(bf16[128,2048]{1,0:T(8,128)(2,1)S(1)} %get-tuple-element.234), channel_id=1, source_target_pairs={{0,2},{2,0},{1,3},{3,1},{4,6},{6,4},{5,7},{7,5},{8,10},{10,8},{9,1... | collective-permute-start | bytes 1572872 | tf_op jit(solution)/shard_map/ppermute | solution.py:32
  34.5 23.4 %collective-permute-start.4 = (bf16[128,2048]{1,0:T(8,128)(2,1)S(1)}, bf16[128,2048]{1,0:T(8,128)(2,1)S(1)}, u32[]{:S(2)}, u32[]{:S(2)}) collective-permute-start(bf16[128,2048]{1,0:T(8,128)(2,1)S(1)} %get-tuple-element.234), channel_id=1, source_target_pairs={{0,1},{1,0},{2,3},{3,2},{4,5},{5,4},{6,7},{7,6},{8,9},{9,8},{10,11... | collective-permute-start | bytes 1572872 | tf_op jit(solution)/shard_map/ppermute | solution.py:32
  38.3 21.1 %collective-permute-start.7 = (bf16[128,1024]{1,0:T(8,128)(2,1)S(1)}, bf16[128,1024]{1,0:T(8,128)(2,1)S(1)}, u32[]{:S(2)}, u32[]{:S(2)}) collective-permute-start(bf16[128,1024]{1,0:T(8,128)(2,1)S(1)} %get-tuple-element.263), channel_id=1, source_target_pairs={{0,4},{4,0},{1,5},{5,1},{2,6},{6,2},{3,7},{7,3},{8,12},{12,8},{9,1... | collective-permute-start | bytes 786440 | tf_op jit(solution)/shard_map/ppermute | solution.py:32
  57.8 12.7 %collective-permute-start.5 = (bf16[128,2048]{1,0:T(8,128)(2,1)S(1)}, bf16[128,2048]{1,0:T(8,128)(2,1)}, u32[]{:S(2)}, u32[]{:S(2)}) collective-permute-start(bf16[128,2048]{1,0:T(8,128)(2,1)S(1)} %collective-permute-done.3), channel_id=1, source_target_pairs={{0,1},{1,0},{2,3},{3,2},{4,5},{5,4},{6,7},{7,6},{8,9},{9,8},{10,11... | collective-permute-start | bytes 1572872 | tf_op jit(solution)/shard_map/ppermute | solution.py:32
  73.3 35.0 %collective-permute-start.11 = (bf16[128,2048]{1,0:T(8,128)(2,1)S(1)}, bf16[128,2048]{1,0:T(8,128)(2,1)}, u32[]{:S(2)}, u32[]{:S(2)}) collective-permute-start(bf16[128,2048]{1,0:T(8,128)(2,1)S(1)} %pad_maximum_fusion.7.b_ref), channel_id=1, source_target_pairs={{0,2},{2,0},{1,3},{3,1},{4,6},{6,4},{5,7},{7,5},{8,10},{10,8},{9,1... | collective-permute-start | bytes 1572872 | tf_op jit(solution)/shard_map/ppermute | solution.py:32
  76.5 31.8 %collective-permute-start.12 = (bf16[128,2048]{1,0:T(8,128)(2,1)S(1)}, bf16[128,2048]{1,0:T(8,128)(2,1)}, u32[]{:S(2)}, u32[]{:S(2)}) collective-permute-start(bf16[128,2048]{1,0:T(8,128)(2,1)S(1)} %pad_maximum_fusion.7.b_ref), channel_id=1, source_target_pairs={{0,1},{1,0},{2,3},{3,2},{4,5},{5,4},{6,7},{7,6},{8,9},{9,8},{10,11... | collective-permute-start | bytes 1572872 | tf_op jit(solution)/shard_map/ppermute | solution.py:32
  81.0 13.0 %collective-permute-start.10 = (bf16[512,256]{1,0:T(8,128)(2,1)S(1)}, bf16[512,256]{1,0:T(8,128)(2,1)S(1)}, u32[]{:S(2)}, u32[]{:S(2)}) collective-permute-start(bf16[512,256]{1,0:T(8,128)(2,1)S(1)} %fusion.15), channel_id=1, source_target_pairs={{0,12},{4,8},{8,4},{12,0},{1,13},{5,9},{9,5},{13,1},{2,14},{6,10},... | collective-permute-start | bytes 786440 | tf_op jit(solution)/shard_map/ppermute | solution.py:84
  81.8 16.7 %collective-permute-start.9 = (bf16[512,256]{1,0:T(8,128)(2,1)S(1)}, bf16[512,256]{1,0:T(8,128)(2,1)S(1)}, u32[]{:S(2)}, u32[]{:S(2)}) collective-permute-start(bf16[512,256]{1,0:T(8,128)(2,1)S(1)} %fusion.15), channel_id=1, source_target_pairs={{0,8},{4,12},{8,0},{12,4},{1,9},{5,13},{9,1},{13,5},{2,10},{6,14},... | collective-permute-start | bytes 786440 | tf_op jit(solution)/shard_map/ppermute | solution.py:84
  82.1 16.4 %collective-permute-start.8 = (bf16[512,256]{1,0:T(8,128)(2,1)S(1)}, bf16[512,256]{1,0:T(8,128)(2,1)S(1)}, u32[]{:S(2)}, u32[]{:S(2)}) collective-permute-start(bf16[512,256]{1,0:T(8,128)(2,1)S(1)} %fusion.15), channel_id=1, source_target_pairs={{0,4},{4,0},{8,12},{12,8},{1,5},{5,1},{9,13},{13,9},{2,6},{6,2},{1... | collective-permute-start | bytes 786440 | tf_op jit(solution)/shard_map/ppermute | solution.py:84
  108.4 14.9 %collective-permute-start.14 = (bf16[128,2048]{1,0:T(8,128)(2,1)S(1)}, bf16[128,2048]{1,0:T(8,128)(2,1)S(1)}, u32[]{:S(2)}, u32[]{:S(2)}) collective-permute-start(bf16[128,2048]{1,0:T(8,128)(2,1)S(1)} %get-tuple-element.211), channel_id=1, source_target_pairs={{0,1},{1,0},{2,3},{3,2},{4,5},{5,4},{6,7},{7,6},{8,9},{9,8},{10,11... | collective-permute-start | bytes 1572872 | tf_op jit(solution)/shard_map/ppermute | solution.py:32
  110.0 47.1 %collective-permute-start.13 = (bf16[128,2048]{1,0:T(8,128)(2,1)S(1)}, bf16[128,2048]{1,0:T(8,128)(2,1)S(1)}, u32[]{:S(2)}, u32[]{:S(2)}) collective-permute-start(bf16[128,2048]{1,0:T(8,128)(2,1)S(1)} %get-tuple-element.212), channel_id=1, source_target_pairs={{0,1},{1,0},{2,3},{3,2},{4,5},{5,4},{6,7},{7,6},{8,9},{9,8},{10,11... | collective-permute-start | bytes 1572872 | tf_op jit(solution)/shard_map/ppermute | solution.py:32
  110.5 45.1 %collective-permute-start.16 = (bf16[128,2048]{1,0:T(8,128)(2,1)}, bf16[128,2048]{1,0:T(8,128)(2,1)S(1)}, u32[]{:S(2)}, u32[]{:S(2)}) collective-permute-start(bf16[128,2048]{1,0:T(8,128)(2,1)} %collective-permute-done.11), channel_id=1, source_target_pairs={{0,1},{1,0},{2,3},{3,2},{4,5},{5,4},{6,7},{7,6},{8,9},{9,8},{10,11... | collective-permute-start | bytes 1572872 | tf_op jit(solution)/shard_map/ppermute | solution.py:32
  123.5 33.6 %collective-permute-start.15 = (bf16[128,2048]{1,0:T(8,128)(2,1)S(1)}, bf16[128,2048]{1,0:T(8,128)(2,1)S(1)}, u32[]{:S(2)}, u32[]{:S(2)}) collective-permute-start(bf16[128,2048]{1,0:T(8,128)(2,1)S(1)} %add_convert_fusion.6), channel_id=1, source_target_pairs={{0,2},{2,0},{1,3},{3,1},{4,6},{6,4},{5,7},{7,5},{8,10},{10,8},{9,1... | collective-permute-start | bytes 1572872 | tf_op jit(solution)/shard_map/ppermute | solution.py:32
  159.9 25.0 %collective-permute-start.17 = (bf16[128,2048]{1,0:T(8,128)(2,1)S(1)}, bf16[128,2048]{1,0:T(8,128)(2,1)}, u32[]{:S(2)}, u32[]{:S(2)}) collective-permute-start(bf16[128,2048]{1,0:T(8,128)(2,1)S(1)} %get-tuple-element.196), channel_id=1, source_target_pairs={{0,2},{2,0},{1,3},{3,1},{4,6},{6,4},{5,7},{7,5},{8,10},{10,8},{9,1... | collective-permute-start | bytes 1572872 | tf_op jit(solution)/shard_map/ppermute | solution.py:32
  161.1 23.9 %collective-permute-start.18 = (bf16[128,2048]{1,0:T(8,128)(2,1)S(1)}, bf16[128,2048]{1,0:T(8,128)(2,1)}, u32[]{:S(2)}, u32[]{:S(2)}) collective-permute-start(bf16[128,2048]{1,0:T(8,128)(2,1)S(1)} %get-tuple-element.196), channel_id=1, source_target_pairs={{0,1},{1,0},{2,3},{3,2},{4,5},{5,4},{6,7},{7,6},{8,9},{9,8},{10,11... | collective-permute-start | bytes 1572872 | tf_op jit(solution)/shard_map/ppermute | solution.py:32
  185.0 13.3 %collective-permute-start.19 = (bf16[128,2048]{1,0:T(8,128)(2,1)}, bf16[128,2048]{1,0:T(8,128)(2,1)S(1)}, u32[]{:S(2)}, u32[]{:S(2)}) collective-permute-start(bf16[128,2048]{1,0:T(8,128)(2,1)} %collective-permute-done.17), channel_id=1, source_target_pairs={{0,1},{1,0},{2,3},{3,2},{4,5},{5,4},{6,7},{7,6},{8,9},{9,8},{10,11... | collective-permute-start | bytes 1572872 | tf_op jit(solution)/shard_map/ppermute | solution.py:32
  223.5 12.1 %collective-permute-start.21 = (bf16[128,2048]{1,0:T(8,128)(2,1)S(1)}, bf16[128,2048]{1,0:T(8,128)(2,1)S(1)}, u32[]{:S(2)}, u32[]{:S(2)}) collective-permute-start(bf16[128,2048]{1,0:T(8,128)(2,1)S(1)} %get-tuple-element.209), channel_id=1, source_target_pairs={{0,1},{1,0},{2,3},{3,2},{4,5},{5,4},{6,7},{7,6},{8,9},{9,8},{10,11... | collective-permute-start | bytes 1572872 | tf_op jit(solution)/shard_map/ppermute | solution.py:32
  235.6 13.1 %collective-permute-start.23 = (bf16[1024,2048]{1,0:T(8,128)(2,1)S(1)}, bf16[1024,2048]{1,0:T(8,128)(2,1)S(1)}, u32[]{:S(2)}, u32[]{:S(2)}) collective-permute-start(bf16[1024,2048]{1,0:T(8,128)(2,1)S(1)} %shard_map.292), channel_id=1, source_target_pairs={{0,16},{16,0},{1,17},{17,1},{2,18},{18,2},{3,19},{19,3},{4,20},{20... | collective-permute-start | bytes 12582920 | tf_op jit(solution)/shard_map/ppermute | solution.py:32
  235.6 17.9 %collective-permute-start.24 = (bf16[2048,1024]{1,0:T(8,128)(2,1)}, bf16[2048,1024]{1,0:T(8,128)(2,1)}, u32[]{:S(2)}, u32[]{:S(2)}) collective-permute-start(bf16[2048,1024]{1,0:T(8,128)(2,1)} %shard_map.293), channel_id=1, source_target_pairs={{0,16},{16,0},{1,17},{17,1},{2,18},{18,2},{3,19},{19,3},{4,20},{20... | collective-permute-start | bytes 12582920 | tf_op jit(solution)/shard_map/ppermute | solution.py:32
  236.2 26.0 %collective-permute-start.20 = (bf16[128,2048]{1,0:T(8,128)(2,1)}, bf16[128,2048]{1,0:T(8,128)(2,1)S(1)}, u32[]{:S(2)}, u32[]{:S(2)}) collective-permute-start(bf16[128,2048]{1,0:T(8,128)(2,1)} %get-tuple-element.210), channel_id=1, source_target_pairs={{0,1},{1,0},{2,3},{3,2},{4,5},{5,4},{6,7},{7,6},{8,9},{9,8},{10,11... | collective-permute-start | bytes 1572872 | tf_op jit(solution)/shard_map/ppermute | solution.py:32
  237.4 27.4 %collective-permute-start.22 = (bf16[128,2048]{1,0:T(8,128)(2,1)}, bf16[128,2048]{1,0:T(8,128)(2,1)}, u32[]{:S(2)}, u32[]{:S(2)}) collective-permute-start(bf16[128,2048]{1,0:T(8,128)(2,1)} %add_convert_fusion.4), channel_id=1, source_target_pairs={{0,2},{2,0},{1,3},{3,1},{4,6},{6,4},{5,7},{7,5},{8,10},{10,8},{9,1... | collective-permute-start | bytes 1572872 | tf_op jit(solution)/shard_map/ppermute | solution.py:32
  264.7 116.7 %reduce-scatter.6.cloned.1.call-start = ((), (), s32[]{:S(2)}) async-start(), calls=%async_computation.7 | async-start | bytes 5242880 | tf_op jit(solution)/shard_map/reduce_scatter | solution.py:93
  265.3 187.2 %reduce-scatter.8.cloned.1.call-start = ((), (), s32[]{:S(2)}) async-start(), calls=%async_computation.8 | async-start | bytes 4718592 | tf_op jit(solution)/shard_map/reduce_scatter | solution.py:596
  272.1 25.0 %collective-permute-start.25 = (bf16[128,2048]{1,0:T(8,128)(2,1)}, bf16[128,2048]{1,0:T(8,128)(2,1)}, u32[]{:S(2)}, u32[]{:S(2)}) collective-permute-start(bf16[128,2048]{1,0:T(8,128)(2,1)} %get-tuple-element.108), channel_id=1, source_target_pairs={{0,2},{2,0},{1,3},{3,1},{4,6},{6,4},{5,7},{7,5},{8,10},{10,8},{9,1... | collective-permute-start | bytes 1572872 | tf_op jit(solution)/shard_map/ppermute | solution.py:32
  272.1 25.2 %collective-permute-start.26 = (bf16[128,2048]{1,0:T(8,128)(2,1)}, bf16[128,2048]{1,0:T(8,128)(2,1)}, u32[]{:S(2)}, u32[]{:S(2)}) collective-permute-start(bf16[128,2048]{1,0:T(8,128)(2,1)} %get-tuple-element.108), channel_id=1, source_target_pairs={{0,1},{1,0},{2,3},{3,2},{4,5},{5,4},{6,7},{7,6},{8,9},{9,8},{10,11... | collective-permute-start | bytes 1572872 | tf_op jit(solution)/shard_map/ppermute | solution.py:32
  297.3 13.8 %collective-permute-start.27 = (bf16[128,2048]{1,0:T(8,128)(2,1)}, bf16[128,2048]{1,0:T(8,128)(2,1)S(1)}, u32[]{:S(2)}, u32[]{:S(2)}) collective-permute-start(bf16[128,2048]{1,0:T(8,128)(2,1)} %collective-permute-done.25), channel_id=1, source_target_pairs={{0,1},{1,0},{2,3},{3,2},{4,5},{5,4},{6,7},{7,6},{8,9},{9,8},{10,11... | collective-permute-start | bytes 1572872 | tf_op jit(solution)/shard_map/ppermute | solution.py:32
  323.1 21.1 %collective-permute-start.28 = (bf16[1024,256]{1,0:T(8,128)(2,1)S(1)}, bf16[1024,256]{1,0:T(8,128)(2,1)S(1)}, u32[]{:S(2)}, u32[]{:S(2)}) collective-permute-start(bf16[1024,256]{1,0:T(8,128)(2,1)S(1)} %get-tuple-element.216), channel_id=1, source_target_pairs={{0,8},{4,12},{8,0},{12,4},{1,9},{5,13},{9,1},{13,5},{2,10},{6,14},... | collective-permute-start | bytes 1572872 | tf_op jit(solution)/shard_map/ppermute | solution.py:84
  328.6 52.8 %collective-permute-start.31 = (bf16[128,2048]{1,0:T(8,128)(2,1)}, bf16[128,2048]{1,0:T(8,128)(2,1)}, u32[]{:S(2)}, u32[]{:S(2)}) collective-permute-start(bf16[128,2048]{1,0:T(8,128)(2,1)} %get-tuple-element.208), channel_id=1, source_target_pairs={{0,1},{1,0},{2,3},{3,2},{4,5},{5,4},{6,7},{7,6},{8,9},{9,8},{10,11... | collective-permute-start | bytes 1572872 | tf_op jit(solution)/shard_map/ppermute | solution.py:32
  328.8 23.7 %collective-permute-start.32 = (bf16[128,2048]{1,0:T(8,128)(2,1)S(1)}, bf16[128,2048]{1,0:T(8,128)(2,1)S(1)}, u32[]{:S(2)}, u32[]{:S(2)}) collective-permute-start(bf16[128,2048]{1,0:T(8,128)(2,1)S(1)} %get-tuple-element.207), channel_id=1, source_target_pairs={{0,1},{1,0},{2,3},{3,2},{4,5},{5,4},{6,7},{7,6},{8,9},{9,8},{10,11... | collective-permute-start | bytes 1572872 | tf_op jit(solution)/shard_map/ppermute | solution.py:32
  344.3 12.6 %collective-permute-start.29 = (bf16[512,256]{1,0:T(8,128)(2,1)S(1)}, bf16[512,256]{1,0:T(8,128)(2,1)S(1)}, u32[]{:S(2)}, u32[]{:S(2)}) collective-permute-start(bf16[512,256]{1,0:T(8,128)(2,1)S(1)} %dynamic-slice_convert_fusion), channel_id=1, source_target_pairs={{0,4},{4,0},{1,5},{5,1},{2,6},{6,2},{3,7},{7,3},{8,12},{12,8},{9,1... | collective-permute-start | bytes 786440 | tf_op jit(solution)/shard_map/ppermute | solution.py:32
  353.5 27.9 %collective-permute-start.33 = (bf16[128,2048]{1,0:T(8,128)(2,1)}, bf16[128,2048]{1,0:T(8,128)(2,1)}, u32[]{:S(2)}, u32[]{:S(2)}) collective-permute-start(bf16[128,2048]{1,0:T(8,128)(2,1)} %add_convert_fusion.3), channel_id=1, source_target_pairs={{0,2},{2,0},{1,3},{3,1},{4,6},{6,4},{5,7},{7,5},{8,10},{10,8},{9,1... | collective-permute-start | bytes 1572872 | tf_op jit(solution)/shard_map/ppermute | solution.py:32
  357.7 10.5 %collective-permute-start.30 = (bf16[256,256]{1,0:T(8,128)(2,1)}, bf16[256,256]{1,0:T(8,128)(2,1)}, u32[]{:S(2)}, u32[]{:S(2)}) collective-permute-start(bf16[256,256]{1,0:T(8,128)(2,1)} %pad_maximum_fusion.18), channel_id=1, source_target_pairs={{0,1},{1,0},{2,3},{3,2},{4,5},{5,4},{6,7},{7,6},{8,9},{9,8},{10,11... | collective-permute-start | bytes 393224 | tf_op jit(solution)/shard_map/ppermute | solution.py:32
  369.1 11.4 %collective-permute-start.34 = (bf16[128,256]{1,0:T(8,128)(2,1)S(1)}, bf16[128,256]{1,0:T(8,128)(2,1)}, u32[]{:S(2)}, u32[]{:S(2)}) collective-permute-start(bf16[128,256]{1,0:T(8,128)(2,1)S(1)} %add_convert_fusion.11), channel_id=1, source_target_pairs={{0,2},{2,0},{1,3},{3,1},{4,6},{6,4},{5,7},{7,5},{8,10},{10,8},{9,1... | collective-permute-start | bytes 196616 | tf_op jit(solution)/shard_map/ppermute | solution.py:32
  372.1 19.9 %collective-permute-start.36 = (bf16[128,2048]{1,0:T(8,128)(2,1)}, bf16[128,2048]{1,0:T(8,128)(2,1)}, u32[]{:S(2)}, u32[]{:S(2)}) collective-permute-start(bf16[128,2048]{1,0:T(8,128)(2,1)} %get-tuple-element.206), channel_id=1, source_target_pairs={{0,1},{1,0},{2,3},{3,2},{4,5},{5,4},{6,7},{7,6},{8,9},{9,8},{10,11... | collective-permute-start | bytes 1572872 | tf_op jit(solution)/shard_map/ppermute | solution.py:32
  372.7 42.8 %collective-permute-start.40 = (bf16[128,2048]{1,0:T(8,128)(2,1)}, bf16[128,2048]{1,0:T(8,128)(2,1)}, u32[]{:S(2)}, u32[]{:S(2)}) collective-permute-start(bf16[128,2048]{1,0:T(8,128)(2,1)} %get-tuple-element.205), channel_id=1, source_target_pairs={{0,1},{1,0},{2,3},{3,2},{4,5},{5,4},{6,7},{7,6},{8,9},{9,8},{10,11... | collective-permute-start | bytes 1572872 | tf_op jit(solution)/shard_map/ppermute | solution.py:32
  390.8 47.5 %collective-permute-start.50 = (bf16[512,1024]{1,0:T(8,128)(2,1)}, bf16[512,1024]{1,0:T(8,128)(2,1)}, u32[]{:S(2)}, u32[]{:S(2)}) collective-permute-start(bf16[512,1024]{1,0:T(8,128)(2,1)} %reduce-scatter.6.cloned.1.call-done), channel_id=1, source_target_pairs={{0,16},{16,0},{1,17},{17,1},{2,18},{18,2},{3,19},{19,3},{4,20},{20... | collective-permute-start | bytes 3145736 | tf_op jit(solution)/shard_map/ppermute | solution.py:32
  394.6 11.2 %collective-permute-start.39 = (bf16[304,512]{1,0:T(8,128)(2,1)S(1)}, bf16[304,512]{1,0:T(8,128)(2,1)S(1)}, u32[]{:S(2)}, u32[]{:S(2)}) collective-permute-start(bf16[304,512]{1,0:T(8,128)(2,1)S(1)} %pad_maximum_fusion.13), channel_id=1, source_target_pairs={{0,12},{4,8},{8,4},{12,0},{1,13},{5,9},{9,5},{13,1},{2,14},{6,10},... | collective-permute-start | bytes 933896 | tf_op jit(solution)/shard_map/ppermute | solution.py:84
  396.6 17.6 %collective-permute-start.38 = (bf16[304,512]{1,0:T(8,128)(2,1)S(1)}, bf16[304,512]{1,0:T(8,128)(2,1)S(1)}, u32[]{:S(2)}, u32[]{:S(2)}) collective-permute-start(bf16[304,512]{1,0:T(8,128)(2,1)S(1)} %pad_maximum_fusion.12), channel_id=1, source_target_pairs={{0,8},{4,12},{8,0},{12,4},{1,9},{5,13},{9,1},{13,5},{2,10},{6,14},... | collective-permute-start | bytes 933896 | tf_op jit(solution)/shard_map/ppermute | solution.py:84
  397.6 16.5 %collective-permute-start.37 = (bf16[304,512]{1,0:T(8,128)(2,1)S(1)}, bf16[304,512]{1,0:T(8,128)(2,1)S(1)}, u32[]{:S(2)}, u32[]{:S(2)}) collective-permute-start(bf16[304,512]{1,0:T(8,128)(2,1)S(1)} %pad_maximum_fusion.11), channel_id=1, source_target_pairs={{0,4},{4,0},{8,12},{12,8},{1,5},{5,1},{9,13},{13,9},{2,6},{6,2},{1... | collective-permute-start | bytes 933896 | tf_op jit(solution)/shard_map/ppermute | solution.py:84
  405.8 24.5 %collective-permute-start.41 = (bf16[128,2048]{1,0:T(8,128)(2,1)S(1)}, bf16[128,2048]{1,0:T(8,128)(2,1)S(1)}, u32[]{:S(2)}, u32[]{:S(2)}) collective-permute-start(bf16[128,2048]{1,0:T(8,128)(2,1)S(1)} %add_convert_fusion.1), channel_id=1, source_target_pairs={{0,2},{2,0},{1,3},{3,1},{4,6},{6,4},{5,7},{7,5},{8,10},{10,8},{9,1... | collective-permute-start | bytes 1572872 | tf_op jit(solution)/shard_map/ppermute | solution.py:32
  430.4 16.9 %collective-permute-start.47 = (bf16[176,512]{1,0:T(8,128)(2,1)S(1)}, bf16[176,512]{1,0:T(8,128)(2,1)S(1)}, u32[]{:S(2)}, u32[]{:S(2)}) collective-permute-start(bf16[176,512]{1,0:T(8,128)(2,1)S(1)} %convert_add_fusion.2), channel_id=1, source_target_pairs={{0,3},{3,0},{1,2},{2,1},{4,7},{7,4},{5,6},{6,5},{8,11},{11,8},{9,1... | collective-permute-start | bytes 540680 | tf_op jit(solution)/shard_map/ppermute | solution.py:631
  432.4 14.9 %collective-permute-start.46 = (bf16[176,512]{1,0:T(8,128)(2,1)S(1)}, bf16[176,512]{1,0:T(8,128)(2,1)S(1)}, u32[]{:S(2)}, u32[]{:S(2)}) collective-permute-start(bf16[176,512]{1,0:T(8,128)(2,1)S(1)} %convert_add_fusion.2), channel_id=1, source_target_pairs={{0,1},{1,0},{2,3},{3,2},{4,5},{5,4},{6,7},{7,6},{8,9},{9,8},{10,11... | collective-permute-start | bytes 540680 | tf_op jit(solution)/shard_map/ppermute | solution.py:32
  432.4 14.9 %collective-permute-start.45 = (bf16[176,512]{1,0:T(8,128)(2,1)S(1)}, bf16[176,512]{1,0:T(8,128)(2,1)S(1)}, u32[]{:S(2)}, u32[]{:S(2)}) collective-permute-start(bf16[176,512]{1,0:T(8,128)(2,1)S(1)} %convert_add_fusion.2), channel_id=1, source_target_pairs={{0,2},{2,0},{1,3},{3,1},{4,6},{6,4},{5,7},{7,5},{8,10},{10,8},{9,1... | collective-permute-start | bytes 540680 | tf_op jit(solution)/shard_map/ppermute | solution.py:32
  (74 other events, 524.6 us)
Sparse Core Ops, SparseCore 0:
  10.7 50.8 all-gather.3
  64.0 68.0 all-gather.5
  134.6 54.3 all-gather.7
  264.9 52.6 reduce-scatter.3
  321.3 58.9 reduce-scatter.5
  384.0 54.4 reduce-scatter.7

commit v5 on v4

--- a/solution.py
+++ b/solution.py
@@ -210,7 +210,7 @@
 
 def feed_forward(x, w, bias, grad_act):
     (m, k), n = x.shape, w.shape[1]
-    tile = min(256, n)
+    tile = min(512, n)
 
     def body(x_ref, w_ref, b_ref, g_ref, a_ref, u_ref):
         u = dot_nn(x_ref[...], w_ref[...]) + b_ref[...]
@@ -592,7 +592,7 @@
     got, final_part, qo_part = tie(got, final_part, qo_part)
     kv_own = add(add(cut(0), got[:t]), swap(add(cut(2), got[t:]), "ch"))
     final_end, final_near = line_scatter_first(final_part)
-    near, far, kv_own, up_part = tie(near, far, kv_own, up_part)
+    near, far, kv_own = tie(near, far, kv_own)
     qo_part = lax.psum_scatter(qo_part, ("ry", "rx", "dp"), scatter_dimension=0, tiled=True)
     unused, grad_own, sums_one = norm_back(
         part, near, far, grad_hidden, centred_one, inv_one, gain_one, kv_own, qkv_weight[:, hidden : hidden + 2 * head]
@@ -617,7 +617,7 @@
     packed = jnp.concatenate(parts).astype(bf16)
     n = packed.shape[0]
     late = jnp.pad(sums_one, ((0, 8), (0, 0))).astype(bf16)
-    grad_own, final_end, down_part = tie(grad_own, final_end, down_part)
+    grad_own, final_end, down_part, up_part = tie(grad_own, final_end, down_part, up_part)
     final_far = line_scatter_second(final_part, final_end)
     grad_w_down = at.both_cores(down_part, 0)
     got = at.exchange(*(lanes_of(a, row_width) for a in (packed, late, kv_part, grad_own)))

time: 468 us -> 475 us (1.015)
  starting transfers between devices: 64.1 us -> 57.3 us
  other arithmetic: 36.4 us -> 41.3 us
    ppermute x14, waiting for transfers between devices: 43.3 us -> 52 us  [row_send(): return lax.ppermute(a, ('ry', 'rx'), pairs)]
    ppermute x37, waiting for transfers between devices: 170 us -> 163 us  [swap(): return lax.ppermute(a, axis, [(0, 1), (1, 0)])]
    unnamed x164 -> x170, local copies, waits for them, and re-layouts: 34.4 us -> 34.5 us
  transfers between devices with their start and end apart: 58 -> 58, of which waited for: 31 -> 34; matrix products, arithmetic and copies ran while one was open for 17% -> 18% of each run, Pallas kernels for 10% -> 11%
where the time goes in v5:
time: 475 us; the launch traced here: 473 us
  waiting for transfers between devices  216 us (45%)
  Pallas kernels  65.1 us (14%)
  starting transfers between devices  57.3 us (12%)
  local copies, waits for them, and re-layouts  56.3 us (12%)
  other arithmetic  41.3 us (9%)
  matrix products  21.9 us (5%)
  between operations  15.8 us (3%)
    ppermute x37, waiting for transfers between devices, swap(): return lax.ppermute(a, axis, [(0, 1), (1, 0)])  163 us
    ppermute x14, waiting for transfers between devices, row_send(): return lax.ppermute(a, ('ry', 'rx'), pairs)  52 us
    ppermute x37, starting transfers between devices, swap(): return lax.ppermute(a, axis, [(0, 1), (1, 0)])  39.7 us
    unnamed x170, local copies, waits for them, and re-layouts  34.5 us
    pallas_call x3, Pallas kernels, multiply(): pl.pallas_call(body, grid=(steps,), in_specs=specs, out_specs=out_spec, o...  16.4 us
    ppermute x14, starting transfers between devices, row_send(): return lax.ppermute(a, ('ry', 'rx'), pairs)  15.9 us
    pallas_call x4, Pallas kernels, outer(): pl.pallas_call(body, grid_spec=pltpu.PrefetchScalarGridSpec(num_scalar_pr...  14.7 us
    pallas_call x1, Pallas kernels, backward(): pl.pallas_call(body, grid_spec=pltpu.PrefetchScalarGridSpec(num_scalar_pr...  11.3 us
  transfers between devices with their start and end apart: 58, of which 34 were waited for; matrix products, arithmetic and copies ran while one was open for 18% of the time, Pallas kernels for 11%

profile of v5, /device:TPU:0, one launch (start us, length us, event | category | flops | bytes accessed | tf_op | source)
XLA Modules:
  0.0 473.5 jit_solution(15113468144864372433)
XLA Ops:
  14.6 4.0 collective-permute-start.2
  20.1 4.0 collective-permute-done.2
  24.1 3.3 collective-permute-done.1
  40.1 18.1 %collective-permute-done.3 = bf16[128,2048]{1,0:T(8,128)(2,1)S(1)} collective-permute-done((bf16[128,2048]{1,0:T(8,128)(2,1)S(1)}, bf16[128,2048]{1,0:T(8,128)(2,1)S(1)}, u32[]{:S(2)}, u32[]{:S(2)}) %collective-permute-start.3) | collective-permute-done | bytes 524320 | tf_op jit(solution)/shard_map/ppermute | solution.py:32
  60.4 10.7 %collective-permute-done.5 = bf16[128,2048]{1,0:T(8,128)(2,1)} collective-permute-done((bf16[128,2048]{1,0:T(8,128)(2,1)S(1)}, bf16[128,2048]{1,0:T(8,128)(2,1)}, u32[]{:S(2)}, u32[]{:S(2)}) %collective-permute-start.5) | collective-permute-done | bytes 524320 | tf_op jit(solution)/shard_map/ppermute | solution.py:32
  71.1 2.7 pad_maximum_fusion.1
  73.8 3.3 collective-permute-start.11
  78.9 2.7 fusion.15
  85.2 2.9 fusion.12.q_ref
  88.0 6.0 %collective-permute-done.10 = bf16[512,256]{1,0:T(8,128)(2,1)S(1)} collective-permute-done((bf16[512,256]{1,0:T(8,128)(2,1)S(1)}, bf16[512,256]{1,0:T(8,128)(2,1)S(1)}, u32[]{:S(2)}, u32[]{:S(2)}) %collective-permute-start.10) | collective-permute-done | bytes 262176 | tf_op jit(solution)/shard_map/ppermute | solution.py:84
  94.0 4.5 collective-permute-done.9
  99.0 8.1 %shard_map.288 = (bf16[512,512]{1,0:T(8,128)(2,1)S(1)}, f32[4,1,512]{2,1,0:T(1,128)S(1)}) custom-call(s32[4,2]{1,0:T(4,128)S(1)} %pad_add_fusion.1.bounds, bf16[512,512]{1,0:T(8,128)(2,1)S(1)} %fusion.12.q_ref, bf16[2048,128]{1,0:T(8,128)(2,1)S(1)} %get-tuple-element.232.k_ref, bf16[2048,128]{1,0:T(8,128)(2,1)S(1)} %get-tuple-element.231.v_ref, ...), custom_call_target="tpu_custom_call" | custom-call | flops 2147483648 | bytes 4194304 | tf_op jit(solution)/shard_map/pallas_call | solution.py:372
  107.1 3.2 convolution_convert_fusion.3
  114.0 11.3 %collective-permute-done.14 = bf16[128,2048]{1,0:T(8,128)(2,1)S(1)} collective-permute-done((bf16[128,2048]{1,0:T(8,128)(2,1)S(1)}, bf16[128,2048]{1,0:T(8,128)(2,1)S(1)}, u32[]{:S(2)}, u32[]{:S(2)}) %collective-permute-start.14) | collective-permute-done | bytes 524320 | tf_op jit(solution)/shard_map/ppermute | solution.py:32
  128.0 29.7 %collective-permute-done.16 = bf16[128,2048]{1,0:T(8,128)(2,1)S(1)} collective-permute-done((bf16[128,2048]{1,0:T(8,128)(2,1)}, bf16[128,2048]{1,0:T(8,128)(2,1)S(1)}, u32[]{:S(2)}, u32[]{:S(2)}) %collective-permute-start.16) | collective-permute-done | bytes 524320 | tf_op jit(solution)/shard_map/ppermute | solution.py:32
  165.3 3.4 copy-done.11
  168.7 5.3 %shard_map.289.g_ref = bf16[512,2048]{1,0:T(8,128)(2,1)S(1)} custom-call(bf16[512,2048]{1,0:T(8,128)(2,1)S(1)} %pad_maximum_fusion.2.x_ref.y_ref, bf16[2048,2048]{1,0:T(8,128)(2,1)S(1)} %copy-done.11), custom_call_target="tpu_custom_call" | custom-call | flops 4294967296 | bytes 12582912 | tf_op jit(solution)/shard_map/pallas_call | solution.py:194
  175.3 11.4 %collective-permute-done.17 = bf16[128,2048]{1,0:T(8,128)(2,1)} collective-permute-done((bf16[128,2048]{1,0:T(8,128)(2,1)S(1)}, bf16[128,2048]{1,0:T(8,128)(2,1)}, u32[]{:S(2)}, u32[]{:S(2)}) %collective-permute-start.17) | collective-permute-done | bytes 524320 | tf_op jit(solution)/shard_map/ppermute | solution.py:32
  186.9 13.8 %collective-permute-done.19 = bf16[128,2048]{1,0:T(8,128)(2,1)S(1)} collective-permute-done((bf16[128,2048]{1,0:T(8,128)(2,1)}, bf16[128,2048]{1,0:T(8,128)(2,1)S(1)}, u32[]{:S(2)}, u32[]{:S(2)}) %collective-permute-start.19) | collective-permute-done | bytes 524320 | tf_op jit(solution)/shard_map/ppermute | solution.py:32
  200.7 2.8 pad_maximum_fusion.3.x_ref
  205.0 3.4 copy-done.30
  210.0 8.5 %shard_map.290 = (bf16[512,2048]{1,0:T(8,128)(2,1)S(1)}, bf16[512,2048]{1,0:T(8,128)(2,1)S(1)}) custom-call(bf16[512,2048]{1,0:T(8,128)(2,1)S(1)} %copy-done.4, bf16[2048,2048]{1,0:T(8,128)(2,1)S(1)} %copy-done.30, f32[1,2048]{1,0:T(1,128)S(1)} %bitcast.68, bf16[512,2048]{1,0:T(8,128)(2,1)S(1)} %copy-done.32), custom_call_target="tpu_custom_call" | custom-call | flops 4294967296 | bytes 16777216 | tf_op jit(solution)/shard_map/pallas_call | solution.py:225
  218.5 5.3 %shard_map.291.p_ref = bf16[512,2048]{1,0:T(8,128)(2,1)S(1)} custom-call(bf16[512,2048]{1,0:T(8,128)(2,1)S(1)} %get-tuple-element.104.x_ref.y_ref, bf16[2048,2048]{1,0:T(8,128)(2,1)S(1)} %copy-done.30), custom_call_target="tpu_custom_call" | custom-call | flops 4294967296 | bytes 12582912 | tf_op jit(solution)/shard_map/pallas_call | solution.py:194
  226.4 2.7 shard_map.292
  229.1 4.4 shard_map.293
  233.5 4.0 collective-permute-done.21
  241.7 8.9 %collective-permute-done.23.refs_0_ = bf16[1024,2048]{1,0:T(8,128)(2,1)S(1)} collective-permute-done((bf16[1024,2048]{1,0:T(8,128)(2,1)S(1)}, bf16[1024,2048]{1,0:T(8,128)(2,1)S(1)}, u32[]{:S(2)}, u32[]{:S(2)}) %collective-permute-start.23) | collective-permute-done | bytes 4194336 | tf_op jit(solution)/shard_map/ppermute | solution.py:32
  250.6 2.7 shard_map.294
  257.0 4.9 %shard_map.295 = bf16[2048,1024]{1,0:T(8,128)(2,1)S(1)} custom-call(s32[1]{0:T(128)} %bitcast.18.half_ref, bf16[512,2048]{1,0:T(8,128)(2,1)S(1)} %copy-done.6, bf16[512,2048]{1,0:T(8,128)(2,1)S(1)} %get-tuple-element.104.x_ref.y_ref, bf16[2048,1024]{1,0:T(8,128)(2,1)} %collective-permute-done.24.refs_0_), custom_call_target="tpu_custom_call" | custom-call | flops 1 | bytes 1 | tf_op jit(solution)/shard_map/pallas_call | solution.py:256
  269.4 2.8 shard_map.296
  273.2 2.8 collective-permute-start.26
  278.2 19.9 %collective-permute-done.25 = bf16[128,2048]{1,0:T(8,128)(2,1)} collective-permute-done((bf16[128,2048]{1,0:T(8,128)(2,1)}, bf16[128,2048]{1,0:T(8,128)(2,1)}, u32[]{:S(2)}, u32[]{:S(2)}) %collective-permute-start.25) | collective-permute-done | bytes 524320 | tf_op jit(solution)/shard_map/ppermute | solution.py:32
  302.4 9.7 %collective-permute-done.27 = bf16[128,2048]{1,0:T(8,128)(2,1)S(1)} collective-permute-done((bf16[128,2048]{1,0:T(8,128)(2,1)}, bf16[128,2048]{1,0:T(8,128)(2,1)S(1)}, u32[]{:S(2)}, u32[]{:S(2)}) %collective-permute-start.27) | collective-permute-done | bytes 524320 | tf_op jit(solution)/shard_map/ppermute | solution.py:32
  312.2 3.0 fusion.9.g_ref
  315.2 11.3 %shard_map.297 = (bf16[512,512]{1,0:T(8,128)(2,1)S(1)}, f32[2048,256]{1,0:T(8,128)S(1)}) custom-call(s32[4,2]{1,0:T(4,128)S(1)} %pad_add_fusion.1.bounds, bf16[512,512]{1,0:T(8,128)(2,1)S(1)} %copy-done.36, bf16[512,512]{1,0:T(8,128)(2,1)S(1)} %copy-done.34, bf16[512,512]{1,0:T(8,128)(2,1)S(1)} %fusion.9.g_ref, f32[4,1,512]{2,1,0:T(1,128)S(1)} %get-tuple-element.112.lse_ref, ...), custom_call_target="tpu_custom_call" | custom-call | flops 5368709120 | bytes 8388608 | tf_op jit(solution)/shard_map/pallas_call | solution.py:394
  328.0 3.0 convolution_convert_fusion.p_ref
  336.6 5.8 %shard_map.298 = bf16[512,2048]{1,0:T(8,128)(2,1)S(1)} custom-call(bf16[512,2048]{1,0:T(8,128)(2,1)S(1)} %copy-done.8, bf16[2048,2048]{1,0:T(8,128)(2,1)S(1)} %bitcast.65), custom_call_target="tpu_custom_call" | custom-call | flops 1 | bytes 1 | tf_op jit(solution)/shard_map/pallas_call | solution.py:194
  342.4 9.3 %collective-permute-done.28 = bf16[1024,256]{1,0:T(8,128)(2,1)S(1)} collective-permute-done((bf16[1024,256]{1,0:T(8,128)(2,1)S(1)}, bf16[1024,256]{1,0:T(8,128)(2,1)S(1)}, u32[]{:S(2)}, u32[]{:S(2)}) %collective-permute-start.28) | collective-permute-done | bytes 524320 | tf_op jit(solution)/shard_map/ppermute | solution.py:84
  352.0 4.5 collective-permute-done.32
  362.1 3.0 convolution_convert_fusion.2
  378.1 6.1 %collective-permute-done.34 = bf16[128,256]{1,0:T(8,128)(2,1)} collective-permute-done((bf16[128,256]{1,0:T(8,128)(2,1)}, bf16[128,256]{1,0:T(8,128)(2,1)}, u32[]{:S(2)}, u32[]{:S(2)}) %collective-permute-start.34) | collective-permute-done | bytes 65568 | tf_op jit(solution)/shard_map/ppermute | solution.py:32
  390.2 3.3 shard_map.299
  406.4 4.2 collective-permute-done.39
  411.6 11.0 %collective-permute-done.38 = bf16[304,512]{1,0:T(8,128)(2,1)} collective-permute-done((bf16[304,512]{1,0:T(8,128)(2,1)}, bf16[304,512]{1,0:T(8,128)(2,1)}, u32[]{:S(2)}, u32[]{:S(2)}) %collective-permute-start.38) | collective-permute-done | bytes 311328 | tf_op jit(solution)/shard_map/ppermute | solution.py:84
  425.7 6.2 %collective-permute-done.41 = bf16[128,2048]{1,0:T(8,128)(2,1)} collective-permute-done((bf16[128,2048]{1,0:T(8,128)(2,1)}, bf16[128,2048]{1,0:T(8,128)(2,1)}, u32[]{:S(2)}, u32[]{:S(2)}) %collective-permute-start.41) | collective-permute-done | bytes 524320 | tf_op jit(solution)/shard_map/ppermute | solution.py:32
  435.9 3.2 collective-permute-start.45
  440.1 2.8 collective-permute-done.44
  444.3 2.7 collective-permute-done.43
  (387 shorter events, 147.2 us)
Async XLA Ops:
  7.2 71.7 %all-gather.4.cloned.1.call-start = ((), (), s32[]{:S(2)}) async-start(), calls=%async_computation.3 | async-start | bytes 5898240 | tf_op jit(solution)/shard_map/all_gather | solution.py:501
  10.5 154.7 %all-gather.6.cloned.1.call-start = ((), (), s32[]{:S(2)}) async-start(), calls=%async_computation.4 | async-start | bytes 9437184 | tf_op jit(solution)/shard_map/all_gather | solution.py:501
  11.7 191.7 %all-gather.8.cloned.1.call-start = ((), (), s32[]{:S(2)}) async-start(), calls=%async_computation.5 | async-start | bytes 9437184 | tf_op jit(solution)/shard_map/all_gather | solution.py:501
  14.2 346.1 %reduce-scatter.4.cloned.1.call-start = ((), (), s32[]{:S(2)}) async-start(), calls=%async_computation.6 | async-start | bytes 5242880 | tf_op jit(solution)/shard_map/reduce_scatter | solution.py:93
  19.1 10.2 %collective-permute-start = (bf16[144,512]{1,0:T(8,128)(2,1)S(1)}, bf16[144,512]{1,0:T(8,128)(2,1)S(1)}, u32[]{:S(2)}, u32[]{:S(2)}) collective-permute-start(bf16[144,512]{1,0:T(8,128)(2,1)S(1)} %get-tuple-element.295), channel_id=1, source_target_pairs={{0,4},{4,0},{8,12},{12,8},{1,5},{5,1},{9,13},{13,9},{2,6},{6,2},{1... | collective-permute-start | bytes 442376 | tf_op jit(solution)/shard_map/ppermute | solution.py:84
  32.5 25.7 %collective-permute-start.3 = (bf16[128,2048]{1,0:T(8,128)(2,1)S(1)}, bf16[128,2048]{1,0:T(8,128)(2,1)S(1)}, u32[]{:S(2)}, u32[]{:S(2)}) collective-permute-start(bf16[128,2048]{1,0:T(8,128)(2,1)S(1)} %get-tuple-element.234), channel_id=1, source_target_pairs={{0,2},{2,0},{1,3},{3,1},{4,6},{6,4},{5,7},{7,5},{8,10},{10,8},{9,1... | collective-permute-start | bytes 1572872 | tf_op jit(solution)/shard_map/ppermute | solution.py:32
  35.1 23.4 %collective-permute-start.4 = (bf16[128,2048]{1,0:T(8,128)(2,1)S(1)}, bf16[128,2048]{1,0:T(8,128)(2,1)S(1)}, u32[]{:S(2)}, u32[]{:S(2)}) collective-permute-start(bf16[128,2048]{1,0:T(8,128)(2,1)S(1)} %get-tuple-element.234), channel_id=1, source_target_pairs={{0,1},{1,0},{2,3},{3,2},{4,5},{5,4},{6,7},{7,6},{8,9},{9,8},{10,11... | collective-permute-start | bytes 1572872 | tf_op jit(solution)/shard_map/ppermute | solution.py:32
  38.3 21.7 %collective-permute-start.7 = (bf16[128,1024]{1,0:T(8,128)(2,1)S(1)}, bf16[128,1024]{1,0:T(8,128)(2,1)S(1)}, u32[]{:S(2)}, u32[]{:S(2)}) collective-permute-start(bf16[128,1024]{1,0:T(8,128)(2,1)S(1)} %get-tuple-element.263), channel_id=1, source_target_pairs={{0,4},{4,0},{1,5},{5,1},{2,6},{6,2},{3,7},{7,3},{8,12},{12,8},{9,1... | collective-permute-start | bytes 786440 | tf_op jit(solution)/shard_map/ppermute | solution.py:32
  58.4 12.7 %collective-permute-start.5 = (bf16[128,2048]{1,0:T(8,128)(2,1)S(1)}, bf16[128,2048]{1,0:T(8,128)(2,1)}, u32[]{:S(2)}, u32[]{:S(2)}) collective-permute-start(bf16[128,2048]{1,0:T(8,128)(2,1)S(1)} %collective-permute-done.3), channel_id=1, source_target_pairs={{0,1},{1,0},{2,3},{3,2},{4,5},{5,4},{6,7},{7,6},{8,9},{9,8},{10,11... | collective-permute-start | bytes 1572872 | tf_op jit(solution)/shard_map/ppermute | solution.py:32
  73.8 36.5 %collective-permute-start.11 = (bf16[128,2048]{1,0:T(8,128)(2,1)S(1)}, bf16[128,2048]{1,0:T(8,128)(2,1)}, u32[]{:S(2)}, u32[]{:S(2)}) collective-permute-start(bf16[128,2048]{1,0:T(8,128)(2,1)S(1)} %pad_maximum_fusion.7.b_ref), channel_id=1, source_target_pairs={{0,2},{2,0},{1,3},{3,1},{4,6},{6,4},{5,7},{7,5},{8,10},{10,8},{9,1... | collective-permute-start | bytes 1572872 | tf_op jit(solution)/shard_map/ppermute | solution.py:32
  77.1 33.2 %collective-permute-start.12 = (bf16[128,2048]{1,0:T(8,128)(2,1)S(1)}, bf16[128,2048]{1,0:T(8,128)(2,1)}, u32[]{:S(2)}, u32[]{:S(2)}) collective-permute-start(bf16[128,2048]{1,0:T(8,128)(2,1)S(1)} %pad_maximum_fusion.7.b_ref), channel_id=1, source_target_pairs={{0,1},{1,0},{2,3},{3,2},{4,5},{5,4},{6,7},{7,6},{8,9},{9,8},{10,11... | collective-permute-start | bytes 1572872 | tf_op jit(solution)/shard_map/ppermute | solution.py:32
  81.6 12.4 %collective-permute-start.10 = (bf16[512,256]{1,0:T(8,128)(2,1)S(1)}, bf16[512,256]{1,0:T(8,128)(2,1)S(1)}, u32[]{:S(2)}, u32[]{:S(2)}) collective-permute-start(bf16[512,256]{1,0:T(8,128)(2,1)S(1)} %fusion.15), channel_id=1, source_target_pairs={{0,12},{4,8},{8,4},{12,0},{1,13},{5,9},{9,5},{13,1},{2,14},{6,10},... | collective-permute-start | bytes 786440 | tf_op jit(solution)/shard_map/ppermute | solution.py:84
  82.4 16.1 %collective-permute-start.9 = (bf16[512,256]{1,0:T(8,128)(2,1)S(1)}, bf16[512,256]{1,0:T(8,128)(2,1)S(1)}, u32[]{:S(2)}, u32[]{:S(2)}) collective-permute-start(bf16[512,256]{1,0:T(8,128)(2,1)S(1)} %fusion.15), channel_id=1, source_target_pairs={{0,8},{4,12},{8,0},{12,4},{1,9},{5,13},{9,1},{13,5},{2,10},{6,14},... | collective-permute-start | bytes 786440 | tf_op jit(solution)/shard_map/ppermute | solution.py:84
  82.7 15.8 %collective-permute-start.8 = (bf16[512,256]{1,0:T(8,128)(2,1)S(1)}, bf16[512,256]{1,0:T(8,128)(2,1)S(1)}, u32[]{:S(2)}, u32[]{:S(2)}) collective-permute-start(bf16[512,256]{1,0:T(8,128)(2,1)S(1)} %fusion.15), channel_id=1, source_target_pairs={{0,4},{4,0},{8,12},{12,8},{1,5},{5,1},{9,13},{13,9},{2,6},{6,2},{1... | collective-permute-start | bytes 786440 | tf_op jit(solution)/shard_map/ppermute | solution.py:84
  110.4 14.9 %collective-permute-start.14 = (bf16[128,2048]{1,0:T(8,128)(2,1)S(1)}, bf16[128,2048]{1,0:T(8,128)(2,1)S(1)}, u32[]{:S(2)}, u32[]{:S(2)}) collective-permute-start(bf16[128,2048]{1,0:T(8,128)(2,1)S(1)} %get-tuple-element.211), channel_id=1, source_target_pairs={{0,1},{1,0},{2,3},{3,2},{4,5},{5,4},{6,7},{7,6},{8,9},{9,8},{10,11... | collective-permute-start | bytes 1572872 | tf_op jit(solution)/shard_map/ppermute | solution.py:32
  112.0 47.1 %collective-permute-start.13 = (bf16[128,2048]{1,0:T(8,128)(2,1)S(1)}, bf16[128,2048]{1,0:T(8,128)(2,1)S(1)}, u32[]{:S(2)}, u32[]{:S(2)}) collective-permute-start(bf16[128,2048]{1,0:T(8,128)(2,1)S(1)} %get-tuple-element.212), channel_id=1, source_target_pairs={{0,1},{1,0},{2,3},{3,2},{4,5},{5,4},{6,7},{7,6},{8,9},{9,8},{10,11... | collective-permute-start | bytes 1572872 | tf_op jit(solution)/shard_map/ppermute | solution.py:32
  112.5 45.1 %collective-permute-start.16 = (bf16[128,2048]{1,0:T(8,128)(2,1)}, bf16[128,2048]{1,0:T(8,128)(2,1)S(1)}, u32[]{:S(2)}, u32[]{:S(2)}) collective-permute-start(bf16[128,2048]{1,0:T(8,128)(2,1)} %collective-permute-done.11), channel_id=1, source_target_pairs={{0,1},{1,0},{2,3},{3,2},{4,5},{5,4},{6,7},{7,6},{8,9},{9,8},{10,11... | collective-permute-start | bytes 1572872 | tf_op jit(solution)/shard_map/ppermute | solution.py:32
  125.5 33.6 %collective-permute-start.15 = (bf16[128,2048]{1,0:T(8,128)(2,1)S(1)}, bf16[128,2048]{1,0:T(8,128)(2,1)S(1)}, u32[]{:S(2)}, u32[]{:S(2)}) collective-permute-start(bf16[128,2048]{1,0:T(8,128)(2,1)S(1)} %add_convert_fusion.6), channel_id=1, source_target_pairs={{0,2},{2,0},{1,3},{3,1},{4,6},{6,4},{5,7},{7,5},{8,10},{10,8},{9,1... | collective-permute-start | bytes 1572872 | tf_op jit(solution)/shard_map/ppermute | solution.py:32
  161.9 24.8 %collective-permute-start.17 = (bf16[128,2048]{1,0:T(8,128)(2,1)S(1)}, bf16[128,2048]{1,0:T(8,128)(2,1)}, u32[]{:S(2)}, u32[]{:S(2)}) collective-permute-start(bf16[128,2048]{1,0:T(8,128)(2,1)S(1)} %get-tuple-element.196), channel_id=1, source_target_pairs={{0,2},{2,0},{1,3},{3,1},{4,6},{6,4},{5,7},{7,5},{8,10},{10,8},{9,1... | collective-permute-start | bytes 1572872 | tf_op jit(solution)/shard_map/ppermute | solution.py:32
  162.9 24.0 %collective-permute-start.18 = (bf16[128,2048]{1,0:T(8,128)(2,1)S(1)}, bf16[128,2048]{1,0:T(8,128)(2,1)}, u32[]{:S(2)}, u32[]{:S(2)}) collective-permute-start(bf16[128,2048]{1,0:T(8,128)(2,1)S(1)} %get-tuple-element.196), channel_id=1, source_target_pairs={{0,1},{1,0},{2,3},{3,2},{4,5},{5,4},{6,7},{7,6},{8,9},{9,8},{10,11... | collective-permute-start | bytes 1572872 | tf_op jit(solution)/shard_map/ppermute | solution.py:32
  186.9 13.8 %collective-permute-start.19 = (bf16[128,2048]{1,0:T(8,128)(2,1)}, bf16[128,2048]{1,0:T(8,128)(2,1)S(1)}, u32[]{:S(2)}, u32[]{:S(2)}) collective-permute-start(bf16[128,2048]{1,0:T(8,128)(2,1)} %collective-permute-done.17), channel_id=1, source_target_pairs={{0,1},{1,0},{2,3},{3,2},{4,5},{5,4},{6,7},{7,6},{8,9},{9,8},{10,11... | collective-permute-start | bytes 1572872 | tf_op jit(solution)/shard_map/ppermute | solution.py:32
  224.7 12.7 %collective-permute-start.21 = (bf16[128,2048]{1,0:T(8,128)(2,1)S(1)}, bf16[128,2048]{1,0:T(8,128)(2,1)S(1)}, u32[]{:S(2)}, u32[]{:S(2)}) collective-permute-start(bf16[128,2048]{1,0:T(8,128)(2,1)S(1)} %get-tuple-element.209), channel_id=1, source_target_pairs={{0,1},{1,0},{2,3},{3,2},{4,5},{5,4},{6,7},{7,6},{8,9},{9,8},{10,11... | collective-permute-start | bytes 1572872 | tf_op jit(solution)/shard_map/ppermute | solution.py:32
  237.4 13.1 %collective-permute-start.23 = (bf16[1024,2048]{1,0:T(8,128)(2,1)S(1)}, bf16[1024,2048]{1,0:T(8,128)(2,1)S(1)}, u32[]{:S(2)}, u32[]{:S(2)}) collective-permute-start(bf16[1024,2048]{1,0:T(8,128)(2,1)S(1)} %shard_map.292), channel_id=1, source_target_pairs={{0,16},{16,0},{1,17},{17,1},{2,18},{18,2},{3,19},{19,3},{4,20},{20... | collective-permute-start | bytes 12582920 | tf_op jit(solution)/shard_map/ppermute | solution.py:32
  237.5 17.9 %collective-permute-start.24 = (bf16[2048,1024]{1,0:T(8,128)(2,1)}, bf16[2048,1024]{1,0:T(8,128)(2,1)}, u32[]{:S(2)}, u32[]{:S(2)}) collective-permute-start(bf16[2048,1024]{1,0:T(8,128)(2,1)} %shard_map.293), channel_id=1, source_target_pairs={{0,16},{16,0},{1,17},{17,1},{2,18},{18,2},{3,19},{19,3},{4,20},{20... | collective-permute-start | bytes 12582920 | tf_op jit(solution)/shard_map/ppermute | solution.py:32
  238.0 26.0 %collective-permute-start.20 = (bf16[128,2048]{1,0:T(8,128)(2,1)}, bf16[128,2048]{1,0:T(8,128)(2,1)S(1)}, u32[]{:S(2)}, u32[]{:S(2)}) collective-permute-start(bf16[128,2048]{1,0:T(8,128)(2,1)} %get-tuple-element.210), channel_id=1, source_target_pairs={{0,1},{1,0},{2,3},{3,2},{4,5},{5,4},{6,7},{7,6},{8,9},{9,8},{10,11... | collective-permute-start | bytes 1572872 | tf_op jit(solution)/shard_map/ppermute | solution.py:32
  239.5 26.0 %collective-permute-start.22 = (bf16[128,2048]{1,0:T(8,128)(2,1)}, bf16[128,2048]{1,0:T(8,128)(2,1)}, u32[]{:S(2)}, u32[]{:S(2)}) collective-permute-start(bf16[128,2048]{1,0:T(8,128)(2,1)} %add_convert_fusion.4), channel_id=1, source_target_pairs={{0,2},{2,0},{1,3},{3,1},{4,6},{6,4},{5,7},{7,5},{8,10},{10,8},{9,1... | collective-permute-start | bytes 1572872 | tf_op jit(solution)/shard_map/ppermute | solution.py:32
  265.6 130.2 %reduce-scatter.6.cloned.1.call-start = ((), (), s32[]{:S(2)}) async-start(), calls=%async_computation.7 | async-start | bytes 5242880 | tf_op jit(solution)/shard_map/reduce_scatter | solution.py:93
  266.2 193.5 %reduce-scatter.8.cloned.1.call-start = ((), (), s32[]{:S(2)}) async-start(), calls=%async_computation.8 | async-start | bytes 4718592 | tf_op jit(solution)/shard_map/reduce_scatter | solution.py:596
  273.2 24.9 %collective-permute-start.25 = (bf16[128,2048]{1,0:T(8,128)(2,1)}, bf16[128,2048]{1,0:T(8,128)(2,1)}, u32[]{:S(2)}, u32[]{:S(2)}) collective-permute-start(bf16[128,2048]{1,0:T(8,128)(2,1)} %get-tuple-element.108), channel_id=1, source_target_pairs={{0,2},{2,0},{1,3},{3,1},{4,6},{6,4},{5,7},{7,5},{8,10},{10,8},{9,1... | collective-permute-start | bytes 1572872 | tf_op jit(solution)/shard_map/ppermute | solution.py:32
  273.2 25.0 %collective-permute-start.26 = (bf16[128,2048]{1,0:T(8,128)(2,1)}, bf16[128,2048]{1,0:T(8,128)(2,1)}, u32[]{:S(2)}, u32[]{:S(2)}) collective-permute-start(bf16[128,2048]{1,0:T(8,128)(2,1)} %get-tuple-element.108), channel_id=1, source_target_pairs={{0,1},{1,0},{2,3},{3,2},{4,5},{5,4},{6,7},{7,6},{8,9},{9,8},{10,11... | collective-permute-start | bytes 1572872 | tf_op jit(solution)/shard_map/ppermute | solution.py:32
  298.2 13.9 %collective-permute-start.27 = (bf16[128,2048]{1,0:T(8,128)(2,1)}, bf16[128,2048]{1,0:T(8,128)(2,1)S(1)}, u32[]{:S(2)}, u32[]{:S(2)}) collective-permute-start(bf16[128,2048]{1,0:T(8,128)(2,1)} %collective-permute-done.25), channel_id=1, source_target_pairs={{0,1},{1,0},{2,3},{3,2},{4,5},{5,4},{6,7},{7,6},{8,9},{9,8},{10,11... | collective-permute-start | bytes 1572872 | tf_op jit(solution)/shard_map/ppermute | solution.py:32
  326.9 24.9 %collective-permute-start.28 = (bf16[1024,256]{1,0:T(8,128)(2,1)S(1)}, bf16[1024,256]{1,0:T(8,128)(2,1)S(1)}, u32[]{:S(2)}, u32[]{:S(2)}) collective-permute-start(bf16[1024,256]{1,0:T(8,128)(2,1)S(1)} %get-tuple-element.216), channel_id=1, source_target_pairs={{0,8},{4,12},{8,0},{12,4},{1,9},{5,13},{9,1},{13,5},{2,10},{6,14},... | collective-permute-start | bytes 1572872 | tf_op jit(solution)/shard_map/ppermute | solution.py:84
  332.0 53.2 %collective-permute-start.31 = (bf16[128,2048]{1,0:T(8,128)(2,1)}, bf16[128,2048]{1,0:T(8,128)(2,1)}, u32[]{:S(2)}, u32[]{:S(2)}) collective-permute-start(bf16[128,2048]{1,0:T(8,128)(2,1)} %get-tuple-element.208), channel_id=1, source_target_pairs={{0,1},{1,0},{2,3},{3,2},{4,5},{5,4},{6,7},{7,6},{8,9},{9,8},{10,11... | collective-permute-start | bytes 1572872 | tf_op jit(solution)/shard_map/ppermute | solution.py:32
  332.8 23.7 %collective-permute-start.32 = (bf16[128,2048]{1,0:T(8,128)(2,1)S(1)}, bf16[128,2048]{1,0:T(8,128)(2,1)S(1)}, u32[]{:S(2)}, u32[]{:S(2)}) collective-permute-start(bf16[128,2048]{1,0:T(8,128)(2,1)S(1)} %get-tuple-element.207), channel_id=1, source_target_pairs={{0,1},{1,0},{2,3},{3,2},{4,5},{5,4},{6,7},{7,6},{8,9},{9,8},{10,11... | collective-permute-start | bytes 1572872 | tf_op jit(solution)/shard_map/ppermute | solution.py:32
  357.4 27.7 %collective-permute-start.33 = (bf16[128,2048]{1,0:T(8,128)(2,1)}, bf16[128,2048]{1,0:T(8,128)(2,1)}, u32[]{:S(2)}, u32[]{:S(2)}) collective-permute-start(bf16[128,2048]{1,0:T(8,128)(2,1)} %add_convert_fusion.3), channel_id=1, source_target_pairs={{0,2},{2,0},{1,3},{3,1},{4,6},{6,4},{5,7},{7,5},{8,10},{10,8},{9,1... | collective-permute-start | bytes 1572872 | tf_op jit(solution)/shard_map/ppermute | solution.py:32
  361.0 10.3 %collective-permute-start.30 = (bf16[256,256]{1,0:T(8,128)(2,1)}, bf16[256,256]{1,0:T(8,128)(2,1)}, u32[]{:S(2)}, u32[]{:S(2)}) collective-permute-start(bf16[256,256]{1,0:T(8,128)(2,1)} %pad_maximum_fusion.18), channel_id=1, source_target_pairs={{0,1},{1,0},{2,3},{3,2},{4,5},{5,4},{6,7},{7,6},{8,9},{9,8},{10,11... | collective-permute-start | bytes 393224 | tf_op jit(solution)/shard_map/ppermute | solution.py:32
  372.8 11.4 %collective-permute-start.34 = (bf16[128,256]{1,0:T(8,128)(2,1)}, bf16[128,256]{1,0:T(8,128)(2,1)}, u32[]{:S(2)}, u32[]{:S(2)}) collective-permute-start(bf16[128,256]{1,0:T(8,128)(2,1)} %add_convert_fusion.11), channel_id=1, source_target_pairs={{0,2},{2,0},{1,3},{3,1},{4,6},{6,4},{5,7},{7,5},{8,10},{10,8},{9,1... | collective-permute-start | bytes 196616 | tf_op jit(solution)/shard_map/ppermute | solution.py:32
  376.1 19.7 %collective-permute-start.36 = (bf16[128,2048]{1,0:T(8,128)(2,1)}, bf16[128,2048]{1,0:T(8,128)(2,1)}, u32[]{:S(2)}, u32[]{:S(2)}) collective-permute-start(bf16[128,2048]{1,0:T(8,128)(2,1)} %get-tuple-element.206), channel_id=1, source_target_pairs={{0,1},{1,0},{2,3},{3,2},{4,5},{5,4},{6,7},{7,6},{8,9},{9,8},{10,11... | collective-permute-start | bytes 1572872 | tf_op jit(solution)/shard_map/ppermute | solution.py:32
  376.4 49.3 %collective-permute-start.40 = (bf16[128,2048]{1,0:T(8,128)(2,1)}, bf16[128,2048]{1,0:T(8,128)(2,1)}, u32[]{:S(2)}, u32[]{:S(2)}) collective-permute-start(bf16[128,2048]{1,0:T(8,128)(2,1)} %get-tuple-element.205), channel_id=1, source_target_pairs={{0,1},{1,0},{2,3},{3,2},{4,5},{5,4},{6,7},{7,6},{8,9},{9,8},{10,11... | collective-permute-start | bytes 1572872 | tf_op jit(solution)/shard_map/ppermute | solution.py:32
  399.2 11.4 %collective-permute-start.39 = (bf16[304,512]{1,0:T(8,128)(2,1)}, bf16[304,512]{1,0:T(8,128)(2,1)}, u32[]{:S(2)}, u32[]{:S(2)}) collective-permute-start(bf16[304,512]{1,0:T(8,128)(2,1)} %pad_maximum_fusion.13), channel_id=1, source_target_pairs={{0,12},{4,8},{8,4},{12,0},{1,13},{5,9},{9,5},{13,1},{2,14},{6,10},... | collective-permute-start | bytes 933896 | tf_op jit(solution)/shard_map/ppermute | solution.py:84
  400.8 21.8 %collective-permute-start.38 = (bf16[304,512]{1,0:T(8,128)(2,1)}, bf16[304,512]{1,0:T(8,128)(2,1)}, u32[]{:S(2)}, u32[]{:S(2)}) collective-permute-start(bf16[304,512]{1,0:T(8,128)(2,1)} %pad_maximum_fusion.12), channel_id=1, source_target_pairs={{0,8},{4,12},{8,0},{12,4},{1,9},{5,13},{9,1},{13,5},{2,10},{6,14},... | collective-permute-start | bytes 933896 | tf_op jit(solution)/shard_map/ppermute | solution.py:84
  402.6 21.0 %collective-permute-start.37 = (bf16[304,512]{1,0:T(8,128)(2,1)}, bf16[304,512]{1,0:T(8,128)(2,1)}, u32[]{:S(2)}, u32[]{:S(2)}) collective-permute-start(bf16[304,512]{1,0:T(8,128)(2,1)} %pad_maximum_fusion.11), channel_id=1, source_target_pairs={{0,4},{4,0},{8,12},{12,8},{1,5},{5,1},{9,13},{13,9},{2,6},{6,2},{1... | collective-permute-start | bytes 933896 | tf_op jit(solution)/shard_map/ppermute | solution.py:84
  406.2 25.6 %collective-permute-start.41 = (bf16[128,2048]{1,0:T(8,128)(2,1)}, bf16[128,2048]{1,0:T(8,128)(2,1)}, u32[]{:S(2)}, u32[]{:S(2)}) collective-permute-start(bf16[128,2048]{1,0:T(8,128)(2,1)} %add_convert_fusion.1), channel_id=1, source_target_pairs={{0,2},{2,0},{1,3},{3,1},{4,6},{6,4},{5,7},{7,5},{8,10},{10,8},{9,1... | collective-permute-start | bytes 1572872 | tf_op jit(solution)/shard_map/ppermute | solution.py:32
  433.4 9.5 %collective-permute-start.44 = (bf16[128,512]{1,0:T(8,128)(2,1)S(1)}, bf16[128,512]{1,0:T(8,128)(2,1)S(1)}, u32[]{:S(2)}, u32[]{:S(2)}) collective-permute-start(bf16[128,512]{1,0:T(8,128)(2,1)S(1)} %get-tuple-element.252), channel_id=1, source_target_pairs={{0,12},{4,8},{8,4},{12,0},{1,13},{5,9},{9,5},{13,1},{2,14},{6,10},... | collective-permute-start | bytes 393224 | tf_op jit(solution)/shard_map/ppermute | solution.py:84
  434.7 13.2 %collective-permute-start.47 = (bf16[176,512]{1,0:T(8,128)(2,1)S(1)}, bf16[176,512]{1,0:T(8,128)(2,1)S(1)}, u32[]{:S(2)}, u32[]{:S(2)}) collective-permute-start(bf16[176,512]{1,0:T(8,128)(2,1)S(1)} %convert_add_fusion.2), channel_id=1, source_target_pairs={{0,3},{3,0},{1,2},{2,1},{4,7},{7,4},{5,6},{6,5},{8,11},{11,8},{9,1... | collective-permute-start | bytes 540680 | tf_op jit(solution)/shard_map/ppermute | solution.py:631
  435.9 13.5 %collective-permute-start.46 = (bf16[176,512]{1,0:T(8,128)(2,1)S(1)}, bf16[176,512]{1,0:T(8,128)(2,1)S(1)}, u32[]{:S(2)}, u32[]{:S(2)}) collective-permute-start(bf16[176,512]{1,0:T(8,128)(2,1)S(1)} %convert_add_fusion.2), channel_id=1, source_target_pairs={{0,1},{1,0},{2,3},{3,2},{4,5},{5,4},{6,7},{7,6},{8,9},{9,8},{10,11... | collective-permute-start | bytes 540680 | tf_op jit(solution)/shard_map/ppermute | solution.py:32
  435.9 14.4 %collective-permute-start.45 = (bf16[176,512]{1,0:T(8,128)(2,1)S(1)}, bf16[176,512]{1,0:T(8,128)(2,1)S(1)}, u32[]{:S(2)}, u32[]{:S(2)}) collective-permute-start(bf16[176,512]{1,0:T(8,128)(2,1)S(1)} %convert_add_fusion.2), channel_id=1, source_target_pairs={{0,2},{2,0},{1,3},{3,1},{4,6},{6,4},{5,7},{7,5},{8,10},{10,8},{9,1... | collective-permute-start | bytes 540680 | tf_op jit(solution)/shard_map/ppermute | solution.py:32
  447.9 12.0 %collective-permute-start.51 = (bf16[1024,512]{1,0:T(8,128)(2,1)S(1)}, bf16[1024,512]{1,0:T(8,128)(2,1)}, u32[]{:S(2)}, u32[]{:S(2)}) collective-permute-start(bf16[1024,512]{1,0:T(8,128)(2,1)S(1)} %copy-done.44), channel_id=1, source_target_pairs={{0,16},{16,0},{1,17},{17,1},{2,18},{18,2},{3,19},{19,3},{4,20},{20... | collective-permute-start | bytes 3145736 | tf_op jit(solution)/shard_map/ppermute | solution.py:32
  (77 other events, 600.4 us)
Sparse Core Ops, SparseCore 0:
  10.7 50.8 all-gather.3
  64.0 68.0 all-gather.5
  134.7 54.3 all-gather.7
  265.7 51.2 reduce-scatter.3
  320.6 62.0 reduce-scatter.5
  386.5 61.4 reduce-scatter.7
